TPU v7x, 512 devices: a whole 4x4x16 slice. The times are simulated.
512 devices in a mesh: peer: 16 (over z_lo, x), zero: 32 (over y, z_hi, core).
Axes of the slice: x: 4, y: 4, z: 16 (z_hi: 4, z_lo: 4; z = z_hi * 4 + z_lo), core: 2. Of those that a mesh axis runs over, the one named last changes fastest.
Arguments:
- step: int32 [1], replicated, may hold values from 0 to 63
- grads: bfloat16 [16, 32, 1, 2, 128, 3584], P('peer', 'zero'), may hold values from -64 to 64
- master: float32 [16, 2, 128, 3584], P('peer', None, 'zero'), may hold values from -4 to 4
- first_moment: float32 [16, 2, 128, 3584], P('peer', None, 'zero'), may hold values from -1.75 to 1.75
- second_moment: float32 [16, 2, 128, 3584], P('peer', None, 'zero'), may hold values from 0.01 to 1
Outputs:
- new_master: float32 [16, 2, 128, 3584], P('peer', None, 'zero')
- new_first: float32 [16, 2, 128, 3584], P('peer', None, 'zero')
- new_second: float32 [16, 2, 128, 3584], P('peer', None, 'zero')
- params_bf16: bfloat16 [16, 2, 128, 3584], P('peer')
All inputs are finite; a program needn't handle non-finite values.
Results may differ from a plain program's by a relative error of at most 0.001.
Values may be sent and summed in bfloat16 or wider, within the bound.
No kernel may reach another device: no remote copies, remote signals or barrier semaphores. Data moves between devices by JAX's collectives and lax.ppermute only.
A program may use at most 64 MiB of HBM per device.

v0:
```python
import jax
import jax.numpy as jnp
from jax import lax
from jax.sharding import Mesh, PartitionSpec as P

PEER = ("zlo", "x")
ZERO = ("y", "zhi", "core")
F32 = jnp.float32
BF16 = jnp.bfloat16


def shifted(block, axis, distance):
    n = lax.axis_size(axis)
    return lax.ppermute(block, axis, [(i, (i + distance) % n) for i in range(n)])


def piece(stack, index):
    return lax.dynamic_index_in_dim(stack, index, 0, keepdims=False)


def reduce_over(stack, axis):
    n = lax.axis_size(axis)
    me = lax.axis_index(axis)
    total = piece(stack, me)
    for k in (1, n - 1, 2):
        total = total + shifted(piece(stack, (me + k) % n), axis, k)
    return total


def body(step, grads, master, first_moment, second_moment):
    t = step[0]
    power = (t + 1).astype(F32)
    corr_one = 1.0 - jnp.power(F32(0.9), power)
    corr_two = 1.0 - jnp.power(F32(0.95), power)
    depth = master.shape[-1]
    ny, nz, nc = (lax.axis_size(a) for a in ZERO)

    local = grads[0, 0, 0].reshape(2, ny, nz, nc, 4, depth)
    local = local.transpose(3, 1, 2, 0, 4, 5).reshape(nc, ny, nz * 8, depth)
    core = lax.axis_index("core")
    theirs = shifted(piece(local, 1 - core), "core", 1)
    part = piece(local, core).astype(F32) + theirs.astype(F32)
    part = reduce_over(part, "y")
    part = reduce_over(part.reshape(nz, 8, depth), "zhi")
    mean_grad = part.reshape(2, 4, depth) * (1.0 / 32)

    new_first = 0.9 * first_moment[0] + 0.1 * mean_grad
    new_second = 0.95 * second_moment[0] + 0.05 * mean_grad * mean_grad
    updated = master[0] - 0.05 * (
        new_first / corr_one / (jnp.sqrt(new_second / corr_two) + 1e-08) + 0.1 * master[0]
    )
    partner = lax.switch(
        t % 3, [lambda u, d=d: shifted(u, PEER, d) for d in (1, 2, 4)], updated
    )
    averaged = (updated + partner) * 0.5

    whole = averaged.astype(BF16).reshape(8, depth)
    whole = lax.all_gather(whole, "zhi", axis=0)
    whole = lax.all_gather(whole, "y", axis=0)
    other = shifted(whole, "core", 1)
    pair = jnp.where(core == 0, jnp.stack([whole, other]), jnp.stack([other, whole]))
    pair = pair.reshape(nc, ny, nz, 2, 4, depth).transpose(3, 1, 2, 0, 4, 5)
    whole = pair.reshape(2, ny * nz * nc * 4, depth)
    return (averaged[None], new_first[None], new_second[None], whole[None])


def solution(mesh):
    fine = Mesh(mesh.devices.reshape(4, 4, 4, 4, 2), PEER + ZERO)
    shard = P(PEER, None, ZERO, None)
    return jax.shard_map(
        body,
        mesh=fine,
        in_specs=(P(), P(PEER, ZERO, None, None, None, None), shard, shard, shard),
        out_specs=(shard, shard, shard, P(PEER, None, None, None)),
        check_vma=False,
    )
```

profile of v0, /device:TPU:1, one launch (start us, length us, event | category | flops | bytes accessed | tf_op | source)
XLA Modules:
  0.0 138.1 jit_solution(6460777475011930376)
XLA Ops:
  0.6 3.1 %reshape_squeeze.3 = bf16[2,4,4,2,4,3584]{5,4,3,2,1,0:T(4,128)(2,1)S(1)} reshape(bf16[1,1,1,2,128,3584]{5,4,3,2,1,0:T(8,128)(2,1)} %param.9) | data formatting | bytes 3670016 | tf_op jit(solution)/shard_map/reshape;squeeze | solution.py:38
  3.8 2.6 %copy.18 = bf16[2,4,4,2,4,3584]{5,1,4,0,2,3:T(4,128)(2,1)} copy(bf16[2,4,4,2,4,3584]{5,4,3,2,1,0:T(4,128)(2,1)S(1)} %reshape_squeeze.3) | data formatting | bytes 3670016 | tf_op jit(solution)/shard_map/reshape;squeeze | solution.py:38
  6.4 0.0 copy-start
  6.4 1.6 %dynamic-slice_bitcast_fusion = bf16[4,32,3584]{2,0,1:T(4,128)(2,1)S(1)} fusion(bf16[2,4,32,3584]{3,1,2,0:T(4,128)(2,1)} %bitcast.74, s32[]{:T(128)S(6)} %select_n.74), kind=kLoop, calls=%fused_computation.3 | loop fusion | bytes 1835012 | tf_op jit(solution)/shard_map/jit(dynamic_index_in_dim)/squeeze | solution.py:18
  8.1 8.8 %collective-permute-start.3 = (bf16[4,32,3584]{2,0,1:T(4,128)(2,1)S(1)}, bf16[4,32,3584]{2,0,1:T(4,128)(2,1)}, u32[]{:S(2)}, u32[]{:S(2)}) collective-permute-start(bf16[4,32,3584]{2,0,1:T(4,128)(2,1)S(1)} %dynamic-slice_bitcast_fusion), channel_id=1, source_target_pairs={{0,1},{1,0},{2,3},{3,2},{4,5},{5,4},{6,7},{7,6},{8,9},{9,8},{10,11... | collective-permute-start | bytes 2752520 | tf_op jit(solution)/shard_map/ppermute | solution.py:14
  16.9 2.2 %collective-permute-done.3 = bf16[4,32,3584]{2,0,1:T(4,128)(2,1)} collective-permute-done((bf16[4,32,3584]{2,0,1:T(4,128)(2,1)S(1)}, bf16[4,32,3584]{2,0,1:T(4,128)(2,1)}, u32[]{:S(2)}, u32[]{:S(2)}) %collective-permute-start.3) | collective-permute-done | bytes 917536 | tf_op jit(solution)/shard_map/ppermute | solution.py:14
  19.1 0.0 copy-done
  19.1 1.7 %convert_add_fusion = f32[4,32,3584]{2,0,1:T(4,128)S(1)} fusion(bf16[4,32,3584]{2,0,1:T(4,128)(2,1)} %collective-permute-done.3, bf16[2,4,32,3584]{3,1,2,0:T(4,128)(2,1)S(1)} %bitcast.75, s32[]{:T(128)S(6)} %select_n.73), kind=kLoop, calls=%fused_computation.2 | loop fusion | flops 1376256 | bytes 3670020 | tf_op jit(solution)/shard_map/add | solution.py:42
  20.7 1.6 %constant_dynamic-slice_fusion.3 = (f32[1,32,3584]{2,0,1:T(1,128)S(1)}, f32[1,32,3584]{2,0,1:T(1,128)S(1)}, f32[1,32,3584]{2,0,1:T(1,128)S(1)}, f32[1,32,3584]{2,0,1:T(1,128)S(1)}) fusion(f32[4,32,3584]{2,0,1:T(4,128)S(1)} %convert_add_fusion, s32[]{:T(128)S(6)} %select_n.75, s32[]{:T(128)S(6)} %select_n.81, s32[]{:T(128)S(6)} %select_n.79, s32[]{:T(128)S(6)} %select_n.77), kind=kLoop, calls=%fused_computation.34 | loop fusion | bytes 3670032 | tf_op jit(solution)/shard_map/jit(dynamic_index_in_dim)/dynamic_slice | solution.py:18
  22.3 1.9 %collective-permute-start.6 = (f32[32,3584]{1,0:T(8,128)S(1)}, f32[32,3584]{1,0:T(8,128)S(1)}, u32[]{:S(2)}, u32[]{:S(2)}) collective-permute-start(f32[32,3584]{1,0:T(8,128)S(1)} %bitcast.78), channel_id=1, source_target_pairs={{0,16},{8,24},{16,0},{24,8},{1,17},{9,25},{17,1},{25,9},{2,18},{10... | collective-permute-start | bytes 1376264 | tf_op jit(solution)/shard_map/ppermute | solution.py:14
  24.3 1.9 %collective-permute-start.5 = (f32[32,3584]{1,0:T(8,128)S(1)}, f32[32,3584]{1,0:T(8,128)S(1)}, u32[]{:S(2)}, u32[]{:S(2)}) collective-permute-start(f32[32,3584]{1,0:T(8,128)S(1)} %bitcast.79), channel_id=1, source_target_pairs={{0,24},{8,0},{16,8},{24,16},{1,25},{9,1},{17,9},{25,17},{2,26},{10... | collective-permute-start | bytes 1376264 | tf_op jit(solution)/shard_map/ppermute | solution.py:14
  26.3 3.4 %collective-permute-start.4 = (f32[32,3584]{1,0:T(8,128)S(1)}, f32[32,3584]{1,0:T(8,128)S(1)}, u32[]{:S(2)}, u32[]{:S(2)}) collective-permute-start(f32[32,3584]{1,0:T(8,128)S(1)} %bitcast.80), channel_id=1, source_target_pairs={{0,8},{8,16},{16,24},{24,0},{1,9},{9,17},{17,25},{25,1},{2,10},{10... | collective-permute-start | bytes 1376264 | tf_op jit(solution)/shard_map/ppermute | solution.py:14
  29.7 7.8 %collective-permute-done.6 = f32[32,3584]{1,0:T(8,128)S(1)} collective-permute-done((f32[32,3584]{1,0:T(8,128)S(1)}, f32[32,3584]{1,0:T(8,128)S(1)}, u32[]{:S(2)}, u32[]{:S(2)}) %collective-permute-start.6) | collective-permute-done | bytes 458784 | tf_op jit(solution)/shard_map/ppermute | solution.py:14
  37.5 4.8 %collective-permute-done.5 = f32[32,3584]{1,0:T(8,128)S(1)} collective-permute-done((f32[32,3584]{1,0:T(8,128)S(1)}, f32[32,3584]{1,0:T(8,128)S(1)}, u32[]{:S(2)}, u32[]{:S(2)}) %collective-permute-start.5) | collective-permute-done | bytes 458784 | tf_op jit(solution)/shard_map/ppermute | solution.py:14
  42.3 5.7 %collective-permute-done.4 = f32[32,3584]{1,0:T(8,128)S(1)} collective-permute-done((f32[32,3584]{1,0:T(8,128)S(1)}, f32[32,3584]{1,0:T(8,128)S(1)}, u32[]{:S(2)}, u32[]{:S(2)}) %collective-permute-start.4) | collective-permute-done | bytes 458784 | tf_op jit(solution)/shard_map/ppermute | solution.py:14
  48.0 0.0 copy-start.1
  48.0 0.0 copy-start.2
  48.0 0.0 copy-start.3
  48.0 0.1 fusion.3
  48.2 10.2 %collective-permute-start.9 = (f32[8,3584]{1,0:T(8,128)S(1)}, f32[8,3584]{1,0:T(8,128)S(1)}, u32[]{:S(2)}, u32[]{:S(2)}) collective-permute-start(f32[8,3584]{1,0:T(8,128)S(1)} %get-tuple-element.26), channel_id=1, source_target_pairs={{0,4},{2,6},{4,0},{6,2},{1,5},{3,7},{5,1},{7,3},{8,12},{10,14},{12... | collective-permute-start | bytes 344072 | tf_op jit(solution)/shard_map/ppermute | solution.py:14
  58.4 1.9 %collective-permute-start.8 = (f32[8,3584]{1,0:T(8,128)S(1)}, f32[8,3584]{1,0:T(8,128)S(1)}, u32[]{:S(2)}, u32[]{:S(2)}) collective-permute-start(f32[8,3584]{1,0:T(8,128)S(1)} %get-tuple-element.27), channel_id=1, source_target_pairs={{0,6},{2,0},{4,2},{6,4},{1,7},{3,1},{5,3},{7,5},{8,14},{10,8},{12,... | collective-permute-start | bytes 344072 | tf_op jit(solution)/shard_map/ppermute | solution.py:14
  60.3 7.3 %collective-permute-start.7 = (f32[8,3584]{1,0:T(8,128)S(1)}, f32[8,3584]{1,0:T(8,128)S(1)}, u32[]{:S(2)}, u32[]{:S(2)}) collective-permute-start(f32[8,3584]{1,0:T(8,128)S(1)} %get-tuple-element.25), channel_id=1, source_target_pairs={{0,2},{2,4},{4,6},{6,0},{1,3},{3,5},{5,7},{7,1},{8,10},{10,12},{12... | collective-permute-start | bytes 344072 | tf_op jit(solution)/shard_map/ppermute | solution.py:14
  68.3 0.0 collective-permute-done.9
  68.3 10.9 %collective-permute-done.8 = f32[8,3584]{1,0:T(8,128)S(1)} collective-permute-done((f32[8,3584]{1,0:T(8,128)S(1)}, f32[8,3584]{1,0:T(8,128)S(1)}, u32[]{:S(2)}, u32[]{:S(2)}) %collective-permute-start.8) | collective-permute-done | bytes 114720 | tf_op jit(solution)/shard_map/ppermute | solution.py:14
  79.2 0.0 collective-permute-done.7
  79.4 0.0 copy-done.1
  79.4 0.0 copy-done.2
  79.4 0.0 copy-done.3
  79.4 0.2 bitcast_subtract_fusion
  79.6 9.9 %conditional.1 = (f32[2,4,3584]{2,1,0:T(4,128)}) conditional(s32[]{:T(128)} %clamp.3, f32[2,4,3584]{2,1,0:T(4,128)S(1)} %bitcast_subtract_fusion, f32[2,4,3584]{2,1,0:T(4,128)S(1)} %bitcast_subtract_fusion, f32[2,4,3584]{2,1,0:T(4,128)S(1)} %bitcast_subtract_fusion), branch_computations={%region_0.1_spmd, %region_1.2_spmd, %region_2.3_spmd} | conditional | bytes 458800 | solution.py:52
  79.6 5.1 %collective-permute-start.1 = (f32[2,4,3584]{2,1,0:T(4,128)S(1)}, f32[2,4,3584]{2,1,0:T(4,128)}, u32[]{:S(2)}, u32[]{:S(2)}) collective-permute-start(f32[2,4,3584]{2,1,0:T(4,128)S(1)} %param.1), channel_id=1, source_target_pairs={{0,64},{32,96},{64,128},{96,160},{128,192},{160,224},{192,256},{22... | collective-permute-start | bytes 344072 | tf_op jit(solution)/shard_map/cond/branch_1_fun/ppermute | solution.py:14
  84.7 4.7 %collective-permute-done.1 = f32[2,4,3584]{2,1,0:T(4,128)} collective-permute-done((f32[2,4,3584]{2,1,0:T(4,128)S(1)}, f32[2,4,3584]{2,1,0:T(4,128)}, u32[]{:S(2)}, u32[]{:S(2)}) %collective-permute-start.1) | collective-permute-done | bytes 114720 | tf_op jit(solution)/shard_map/cond/branch_1_fun/ppermute | solution.py:14
  89.4 1.6 %fusion.9 = (bf16[2,4,3584]{2,1,0:T(4,128)(2,1)S(1)}, f32[1,2,4,3584]{3,2,1,0:T(4,128)}) fusion(f32[2,4,3584]{2,1,0:T(4,128)S(1)} %bitcast_subtract_fusion, f32[2,4,3584]{2,1,0:T(4,128)} %get-tuple-element.32), kind=kLoop, calls=%fused_computation.29 | loop fusion | flops 86016 | bytes 401408 | tf_op jit(solution)/shard_map/convert_element_type | solution.py:57
  91.1 16.3 %all_gather.9 = bf16[4,8,3584]{2,1,0:T(8,128)(2,1)S(1)} all-gather(bf16[1,8,3584]{2,1,0:T(8,128)(2,1)S(1)} %all_gather_reshape.3), channel_id=1, replica_groups=mesh['zlo'=4,'x'=4,'y'=4,'zhi'=4,'core'=2] {'zhi'}, dimensions={0}, use_global_device_ids=true | all-gather | bytes 286720 | tf_op jit(solution)/shard_map/all_gather | solution.py:58
  107.4 14.1 %all-gather = bf16[16,8,3584]{2,1,0:T(8,128)(2,1)S(1)} all-gather(bf16[4,8,3584]{2,1,0:T(8,128)(2,1)S(1)} %all_gather.9), channel_id=2, replica_groups=mesh['zlo'=4,'x'=4,'y'=4,'zhi'=4,'core'=2] {'y'}, dimensions={0}, use_global_device_ids=true | all-gather | bytes 1146880 | tf_op jit(solution)/shard_map/all_gather | solution.py:59
  121.4 9.1 %collective-permute-start.10 = (bf16[4,4,8,3584]{3,2,1,0:T(8,128)(2,1)S(1)}, bf16[4,4,8,3584]{3,2,1,0:T(8,128)(2,1)S(1)}, u32[]{:S(2)}, u32[]{:S(2)}) collective-permute-start(bf16[4,4,8,3584]{3,2,1,0:T(8,128)(2,1)S(1)} %bitcast.77), channel_id=1, source_target_pairs={{0,1},{1,0},{2,3},{3,2},{4,5},{5,4},{6,7},{7,6},{8,9},{9,8},{10,11... | collective-permute-start | bytes 2752520 | tf_op jit(solution)/shard_map/ppermute | solution.py:14
  130.6 0.2 stack.14
  130.8 0.8 multiply_add_fusion
  131.6 1.0 collective-permute-done.10
  132.6 0.5 copy.19
  133.1 0.4 copy.20
  133.4 1.4 fusion
  134.8 1.8 %copy.22 = bf16[2,4,4,2,4,3584]{5,0,4,3,2,1:T(2,128)(2,1)S(1)} copy(bf16[2,4,4,2,4,3584]{5,4,0,2,1,3:T(4,128)(2,1)S(1)} %fusion) | data formatting | bytes 3670016 | tf_op jit(solution)/shard_map/transpose | solution.py:62
  136.6 1.4 %copy.23 = bf16[1,2,128,3584]{3,2,1,0:T(8,128)(2,1)} copy(bf16[1,2,128,3584]{3,1,2,0:T(2,128)(2,1)S(1)} %bitcast.73) | data formatting | bytes 3670016
  (11 shorter events, 0.3 us)
Async XLA Ops:
  6.4 12.6 %copy-start = (bf16[2,4,4,2,4,3584]{5,1,4,0,2,3:T(4,128)(2,1)S(1)}, bf16[2,4,4,2,4,3584]{5,1,4,0,2,3:T(4,128)(2,1)}, u32[]{:S(2)}) copy-start(bf16[2,4,4,2,4,3584]{5,1,4,0,2,3:T(4,128)(2,1)} %copy.18) | copy-start | bytes 5505028
  8.1 11.0 %collective-permute-start.3 = (bf16[4,32,3584]{2,0,1:T(4,128)(2,1)S(1)}, bf16[4,32,3584]{2,0,1:T(4,128)(2,1)}, u32[]{:S(2)}, u32[]{:S(2)}) collective-permute-start(bf16[4,32,3584]{2,0,1:T(4,128)(2,1)S(1)} %dynamic-slice_bitcast_fusion), channel_id=1, source_target_pairs={{0,1},{1,0},{2,3},{3,2},{4,5},{5,4},{6,7},{7,6},{8,9},{9,8},{10,11... | collective-permute-start | bytes 2752520 | tf_op jit(solution)/shard_map/ppermute | solution.py:14
  22.3 15.2 %collective-permute-start.6 = (f32[32,3584]{1,0:T(8,128)S(1)}, f32[32,3584]{1,0:T(8,128)S(1)}, u32[]{:S(2)}, u32[]{:S(2)}) collective-permute-start(f32[32,3584]{1,0:T(8,128)S(1)} %bitcast.78), channel_id=1, source_target_pairs={{0,16},{8,24},{16,0},{24,8},{1,17},{9,25},{17,1},{25,9},{2,18},{10... | collective-permute-start | bytes 1376264 | tf_op jit(solution)/shard_map/ppermute | solution.py:14
  24.3 18.0 %collective-permute-start.5 = (f32[32,3584]{1,0:T(8,128)S(1)}, f32[32,3584]{1,0:T(8,128)S(1)}, u32[]{:S(2)}, u32[]{:S(2)}) collective-permute-start(f32[32,3584]{1,0:T(8,128)S(1)} %bitcast.79), channel_id=1, source_target_pairs={{0,24},{8,0},{16,8},{24,16},{1,25},{9,1},{17,9},{25,17},{2,26},{10... | collective-permute-start | bytes 1376264 | tf_op jit(solution)/shard_map/ppermute | solution.py:14
  26.3 21.7 %collective-permute-start.4 = (f32[32,3584]{1,0:T(8,128)S(1)}, f32[32,3584]{1,0:T(8,128)S(1)}, u32[]{:S(2)}, u32[]{:S(2)}) collective-permute-start(f32[32,3584]{1,0:T(8,128)S(1)} %bitcast.80), channel_id=1, source_target_pairs={{0,8},{8,16},{16,24},{24,0},{1,9},{9,17},{17,25},{25,1},{2,10},{10... | collective-permute-start | bytes 1376264 | tf_op jit(solution)/shard_map/ppermute | solution.py:14
  48.0 31.4 %copy-start.1 = (f32[1,2,4,3584]{3,2,1,0:T(4,128)S(1)}, f32[1,2,4,3584]{3,2,1,0:T(4,128)}, u32[]{:S(2)}) copy-start(f32[1,2,4,3584]{3,2,1,0:T(4,128)} %param.12) | copy-start | bytes 344068
  48.0 31.4 %copy-start.2 = (f32[1,2,4,3584]{3,2,1,0:T(4,128)S(1)}, f32[1,2,4,3584]{3,2,1,0:T(4,128)}, u32[]{:S(2)}) copy-start(f32[1,2,4,3584]{3,2,1,0:T(4,128)} %param.11) | copy-start | bytes 344068
  48.0 31.4 %copy-start.3 = (f32[1,2,4,3584]{3,2,1,0:T(4,128)S(1)}, f32[1,2,4,3584]{3,2,1,0:T(4,128)}, u32[]{:S(2)}) copy-start(f32[1,2,4,3584]{3,2,1,0:T(4,128)} %param.10) | copy-start | bytes 344068
  48.2 20.2 %collective-permute-start.9 = (f32[8,3584]{1,0:T(8,128)S(1)}, f32[8,3584]{1,0:T(8,128)S(1)}, u32[]{:S(2)}, u32[]{:S(2)}) collective-permute-start(f32[8,3584]{1,0:T(8,128)S(1)} %get-tuple-element.26), channel_id=1, source_target_pairs={{0,4},{2,6},{4,0},{6,2},{1,5},{3,7},{5,1},{7,3},{8,12},{10,14},{12... | collective-permute-start | bytes 344072 | tf_op jit(solution)/shard_map/ppermute | solution.py:14
  58.4 20.9 %collective-permute-start.8 = (f32[8,3584]{1,0:T(8,128)S(1)}, f32[8,3584]{1,0:T(8,128)S(1)}, u32[]{:S(2)}, u32[]{:S(2)}) collective-permute-start(f32[8,3584]{1,0:T(8,128)S(1)} %get-tuple-element.27), channel_id=1, source_target_pairs={{0,6},{2,0},{4,2},{6,4},{1,7},{3,1},{5,3},{7,5},{8,14},{10,8},{12,... | collective-permute-start | bytes 344072 | tf_op jit(solution)/shard_map/ppermute | solution.py:14
  60.3 18.9 %collective-permute-start.7 = (f32[8,3584]{1,0:T(8,128)S(1)}, f32[8,3584]{1,0:T(8,128)S(1)}, u32[]{:S(2)}, u32[]{:S(2)}) collective-permute-start(f32[8,3584]{1,0:T(8,128)S(1)} %get-tuple-element.25), channel_id=1, source_target_pairs={{0,2},{2,4},{4,6},{6,0},{1,3},{3,5},{5,7},{7,1},{8,10},{10,12},{12... | collective-permute-start | bytes 344072 | tf_op jit(solution)/shard_map/ppermute | solution.py:14
  79.6 9.8 %collective-permute-start.1 = (f32[2,4,3584]{2,1,0:T(4,128)S(1)}, f32[2,4,3584]{2,1,0:T(4,128)}, u32[]{:S(2)}, u32[]{:S(2)}) collective-permute-start(f32[2,4,3584]{2,1,0:T(4,128)S(1)} %param.1), channel_id=1, source_target_pairs={{0,64},{32,96},{64,128},{96,160},{128,192},{160,224},{192,256},{22... | collective-permute-start | bytes 344072 | tf_op jit(solution)/shard_map/cond/branch_1_fun/ppermute | solution.py:14
  121.4 11.2 %collective-permute-start.10 = (bf16[4,4,8,3584]{3,2,1,0:T(8,128)(2,1)S(1)}, bf16[4,4,8,3584]{3,2,1,0:T(8,128)(2,1)S(1)}, u32[]{:S(2)}, u32[]{:S(2)}) collective-permute-start(bf16[4,4,8,3584]{3,2,1,0:T(8,128)(2,1)S(1)} %bitcast.77), channel_id=1, source_target_pairs={{0,1},{1,0},{2,3},{3,2},{4,5},{5,4},{6,7},{7,6},{8,9},{9,8},{10,11... | collective-permute-start | bytes 2752520 | tf_op jit(solution)/shard_map/ppermute | solution.py:14
where the time goes:
time: 139 us; the launch traced here: 138 us
  starting transfers between devices  49.6 us (36%)
  waiting for transfers between devices  37.1 us (27%)
  blocking collectives  30.4 us (22%)
  local copies, waits for them, and re-layouts  13.6 us (10%)
  other arithmetic  5.69 us (4%)
  between operations  1.72 us (1%)
    ppermute x9, starting transfers between devices, shifted(): lax.ppermute(block, axis, [(i, (i + distance) % n) for i in range(n)])  49.6 us
    ppermute x9, waiting for transfers between devices, shifted(): lax.ppermute(block, axis, [(i, (i + distance) % n) for i in range(n)])  37.1 us
    all_gather x1, blocking collectives, body(): whole = lax.all_gather(whole, 'zhi', axis=0)  16.3 us
    all_gather x1, blocking collectives, body(): whole = lax.all_gather(whole, 'y', axis=0)  14.1 us
    another operation x2, local copies, waits for them, and re-layouts, body(): local = grads[0, 0, 0].reshape(2, ny, nz, nc, 4, depth)  5.78 us
  transfers between devices with their start and end apart: 9, of which 7 were waited for; matrix products, arithmetic and copies ran while one was open for 1% of the time, Pallas kernels for 0%

commit v1 on v0

v1 whole, which is shorter than its diff:
```python
import jax
import jax.numpy as jnp
from jax import lax
from jax.experimental import pallas as pl
from jax.experimental.pallas import tpu as pltpu
from jax.sharding import Mesh, PartitionSpec as P

PEER = ("zlo", "x")
ZERO = ("y", "zhi", "core")
F32 = jnp.float32
BF16 = jnp.bfloat16
VMEM = pl.BlockSpec(memory_space=pltpu.VMEM)
SMEM = pl.BlockSpec(memory_space=pltpu.SMEM)
LANES = 512
PARAMS = pltpu.CompilerParams(vmem_limit_bytes=32 * 2**20)


def shifted(block, axis, distance):
    n = lax.axis_size(axis)
    return lax.ppermute(block, axis, [(i, (i + distance) % n) for i in range(n)])


def low_high(a, b):
    row = lax.broadcasted_iota(jnp.int32, a.shape, 0)
    low = jnp.where(row < 4, a, pltpu.roll(b, 4, 0))
    high = jnp.where(row < 4, pltpu.roll(a, 4, 0), b)
    return low, high


def split_kernel(where_ref, grads_ref, mine_ref, theirs_ref):
    first = where_ref[1] == 0
    depth = grads_ref.shape[-1]
    for at in range(0, depth, LANES):
        cols = slice(at, at + LANES)
        a = grads_ref[0, :, cols].astype(F32)
        b = grads_ref[1, :, cols].astype(F32)
        mine, theirs = [], []
        for r in range(0, a.shape[0], 8):
            low, high = low_high(a[r : r + 8], b[r : r + 8])
            mine.append(jnp.where(first, low, high))
            theirs.append(jnp.where(first, high, low))
        mine_ref[0, :, cols] = jnp.concatenate(mine, 0).astype(BF16)
        theirs_ref[0, :, cols] = jnp.concatenate(theirs, 0).astype(BF16)


def split_cores(grads, y, core):
    layers, rows, depth = grads.shape
    ny = lax.axis_size("y")
    per = rows // ny
    out = jax.ShapeDtypeStruct((ny, per, depth), BF16)
    block = pl.BlockSpec((1, per, depth), lambda k, w: (k, 0, 0))
    return pl.pallas_call(
        split_kernel,
        grid_spec=pltpu.PrefetchScalarGridSpec(
            num_scalar_prefetch=1,
            grid=(ny,),
            in_specs=[pl.BlockSpec((layers, per, depth), lambda k, w: (0, (w[0] + k) % ny, 0))],
            out_specs=[block, block],
        ),
        out_shape=(out, out),
        compiler_params=PARAMS,
        name="split_cores",
    )(jnp.stack([y, core]).astype(jnp.int32), grads)


def add_pair_kernel(mine_ref, theirs_ref, *outs):
    for k, out in enumerate(outs):
        out[...] = mine_ref[k].astype(F32) + theirs_ref[k].astype(F32)


def add_pair(mine, theirs):
    n, rows, depth = mine.shape
    out = jax.ShapeDtypeStruct((rows, depth), F32)
    return pl.pallas_call(
        add_pair_kernel,
        in_specs=[VMEM, VMEM],
        out_specs=[VMEM] * n,
        out_shape=[out] * n,
        compiler_params=PARAMS,
        name="add_pair",
    )(mine, theirs)


def add_four_kernel(z_ref, a_ref, b_ref, c_ref, d_ref, *outs):
    n = len(outs)
    for k, out in enumerate(outs):
        at = pl.ds(pl.multiple_of(((z_ref[0] + k) % n) * 8, 8), 8)
        out[...] = (a_ref[at, :] + b_ref[at, :]) + (c_ref[at, :] + d_ref[at, :])


def add_four(z, parts):
    rows, depth = parts[0].shape
    n = rows // 8
    out = jax.ShapeDtypeStruct((8, depth), F32)
    return pl.pallas_call(
        add_four_kernel,
        in_specs=[SMEM] + [VMEM] * 4,
        out_specs=[VMEM] * n,
        out_shape=[out] * n,
        compiler_params=PARAMS,
        name="add_four",
    )(z.astype(jnp.int32)[None], *parts)


def adam_kernel(corr_ref, a_ref, b_ref, c_ref, d_ref, master_ref, first_ref, second_ref, nf_ref, ns_ref, up_ref):
    mean_all = ((a_ref[...] + b_ref[...]) + (c_ref[...] + d_ref[...])) * (1.0 / 32)
    for layer in range(2):
        mean = mean_all[4 * layer : 4 * layer + 4]
        master = master_ref[layer]
        nf = 0.9 * first_ref[layer] + 0.1 * mean
        ns = 0.95 * second_ref[layer] + 0.05 * mean * mean
        nf_ref[layer] = nf
        ns_ref[layer] = ns
        up_ref[layer] = master - 0.05 * (
            nf / corr_ref[0] / (jnp.sqrt(ns / corr_ref[1]) + 1e-08) + 0.1 * master
        )


def adam(corr, parts, master, first, second):
    out = jax.ShapeDtypeStruct(master.shape, F32)
    return pl.pallas_call(
        adam_kernel,
        in_specs=[SMEM] + [VMEM] * 7,
        out_specs=[VMEM] * 3,
        out_shape=[out] * 3,
        compiler_params=PARAMS,
        name="adam",
    )(corr, *parts, master, first, second)


def join_kernel(core_ref, mine_ref, theirs_ref, out_ref):
    first = core_ref[0] == 0
    depth = mine_ref.shape[-1]
    for at in range(0, depth, LANES):
        cols = slice(at, at + LANES)
        mine = mine_ref[:, cols].astype(F32)
        theirs = theirs_ref[:, cols].astype(F32)
        a = jnp.where(first, mine, theirs)
        b = jnp.where(first, theirs, mine)
        lows, highs = [], []
        for r in range(0, a.shape[0], 8):
            low, high = low_high(a[r : r + 8], b[r : r + 8])
            lows.append(low)
            highs.append(high)
        out_ref[0, :, cols] = jnp.concatenate(lows, 0).astype(BF16)
        out_ref[1, :, cols] = jnp.concatenate(highs, 0).astype(BF16)


def join_cores(mine, theirs, core):
    rows, depth = mine.shape
    steps = 4
    per = rows // steps
    block = pl.BlockSpec((per, depth), lambda k, w: (k, 0))
    return pl.pallas_call(
        join_kernel,
        grid_spec=pltpu.PrefetchScalarGridSpec(
            num_scalar_prefetch=1,
            grid=(steps,),
            in_specs=[block, block],
            out_specs=pl.BlockSpec((2, per, depth), lambda k, w: (0, k, 0)),
        ),
        out_shape=jax.ShapeDtypeStruct((2, rows, depth), BF16),
        compiler_params=PARAMS,
        name="join_cores",
    )(core.astype(jnp.int32)[None], mine, theirs)


def body(step, grads, master, first_moment, second_moment):
    t = step[0]
    power = (t + 1).astype(F32)
    corr = jnp.stack([1.0 - jnp.power(F32(0.9), power), 1.0 - jnp.power(F32(0.95), power)])
    depth = master.shape[-1]
    y, z, core = (lax.axis_index(a) for a in ZERO)

    mine, theirs = split_cores(grads[0, 0, 0], y, core)
    parts = add_pair(mine, shifted(theirs, "core", 1))
    two = shifted(parts[2], "y", 2)
    parts = [parts[0], shifted(parts[1], "y", 1), two, shifted(parts[3], "y", 3)]
    parts = add_four(z, parts)
    two = shifted(parts[2], "zhi", 2)
    parts = [parts[0], shifted(parts[1], "zhi", 1), two, shifted(parts[3], "zhi", 3)]
    new_first, new_second, updated = adam(
        corr, parts, master[0], first_moment[0], second_moment[0]
    )
    partner = lax.switch(
        t % 3, [lambda u, d=d: shifted(u, PEER, d) for d in (1, 2, 4)], updated
    )
    averaged = (updated + partner) * 0.5

    whole = averaged.astype(BF16).reshape(8, depth)
    whole = lax.all_gather(whole, "zhi", axis=0, tiled=True)
    whole = lax.all_gather(whole, "y", axis=0, tiled=True)
    whole = join_cores(whole, shifted(whole, "core", 1), core)
    return (averaged[None], new_first[None], new_second[None], whole[None])


def solution(mesh):
    fine = Mesh(mesh.devices.reshape(4, 4, 4, 4, 2), PEER + ZERO)
    shard = P(PEER, None, ZERO, None)
    return jax.shard_map(
        body,
        mesh=fine,
        in_specs=(P(), P(PEER, ZERO, None, None, None, None), shard, shard, shard),
        out_specs=(shard, shard, shard, P(PEER, None, None, None)),
        check_vma=False,
    )
```

time: 139 us -> 135 us (0.971)
  local copies, waits for them, and re-layouts: 13.6 us -> 1.53 us
  waiting for transfers between devices: 37.1 us -> 43.1 us
  Pallas kernels: 0 us -> 4.89 us
  other arithmetic: 5.69 us -> 1.74 us
  blocking collectives: 30.4 us -> 31.8 us
    another operation x5 -> x0, local copies, waits for them, and re-layouts: 6.36 us -> none  [the longest x2 5.78 us: body(): local = grads[0, 0, 0].reshape(2, ny, nz, nc, 4, depth)]
    ppermute x9, waiting for transfers between devices: 37.1 us -> 43.1 us  [shifted(): lax.ppermute(block, axis, [(i, (i + distance) % n) for i in range(n)])]
    pallas_call x0 -> x5, Pallas kernels: none -> 4.89 us  [the longest x1 1.97 us: join_cores(): pl.pallas_call(join_kernel, grid_spec=pltpu.PrefetchScalarGridSpec(num_sc...]
    add x2 -> x0, other arithmetic: 2.42 us -> none  [the longest x1 1.65 us: body(): part = piece(local, core).astype(F32) + theirs.astype(F32)]
    transpose x1 -> x0, local copies, waits for them, and re-layouts: 1.82 us -> none  [body(): pair = pair.reshape(nc, ny, nz, 2, 4, depth).transpose(3, 1, 2, 0, 4, 5)]
    squeeze x2 -> x0, local copies, waits for them, and re-layouts: 1.66 us -> none  [piece(): return lax.dynamic_index_in_dim(stack, index, 0, keepdims=False)]
    dynamic_slice x1 -> x0, local copies, waits for them, and re-layouts: 1.58 us -> none  [piece(): return lax.dynamic_index_in_dim(stack, index, 0, keepdims=False)]
    all_gather x2, blocking collectives: 30.4 us -> 31.8 us  [the longest x1 18.2 us: body(): whole = lax.all_gather(whole, 'zhi', axis=0, tiled=True)]
  transfers between devices with their start and end apart: 9 -> 9, of which waited for: 7 -> 7; matrix products, arithmetic and copies ran while one was open for 1% -> 0% of each run, Pallas kernels for 0% -> 0%
where the time goes in v1:
time: 135 us
  starting transfers between devices  50.3 us (37%)
  waiting for transfers between devices  43.1 us (32%)
  blocking collectives  31.8 us (24%)
  Pallas kernels  4.89 us (4%)
  other arithmetic  1.74 us (1%)
  local copies, waits for them, and re-layouts  1.53 us (1%)
  between operations  1.48 us (1%)
    ppermute x9, starting transfers between devices, shifted(): lax.ppermute(block, axis, [(i, (i + distance) % n) for i in range(n)])  50.3 us
    ppermute x9, waiting for transfers between devices, shifted(): lax.ppermute(block, axis, [(i, (i + distance) % n) for i in range(n)])  43.1 us
    all_gather x1, blocking collectives, body(): whole = lax.all_gather(whole, 'zhi', axis=0, tiled=True)  18.2 us
    all_gather x1, blocking collectives, body(): whole = lax.all_gather(whole, 'y', axis=0, tiled=True)  13.6 us
  transfers between devices with their start and end apart: 9, of which 7 were waited for; matrix products, arithmetic and copies ran while one was open for 0% of the time, Pallas kernels for 0%

profile of v1, /device:TPU:1, one launch (start us, length us, event | category | flops | bytes accessed | tf_op | source)
XLA Modules:
  0.0 134.9 jit_solution(7270384630608758142)
XLA Ops:
  0.6 0.1 pad_add_fusion.where_ref
  0.7 0.0 copy-start
  0.7 1.5 %copy-done = bf16[1,1,1,2,128,3584]{5,4,3,2,1,0:T(8,128)(2,1)S(1)} copy-done((bf16[1,1,1,2,128,3584]{5,4,3,2,1,0:T(8,128)(2,1)S(1)}, bf16[1,1,1,2,128,3584]{5,4,3,2,1,0:T(8,128)(2,1)}, u32[]{:S(2)}) %copy-start) | copy-done | bytes 1835032
  2.2 1.4 %split_cores.1 = (bf16[4,32,3584]{2,1,0:T(8,128)(2,1)S(1)}, bf16[4,32,3584]{2,1,0:T(8,128)(2,1)S(1)}) custom-call(s32[2]{0:T(128)S(1)} %pad_add_fusion.where_ref, bf16[2,128,3584]{2,1,0:T(8,128)(2,1)S(1)} %bitcast.13), custom_call_target="tpu_custom_call" | custom-call | tf_op jit(solution)/shard_map/split_cores/pallas_call | solution.py:52
  3.6 8.8 %collective-permute-start.3 = (bf16[4,32,3584]{2,1,0:T(8,128)(2,1)S(1)}, bf16[4,32,3584]{2,1,0:T(8,128)(2,1)S(1)}, u32[]{:S(2)}, u32[]{:S(2)}) collective-permute-start(bf16[4,32,3584]{2,1,0:T(8,128)(2,1)S(1)} %get-tuple-element.25), channel_id=1, source_target_pairs={{0,1},{1,0},{2,3},{3,2},{4,5},{5,4},{6,7},{7,6},{8,9},{9,8},{10,11... | collective-permute-start | bytes 2752520 | tf_op jit(solution)/shard_map/ppermute | solution.py:20
  12.4 2.1 %collective-permute-done.3.theirs_ref = bf16[4,32,3584]{2,1,0:T(8,128)(2,1)S(1)} collective-permute-done((bf16[4,32,3584]{2,1,0:T(8,128)(2,1)S(1)}, bf16[4,32,3584]{2,1,0:T(8,128)(2,1)S(1)}, u32[]{:S(2)}, u32[]{:S(2)}) %collective-permute-start.3) | collective-permute-done | bytes 917536 | tf_op jit(solution)/shard_map/ppermute | solution.py:20
  14.5 0.0 copy-start.1
  14.5 0.0 copy-start.2
  14.5 0.0 copy-start.3
  14.5 0.2 add_pair.1
  14.6 1.9 %collective-permute-start.4 = (f32[32,3584]{1,0:T(8,128)S(1)}, f32[32,3584]{1,0:T(8,128)S(1)}, u32[]{:S(2)}, u32[]{:S(2)}) collective-permute-start(f32[32,3584]{1,0:T(8,128)S(1)} %get-tuple-element.27), channel_id=1, source_target_pairs={{0,8},{8,16},{16,24},{24,0},{1,9},{9,17},{17,25},{25,1},{2,10},{10... | collective-permute-start | bytes 1376264 | tf_op jit(solution)/shard_map/ppermute | solution.py:20
  16.6 1.9 %collective-permute-start.5 = (f32[32,3584]{1,0:T(8,128)S(1)}, f32[32,3584]{1,0:T(8,128)S(1)}, u32[]{:S(2)}, u32[]{:S(2)}) collective-permute-start(f32[32,3584]{1,0:T(8,128)S(1)} %get-tuple-element.28), channel_id=1, source_target_pairs={{0,16},{8,24},{16,0},{24,8},{1,17},{9,25},{17,1},{25,9},{2,18},{10... | collective-permute-start | bytes 1376264 | tf_op jit(solution)/shard_map/ppermute | solution.py:20
  18.5 4.6 %collective-permute-start.6 = (f32[32,3584]{1,0:T(8,128)S(1)}, f32[32,3584]{1,0:T(8,128)S(1)}, u32[]{:S(2)}, u32[]{:S(2)}) collective-permute-start(f32[32,3584]{1,0:T(8,128)S(1)} %get-tuple-element.29), channel_id=1, source_target_pairs={{0,24},{8,0},{16,8},{24,16},{1,25},{9,1},{17,9},{25,17},{2,26},{10... | collective-permute-start | bytes 1376264 | tf_op jit(solution)/shard_map/ppermute | solution.py:20
  23.1 16.2 %collective-permute-done.4.b_ref = f32[32,3584]{1,0:T(8,128)S(1)} collective-permute-done((f32[32,3584]{1,0:T(8,128)S(1)}, f32[32,3584]{1,0:T(8,128)S(1)}, u32[]{:S(2)}, u32[]{:S(2)}) %collective-permute-start.4) | collective-permute-done | bytes 458784 | tf_op jit(solution)/shard_map/ppermute | solution.py:20
  39.3 0.0 collective-permute-done.5.c_ref
  39.3 2.2 %collective-permute-done.6.d_ref = f32[32,3584]{1,0:T(8,128)S(1)} collective-permute-done((f32[32,3584]{1,0:T(8,128)S(1)}, f32[32,3584]{1,0:T(8,128)S(1)}, u32[]{:S(2)}, u32[]{:S(2)}) %collective-permute-start.6) | collective-permute-done | bytes 458784 | tf_op jit(solution)/shard_map/ppermute | solution.py:20
  41.5 0.1 add_four.1
  41.6 3.6 %collective-permute-start.7 = (f32[8,3584]{1,0:T(8,128)S(1)}, f32[8,3584]{1,0:T(8,128)S(1)}, u32[]{:S(2)}, u32[]{:S(2)}) collective-permute-start(f32[8,3584]{1,0:T(8,128)S(1)} %get-tuple-element.31), channel_id=1, source_target_pairs={{0,2},{2,4},{4,6},{6,0},{1,3},{3,5},{5,7},{7,1},{8,10},{10,12},{12... | collective-permute-start | bytes 344072 | tf_op jit(solution)/shard_map/ppermute | solution.py:20
  45.2 10.6 %collective-permute-start.8 = (f32[8,3584]{1,0:T(8,128)S(1)}, f32[8,3584]{1,0:T(8,128)S(1)}, u32[]{:S(2)}, u32[]{:S(2)}) collective-permute-start(f32[8,3584]{1,0:T(8,128)S(1)} %get-tuple-element.32), channel_id=1, source_target_pairs={{0,4},{2,6},{4,0},{6,2},{1,5},{3,7},{5,1},{7,3},{8,12},{10,14},{12... | collective-permute-start | bytes 344072 | tf_op jit(solution)/shard_map/ppermute | solution.py:20
  55.9 5.2 %collective-permute-start.9 = (f32[8,3584]{1,0:T(8,128)S(1)}, f32[8,3584]{1,0:T(8,128)S(1)}, u32[]{:S(2)}, u32[]{:S(2)}) collective-permute-start(f32[8,3584]{1,0:T(8,128)S(1)} %get-tuple-element.33), channel_id=1, source_target_pairs={{0,6},{2,0},{4,2},{6,4},{1,7},{3,1},{5,3},{7,5},{8,14},{10,8},{12,... | collective-permute-start | bytes 344072 | tf_op jit(solution)/shard_map/ppermute | solution.py:20
  61.8 0.1 pad_maximum_fusion.corr_ref
  61.9 0.0 collective-permute-done.7.b_ref
  61.9 6.1 %collective-permute-done.8.c_ref = f32[8,3584]{1,0:T(8,128)S(1)} collective-permute-done((f32[8,3584]{1,0:T(8,128)S(1)}, f32[8,3584]{1,0:T(8,128)S(1)}, u32[]{:S(2)}, u32[]{:S(2)}) %collective-permute-start.8) | collective-permute-done | bytes 114720 | tf_op jit(solution)/shard_map/ppermute | solution.py:20
  68.0 8.7 %collective-permute-done.9.d_ref = f32[8,3584]{1,0:T(8,128)S(1)} collective-permute-done((f32[8,3584]{1,0:T(8,128)S(1)}, f32[8,3584]{1,0:T(8,128)S(1)}, u32[]{:S(2)}, u32[]{:S(2)}) %collective-permute-start.9) | collective-permute-done | bytes 114720 | tf_op jit(solution)/shard_map/ppermute | solution.py:20
  76.7 0.0 copy-done.1
  76.7 0.0 copy-done.2
  76.7 0.0 copy-done.3
  76.7 1.3 adam.1
  78.0 10.4 %conditional.1 = (f32[2,4,3584]{2,1,0:T(4,128)}) conditional(s32[]{:T(128)} %clamp.3, f32[2,4,3584]{2,1,0:T(4,128)S(1)} %get-tuple-element.34, f32[2,4,3584]{2,1,0:T(4,128)S(1)} %get-tuple-element.34, f32[2,4,3584]{2,1,0:T(4,128)S(1)} %get-tuple-element.34), branch_computations={%region_0.1_spmd, %region_1.2_spmd, %region_2.3_spmd} | conditional | bytes 458800 | solution.py:185
  78.0 4.6 %collective-permute-start.1 = (f32[2,4,3584]{2,1,0:T(4,128)S(1)}, f32[2,4,3584]{2,1,0:T(4,128)}, u32[]{:S(2)}, u32[]{:S(2)}) collective-permute-start(f32[2,4,3584]{2,1,0:T(4,128)S(1)} %param.1), channel_id=1, source_target_pairs={{0,64},{32,96},{64,128},{96,160},{128,192},{160,224},{192,256},{22... | collective-permute-start | bytes 344072 | tf_op jit(solution)/shard_map/cond/branch_1_fun/ppermute | solution.py:20
  82.6 5.7 %collective-permute-done.1 = f32[2,4,3584]{2,1,0:T(4,128)} collective-permute-done((f32[2,4,3584]{2,1,0:T(4,128)S(1)}, f32[2,4,3584]{2,1,0:T(4,128)}, u32[]{:S(2)}, u32[]{:S(2)}) %collective-permute-start.1) | collective-permute-done | bytes 114720 | tf_op jit(solution)/shard_map/cond/branch_1_fun/ppermute | solution.py:20
  88.3 1.6 %fusion = (bf16[2,4,3584]{2,1,0:T(4,128)(2,1)S(1)}, f32[1,2,4,3584]{3,2,1,0:T(4,128)}) fusion(f32[2,4,3584]{2,1,0:T(4,128)S(1)} %get-tuple-element.34, f32[2,4,3584]{2,1,0:T(4,128)} %get-tuple-element.39), kind=kLoop, calls=%fused_computation.1 | loop fusion | flops 86016 | bytes 401408 | tf_op jit(solution)/shard_map/convert_element_type | solution.py:190
  89.9 18.2 %all_gather.6 = bf16[32,3584]{1,0:T(8,128)(2,1)S(1)} all-gather(bf16[8,3584]{1,0:T(8,128)(2,1)S(1)} %reshape.26), channel_id=1, replica_groups=mesh['zlo'=4,'x'=4,'y'=4,'zhi'=4,'core'=2] {'zhi'}, dimensions={0}, use_global_device_ids=true | all-gather | bytes 286720 | tf_op jit(solution)/shard_map/all_gather | solution.py:191
  108.1 13.6 %all_gather.7.mine_ref = bf16[128,3584]{1,0:T(8,128)(2,1)S(1)} all-gather(bf16[32,3584]{1,0:T(8,128)(2,1)S(1)} %all_gather.6), channel_id=1, replica_groups=mesh['zlo'=4,'x'=4,'y'=4,'zhi'=4,'core'=2] {'y'}, dimensions={0}, use_global_device_ids=true | all-gather | bytes 1146880 | tf_op jit(solution)/shard_map/all_gather | solution.py:192
  121.7 9.1 %collective-permute-start.10 = (bf16[128,3584]{1,0:T(8,128)(2,1)S(1)}, bf16[128,3584]{1,0:T(8,128)(2,1)S(1)}, u32[]{:S(2)}, u32[]{:S(2)}) collective-permute-start(bf16[128,3584]{1,0:T(8,128)(2,1)S(1)} %all_gather.7.mine_ref), channel_id=1, source_target_pairs={{0,1},{1,0},{2,3},{3,2},{4,5},{5,4},{6,7},{7,6},{8,9},{9,8},{10,11... | collective-permute-start | bytes 2752520 | tf_op jit(solution)/shard_map/ppermute | solution.py:20
  130.8 2.1 %collective-permute-done.10.theirs_ref = bf16[128,3584]{1,0:T(8,128)(2,1)S(1)} collective-permute-done((bf16[128,3584]{1,0:T(8,128)(2,1)S(1)}, bf16[128,3584]{1,0:T(8,128)(2,1)S(1)}, u32[]{:S(2)}, u32[]{:S(2)}) %collective-permute-start.10) | collective-permute-done | bytes 917536 | tf_op jit(solution)/shard_map/ppermute | solution.py:20
  132.9 2.0 %join_cores.1 = bf16[2,128,3584]{2,1,0:T(8,128)(2,1)} custom-call(s32[1]{0:T(128)} %bitcast.2.core_ref, bf16[128,3584]{1,0:T(8,128)(2,1)S(1)} %all_gather.7.mine_ref, bf16[128,3584]{1,0:T(8,128)(2,1)S(1)} %collective-permute-done.10.theirs_ref), custom_call_target="tpu_custom_call" | custom-call | tf_op jit(solution)/shard_map/join_cores/pallas_call | solution.py:154
  (1 shorter events, 0.0 us)
Async XLA Ops:
  0.7 1.5 %copy-start = (bf16[1,1,1,2,128,3584]{5,4,3,2,1,0:T(8,128)(2,1)S(1)}, bf16[1,1,1,2,128,3584]{5,4,3,2,1,0:T(8,128)(2,1)}, u32[]{:S(2)}) copy-start(bf16[1,1,1,2,128,3584]{5,4,3,2,1,0:T(8,128)(2,1)} %param.9) | copy-start | bytes 5505028
  3.6 10.9 %collective-permute-start.3 = (bf16[4,32,3584]{2,1,0:T(8,128)(2,1)S(1)}, bf16[4,32,3584]{2,1,0:T(8,128)(2,1)S(1)}, u32[]{:S(2)}, u32[]{:S(2)}) collective-permute-start(bf16[4,32,3584]{2,1,0:T(8,128)(2,1)S(1)} %get-tuple-element.25), channel_id=1, source_target_pairs={{0,1},{1,0},{2,3},{3,2},{4,5},{5,4},{6,7},{7,6},{8,9},{9,8},{10,11... | collective-permute-start | bytes 2752520 | tf_op jit(solution)/shard_map/ppermute | solution.py:20
  14.5 62.2 %copy-start.1 = (f32[1,2,4,3584]{3,2,1,0:T(4,128)S(1)}, f32[1,2,4,3584]{3,2,1,0:T(4,128)}, u32[]{:S(2)}) copy-start(f32[1,2,4,3584]{3,2,1,0:T(4,128)} %param.10) | copy-start | bytes 344068
  14.5 62.2 %copy-start.2 = (f32[1,2,4,3584]{3,2,1,0:T(4,128)S(1)}, f32[1,2,4,3584]{3,2,1,0:T(4,128)}, u32[]{:S(2)}) copy-start(f32[1,2,4,3584]{3,2,1,0:T(4,128)} %param.11) | copy-start | bytes 344068
  14.5 62.2 %copy-start.3 = (f32[1,2,4,3584]{3,2,1,0:T(4,128)S(1)}, f32[1,2,4,3584]{3,2,1,0:T(4,128)}, u32[]{:S(2)}) copy-start(f32[1,2,4,3584]{3,2,1,0:T(4,128)} %param.12) | copy-start | bytes 344068
  14.6 24.7 %collective-permute-start.4 = (f32[32,3584]{1,0:T(8,128)S(1)}, f32[32,3584]{1,0:T(8,128)S(1)}, u32[]{:S(2)}, u32[]{:S(2)}) collective-permute-start(f32[32,3584]{1,0:T(8,128)S(1)} %get-tuple-element.27), channel_id=1, source_target_pairs={{0,8},{8,16},{16,24},{24,0},{1,9},{9,17},{17,25},{25,1},{2,10},{10... | collective-permute-start | bytes 1376264 | tf_op jit(solution)/shard_map/ppermute | solution.py:20
  16.6 22.7 %collective-permute-start.5 = (f32[32,3584]{1,0:T(8,128)S(1)}, f32[32,3584]{1,0:T(8,128)S(1)}, u32[]{:S(2)}, u32[]{:S(2)}) collective-permute-start(f32[32,3584]{1,0:T(8,128)S(1)} %get-tuple-element.28), channel_id=1, source_target_pairs={{0,16},{8,24},{16,0},{24,8},{1,17},{9,25},{17,1},{25,9},{2,18},{10... | collective-permute-start | bytes 1376264 | tf_op jit(solution)/shard_map/ppermute | solution.py:20
  18.5 23.0 %collective-permute-start.6 = (f32[32,3584]{1,0:T(8,128)S(1)}, f32[32,3584]{1,0:T(8,128)S(1)}, u32[]{:S(2)}, u32[]{:S(2)}) collective-permute-start(f32[32,3584]{1,0:T(8,128)S(1)} %get-tuple-element.29), channel_id=1, source_target_pairs={{0,24},{8,0},{16,8},{24,16},{1,25},{9,1},{17,9},{25,17},{2,26},{10... | collective-permute-start | bytes 1376264 | tf_op jit(solution)/shard_map/ppermute | solution.py:20
  41.6 20.3 %collective-permute-start.7 = (f32[8,3584]{1,0:T(8,128)S(1)}, f32[8,3584]{1,0:T(8,128)S(1)}, u32[]{:S(2)}, u32[]{:S(2)}) collective-permute-start(f32[8,3584]{1,0:T(8,128)S(1)} %get-tuple-element.31), channel_id=1, source_target_pairs={{0,2},{2,4},{4,6},{6,0},{1,3},{3,5},{5,7},{7,1},{8,10},{10,12},{12... | collective-permute-start | bytes 344072 | tf_op jit(solution)/shard_map/ppermute | solution.py:20
  45.2 22.7 %collective-permute-start.8 = (f32[8,3584]{1,0:T(8,128)S(1)}, f32[8,3584]{1,0:T(8,128)S(1)}, u32[]{:S(2)}, u32[]{:S(2)}) collective-permute-start(f32[8,3584]{1,0:T(8,128)S(1)} %get-tuple-element.32), channel_id=1, source_target_pairs={{0,4},{2,6},{4,0},{6,2},{1,5},{3,7},{5,1},{7,3},{8,12},{10,14},{12... | collective-permute-start | bytes 344072 | tf_op jit(solution)/shard_map/ppermute | solution.py:20
  55.9 20.8 %collective-permute-start.9 = (f32[8,3584]{1,0:T(8,128)S(1)}, f32[8,3584]{1,0:T(8,128)S(1)}, u32[]{:S(2)}, u32[]{:S(2)}) collective-permute-start(f32[8,3584]{1,0:T(8,128)S(1)} %get-tuple-element.33), channel_id=1, source_target_pairs={{0,6},{2,0},{4,2},{6,4},{1,7},{3,1},{5,3},{7,5},{8,14},{10,8},{12,... | collective-permute-start | bytes 344072 | tf_op jit(solution)/shard_map/ppermute | solution.py:20
  78.0 10.4 %collective-permute-start.1 = (f32[2,4,3584]{2,1,0:T(4,128)S(1)}, f32[2,4,3584]{2,1,0:T(4,128)}, u32[]{:S(2)}, u32[]{:S(2)}) collective-permute-start(f32[2,4,3584]{2,1,0:T(4,128)S(1)} %param.1), channel_id=1, source_target_pairs={{0,64},{32,96},{64,128},{96,160},{128,192},{160,224},{192,256},{22... | collective-permute-start | bytes 344072 | tf_op jit(solution)/shard_map/cond/branch_1_fun/ppermute | solution.py:20
  121.7 11.1 %collective-permute-start.10 = (bf16[128,3584]{1,0:T(8,128)(2,1)S(1)}, bf16[128,3584]{1,0:T(8,128)(2,1)S(1)}, u32[]{:S(2)}, u32[]{:S(2)}) collective-permute-start(bf16[128,3584]{1,0:T(8,128)(2,1)S(1)} %all_gather.7.mine_ref), channel_id=1, source_target_pairs={{0,1},{1,0},{2,3},{3,2},{4,5},{5,4},{6,7},{7,6},{8,9},{9,8},{10,11... | collective-permute-start | bytes 2752520 | tf_op jit(solution)/shard_map/ppermute | solution.py:20

commit v2 on v1

--- a/solution.py
+++ b/solution.py
@@ -18,6 +18,15 @@
 def shifted(block, axis, distance):
     n = lax.axis_size(axis)
     return lax.ppermute(block, axis, [(i, (i + distance) % n) for i in range(n)])
+
+
+def turned(block, distance):
+    n = lax.axis_size("zhi")
+    pairs = []
+    for z in range(n):
+        pairs.append((2 * z, 2 * ((z + distance) % n)))
+        pairs.append((2 * z + 1, 2 * ((z - distance) % n) + 1))
+    return lax.ppermute(block, ("zhi", "core"), pairs)
 
 
 def low_high(a, b):
@@ -84,11 +93,12 @@
 def add_four_kernel(z_ref, a_ref, b_ref, c_ref, d_ref, *outs):
     n = len(outs)
     for k, out in enumerate(outs):
-        at = pl.ds(pl.multiple_of(((z_ref[0] + k) % n) * 8, 8), 8)
+        step = jnp.where(z_ref[1] == 0, k, n - k)
+        at = pl.ds(pl.multiple_of(((z_ref[0] + step) % n) * 8, 8), 8)
         out[...] = (a_ref[at, :] + b_ref[at, :]) + (c_ref[at, :] + d_ref[at, :])
 
 
-def add_four(z, parts):
+def add_four(z, core, parts):
     rows, depth = parts[0].shape
     n = rows // 8
     out = jax.ShapeDtypeStruct((8, depth), F32)
@@ -99,11 +109,11 @@
         out_shape=[out] * n,
         compiler_params=PARAMS,
         name="add_four",
-    )(z.astype(jnp.int32)[None], *parts)
-
-
-def adam_kernel(corr_ref, a_ref, b_ref, c_ref, d_ref, master_ref, first_ref, second_ref, nf_ref, ns_ref, up_ref):
-    mean_all = ((a_ref[...] + b_ref[...]) + (c_ref[...] + d_ref[...])) * (1.0 / 32)
+    )(jnp.stack([z, core]).astype(jnp.int32), *parts)
+
+
+def adam_kernel(corr_ref, a_ref, b_ref, c_ref, master_ref, first_ref, second_ref, nf_ref, ns_ref, up_ref):
+    mean_all = (a_ref[...] + (b_ref[...] + c_ref[...])) * (1.0 / 32)
     for layer in range(2):
         mean = mean_all[4 * layer : 4 * layer + 4]
         master = master_ref[layer]
@@ -120,7 +130,7 @@
     out = jax.ShapeDtypeStruct(master.shape, F32)
     return pl.pallas_call(
         adam_kernel,
-        in_specs=[SMEM] + [VMEM] * 7,
+        in_specs=[SMEM] + [VMEM] * 6,
         out_specs=[VMEM] * 3,
         out_shape=[out] * 3,
         compiler_params=PARAMS,
@@ -174,11 +184,12 @@
 
     mine, theirs = split_cores(grads[0, 0, 0], y, core)
     parts = add_pair(mine, shifted(theirs, "core", 1))
-    two = shifted(parts[2], "y", 2)
-    parts = [parts[0], shifted(parts[1], "y", 1), two, shifted(parts[3], "y", 3)]
-    parts = add_four(z, parts)
-    two = shifted(parts[2], "zhi", 2)
-    parts = [parts[0], shifted(parts[1], "zhi", 1), two, shifted(parts[3], "zhi", 3)]
+    one, three, two = (shifted(parts[k], "y", k) for k in (1, 3, 2))
+    own, near, far, back = add_four(z, core, [one, three, two, parts[0]])
+    through = turned(far, 1)
+    back = turned(back, -1)
+    near = turned(near + through, 1)
+    parts = [own, back, near]
     new_first, new_second, updated = adam(
         corr, parts, master[0], first_moment[0], second_moment[0]
     )

time: 135 us -> 126 us (0.933)
  waiting for transfers between devices: 43.1 us -> 28.1 us
  starting transfers between devices: 50.3 us -> 57.9 us
  blocking collectives: 31.8 us -> 29.2 us
    ppermute x9 -> x6, waiting for transfers between devices: 43.1 us -> 22.1 us  [shifted(): lax.ppermute(block, axis, [(i, (i + distance) % n) for i in range(n)])]
    ppermute x0 -> x3, starting transfers between devices: none -> 17.3 us  [turned(): return lax.ppermute(block, ('zhi', 'core'), pairs)]
    ppermute x9 -> x6, starting transfers between devices: 50.3 us -> 40.7 us  [shifted(): lax.ppermute(block, axis, [(i, (i + distance) % n) for i in range(n)])]
    ppermute x0 -> x3, waiting for transfers between devices: none -> 6.02 us  [turned(): return lax.ppermute(block, ('zhi', 'core'), pairs)]
    all_gather x1, blocking collectives: 13.6 us -> 11.1 us  [body(): whole = lax.all_gather(whole, 'y', axis=0, tiled=True)]
where the time goes in v2:
time: 126 us
  starting transfers between devices  57.9 us (46%)
  blocking collectives  29.2 us (23%)
  waiting for transfers between devices  28.1 us (22%)
  Pallas kernels  5.44 us (4%)
  other arithmetic  1.83 us (1%)
  local copies, waits for them, and re-layouts  1.53 us (1%)
  between operations  1.49 us (1%)
    ppermute x6, starting transfers between devices, shifted(): lax.ppermute(block, axis, [(i, (i + distance) % n) for i in range(n)])  40.7 us
    ppermute x6, waiting for transfers between devices, shifted(): lax.ppermute(block, axis, [(i, (i + distance) % n) for i in range(n)])  22.1 us
    all_gather x1, blocking collectives, body(): whole = lax.all_gather(whole, 'zhi', axis=0, tiled=True)  18.1 us
    ppermute x3, starting transfers between devices, turned(): return lax.ppermute(block, ('zhi', 'core'), pairs)  17.3 us
    all_gather x1, blocking collectives, body(): whole = lax.all_gather(whole, 'y', axis=0, tiled=True)  11.1 us
    ppermute x3, waiting for transfers between devices, turned(): return lax.ppermute(block, ('zhi', 'core'), pairs)  6.02 us
  transfers between devices with their start and end apart: 9, of which 7 were waited for; matrix products, arithmetic and copies ran while one was open for 0% of the time, Pallas kernels for 0%

profile of v2, /device:TPU:1, one launch (start us, length us, event | category | flops | bytes accessed | tf_op | source)
XLA Modules:
  0.0 125.5 jit_solution(7252818114842529658)
XLA Ops:
  0.6 0.1 pad_add_fusion.1.where_ref
  0.7 0.0 copy-start
  0.7 1.5 %copy-done = bf16[1,1,1,2,128,3584]{5,4,3,2,1,0:T(8,128)(2,1)S(1)} copy-done((bf16[1,1,1,2,128,3584]{5,4,3,2,1,0:T(8,128)(2,1)S(1)}, bf16[1,1,1,2,128,3584]{5,4,3,2,1,0:T(8,128)(2,1)}, u32[]{:S(2)}) %copy-start) | copy-done | bytes 1835032
  2.2 1.4 %split_cores.1 = (bf16[4,32,3584]{2,1,0:T(8,128)(2,1)S(1)}, bf16[4,32,3584]{2,1,0:T(8,128)(2,1)S(1)}) custom-call(s32[2]{0:T(128)S(1)} %pad_add_fusion.1.where_ref, bf16[2,128,3584]{2,1,0:T(8,128)(2,1)S(1)} %bitcast.13), custom_call_target="tpu_custom_call" | custom-call | tf_op jit(solution)/shard_map/split_cores/pallas_call | solution.py:61
  3.6 8.8 %collective-permute-start.3 = (bf16[4,32,3584]{2,1,0:T(8,128)(2,1)S(1)}, bf16[4,32,3584]{2,1,0:T(8,128)(2,1)S(1)}, u32[]{:S(2)}, u32[]{:S(2)}) collective-permute-start(bf16[4,32,3584]{2,1,0:T(8,128)(2,1)S(1)} %get-tuple-element.25), channel_id=1, source_target_pairs={{0,1},{1,0},{2,3},{3,2},{4,5},{5,4},{6,7},{7,6},{8,9},{9,8},{10,11... | collective-permute-start | bytes 2752520 | tf_op jit(solution)/shard_map/ppermute | solution.py:20
  12.4 2.1 %collective-permute-done.3.theirs_ref = bf16[4,32,3584]{2,1,0:T(8,128)(2,1)S(1)} collective-permute-done((bf16[4,32,3584]{2,1,0:T(8,128)(2,1)S(1)}, bf16[4,32,3584]{2,1,0:T(8,128)(2,1)S(1)}, u32[]{:S(2)}, u32[]{:S(2)}) %collective-permute-start.3) | collective-permute-done | bytes 917536 | tf_op jit(solution)/shard_map/ppermute | solution.py:20
  14.5 0.0 copy-start.1
  14.5 0.0 copy-start.2
  14.5 0.0 copy-start.3
  14.5 0.2 add_pair.1
  14.7 1.9 %collective-permute-start.4 = (f32[32,3584]{1,0:T(8,128)S(1)}, f32[32,3584]{1,0:T(8,128)S(1)}, u32[]{:S(2)}, u32[]{:S(2)}) collective-permute-start(f32[32,3584]{1,0:T(8,128)S(1)} %get-tuple-element.26), channel_id=1, source_target_pairs={{0,8},{8,16},{16,24},{24,0},{1,9},{9,17},{17,25},{25,1},{2,10},{10... | collective-permute-start | bytes 1376264 | tf_op jit(solution)/shard_map/ppermute | solution.py:20
  16.6 4.6 %collective-permute-start.5 = (f32[32,3584]{1,0:T(8,128)S(1)}, f32[32,3584]{1,0:T(8,128)S(1)}, u32[]{:S(2)}, u32[]{:S(2)}) collective-permute-start(f32[32,3584]{1,0:T(8,128)S(1)} %get-tuple-element.27), channel_id=1, source_target_pairs={{0,24},{8,0},{16,8},{24,16},{1,25},{9,1},{17,9},{25,17},{2,26},{10... | collective-permute-start | bytes 1376264 | tf_op jit(solution)/shard_map/ppermute | solution.py:20
  21.2 1.9 %collective-permute-start.6 = (f32[32,3584]{1,0:T(8,128)S(1)}, f32[32,3584]{1,0:T(8,128)S(1)}, u32[]{:S(2)}, u32[]{:S(2)}) collective-permute-start(f32[32,3584]{1,0:T(8,128)S(1)} %get-tuple-element.28), channel_id=1, source_target_pairs={{0,16},{8,24},{16,0},{24,8},{1,17},{9,25},{17,1},{25,9},{2,18},{10... | collective-permute-start | bytes 1376264 | tf_op jit(solution)/shard_map/ppermute | solution.py:20
  23.1 0.1 pad_add_fusion.z_ref
  23.2 16.1 %collective-permute-done.4.a_ref = f32[32,3584]{1,0:T(8,128)S(1)} collective-permute-done((f32[32,3584]{1,0:T(8,128)S(1)}, f32[32,3584]{1,0:T(8,128)S(1)}, u32[]{:S(2)}, u32[]{:S(2)}) %collective-permute-start.4) | collective-permute-done | bytes 458784 | tf_op jit(solution)/shard_map/ppermute | solution.py:20
  39.3 0.0 collective-permute-done.5.b_ref
  39.3 0.0 collective-permute-done.6.c_ref
  39.3 0.6 add_four.1
  40.0 8.3 %collective-permute-start.8 = (f32[8,3584]{1,0:T(8,128)S(1)}, f32[8,3584]{1,0:T(8,128)S(1)}, u32[]{:S(2)}, u32[]{:S(2)}) collective-permute-start(f32[8,3584]{1,0:T(8,128)S(1)} %get-tuple-element.33), channel_id=1, source_target_pairs={{0,2},{1,7},{2,4},{3,1},{4,6},{5,3},{6,0},{7,5},{8,10},{9,15},{10,... | collective-permute-start | bytes 344072 | tf_op jit(solution)/shard_map/ppermute | solution.py:29
  48.3 1.9 %collective-permute-start.7 = (f32[8,3584]{1,0:T(8,128)S(1)}, f32[8,3584]{1,0:T(8,128)S(1)}, u32[]{:S(2)}, u32[]{:S(2)}) collective-permute-start(f32[8,3584]{1,0:T(8,128)S(1)} %get-tuple-element.31), channel_id=1, source_target_pairs={{0,6},{1,3},{2,0},{3,5},{4,2},{5,7},{6,4},{7,1},{8,14},{9,11},{10,... | collective-permute-start | bytes 344072 | tf_op jit(solution)/shard_map/ppermute | solution.py:29
  50.2 2.0 %collective-permute-done.8 = f32[8,3584]{1,0:T(8,128)S(1)} collective-permute-done((f32[8,3584]{1,0:T(8,128)S(1)}, f32[8,3584]{1,0:T(8,128)S(1)}, u32[]{:S(2)}, u32[]{:S(2)}) %collective-permute-start.8) | collective-permute-done | bytes 114720 | tf_op jit(solution)/shard_map/ppermute | solution.py:29
  52.2 7.0 %collective-permute-start.9 = (f32[8,3584]{1,0:T(8,128)S(1)}, f32[8,3584]{1,0:T(8,128)S(1)}, u32[]{:S(2)}, u32[]{:S(2)}) collective-permute-start(f32[8,3584]{1,0:T(8,128)S(1)} %add.15), channel_id=1, source_target_pairs={{0,2},{1,7},{2,4},{3,1},{4,6},{5,3},{6,0},{7,5},{8,10},{9,15},{10,... | collective-permute-start | bytes 344072 | tf_op jit(solution)/shard_map/ppermute | solution.py:29
  60.0 0.1 pad_maximum_fusion.corr_ref
  60.1 1.7 %collective-permute-done.7.b_ref = f32[8,3584]{1,0:T(8,128)S(1)} collective-permute-done((f32[8,3584]{1,0:T(8,128)S(1)}, f32[8,3584]{1,0:T(8,128)S(1)}, u32[]{:S(2)}, u32[]{:S(2)}) %collective-permute-start.7) | collective-permute-done | bytes 114720 | tf_op jit(solution)/shard_map/ppermute | solution.py:29
  61.9 2.3 %collective-permute-done.9.c_ref = f32[8,3584]{1,0:T(8,128)S(1)} collective-permute-done((f32[8,3584]{1,0:T(8,128)S(1)}, f32[8,3584]{1,0:T(8,128)S(1)}, u32[]{:S(2)}, u32[]{:S(2)}) %collective-permute-start.9) | collective-permute-done | bytes 114720 | tf_op jit(solution)/shard_map/ppermute | solution.py:29
  64.1 0.0 copy-done.1
  64.1 0.0 copy-done.2
  64.1 0.0 copy-done.3
  64.1 1.3 %adam.1 = (f32[2,4,3584]{2,1,0:T(4,128)}, f32[2,4,3584]{2,1,0:T(4,128)}, f32[2,4,3584]{2,1,0:T(4,128)S(1)}) custom-call(f32[2]{0:T(128)S(1)} %pad_maximum_fusion.corr_ref, f32[8,3584]{1,0:T(8,128)S(1)} %get-tuple-element.30.a_ref, f32[8,3584]{1,0:T(8,128)S(1)} %collective-permute-done.7.b_ref, f32[8,3584]{1,0:T(8,128)S(1)} %collective-permute-done.9.c_ref, ...), custom_call_target="tpu_custom_call" | custom-call | tf_op jit(solution)/shard_map/adam/pallas_call | solution.py:131
  65.4 7.8 %conditional.1 = (f32[2,4,3584]{2,1,0:T(4,128)}) conditional(s32[]{:T(128)} %clamp.3, f32[2,4,3584]{2,1,0:T(4,128)S(1)} %get-tuple-element.34, f32[2,4,3584]{2,1,0:T(4,128)S(1)} %get-tuple-element.34, f32[2,4,3584]{2,1,0:T(4,128)S(1)} %get-tuple-element.34), branch_computations={%region_0.1_spmd, %region_1.2_spmd, %region_2.3_spmd} | conditional | bytes 458800 | solution.py:196
  65.4 6.0 %collective-permute-start.2 = (f32[2,4,3584]{2,1,0:T(4,128)S(1)}, f32[2,4,3584]{2,1,0:T(4,128)}, u32[]{:S(2)}, u32[]{:S(2)}) collective-permute-start(f32[2,4,3584]{2,1,0:T(4,128)S(1)} %param.2), channel_id=1, source_target_pairs={{0,128},{32,160},{64,192},{96,224},{128,256},{160,288},{192,320},{... | collective-permute-start | bytes 344072 | tf_op jit(solution)/shard_map/cond/branch_2_fun/ppermute | solution.py:20
  71.5 1.8 %collective-permute-done.2 = f32[2,4,3584]{2,1,0:T(4,128)} collective-permute-done((f32[2,4,3584]{2,1,0:T(4,128)S(1)}, f32[2,4,3584]{2,1,0:T(4,128)}, u32[]{:S(2)}, u32[]{:S(2)}) %collective-permute-start.2) | collective-permute-done | bytes 114720 | tf_op jit(solution)/shard_map/cond/branch_2_fun/ppermute | solution.py:20
  73.3 1.6 %fusion = (bf16[2,4,3584]{2,1,0:T(4,128)(2,1)S(1)}, f32[1,2,4,3584]{3,2,1,0:T(4,128)}) fusion(f32[2,4,3584]{2,1,0:T(4,128)S(1)} %get-tuple-element.34, f32[2,4,3584]{2,1,0:T(4,128)} %get-tuple-element.39), kind=kLoop, calls=%fused_computation.1 | loop fusion | flops 86016 | bytes 401408 | tf_op jit(solution)/shard_map/convert_element_type | solution.py:201
  74.9 18.1 %all_gather.6 = bf16[32,3584]{1,0:T(8,128)(2,1)S(1)} all-gather(bf16[8,3584]{1,0:T(8,128)(2,1)S(1)} %reshape.26), channel_id=1, replica_groups=mesh['zlo'=4,'x'=4,'y'=4,'zhi'=4,'core'=2] {'zhi'}, dimensions={0}, use_global_device_ids=true | all-gather | bytes 286720 | tf_op jit(solution)/shard_map/all_gather | solution.py:202
  92.9 11.1 %all_gather.7.mine_ref = bf16[128,3584]{1,0:T(8,128)(2,1)S(1)} all-gather(bf16[32,3584]{1,0:T(8,128)(2,1)S(1)} %all_gather.6), channel_id=1, replica_groups=mesh['zlo'=4,'x'=4,'y'=4,'zhi'=4,'core'=2] {'y'}, dimensions={0}, use_global_device_ids=true | all-gather | bytes 1146880 | tf_op jit(solution)/shard_map/all_gather | solution.py:203
  104.0 17.4 %collective-permute-start.10 = (bf16[128,3584]{1,0:T(8,128)(2,1)S(1)}, bf16[128,3584]{1,0:T(8,128)(2,1)S(1)}, u32[]{:S(2)}, u32[]{:S(2)}) collective-permute-start(bf16[128,3584]{1,0:T(8,128)(2,1)S(1)} %all_gather.7.mine_ref), channel_id=1, source_target_pairs={{0,1},{1,0},{2,3},{3,2},{4,5},{5,4},{6,7},{7,6},{8,9},{9,8},{10,11... | collective-permute-start | bytes 2752520 | tf_op jit(solution)/shard_map/ppermute | solution.py:20
  121.5 2.1 %collective-permute-done.10.theirs_ref = bf16[128,3584]{1,0:T(8,128)(2,1)S(1)} collective-permute-done((bf16[128,3584]{1,0:T(8,128)(2,1)S(1)}, bf16[128,3584]{1,0:T(8,128)(2,1)S(1)}, u32[]{:S(2)}, u32[]{:S(2)}) %collective-permute-start.10) | collective-permute-done | bytes 917536 | tf_op jit(solution)/shard_map/ppermute | solution.py:20
  123.6 2.0 %join_cores.1 = bf16[2,128,3584]{2,1,0:T(8,128)(2,1)} custom-call(s32[1]{0:T(128)} %bitcast.1.core_ref, bf16[128,3584]{1,0:T(8,128)(2,1)S(1)} %all_gather.7.mine_ref, bf16[128,3584]{1,0:T(8,128)(2,1)S(1)} %collective-permute-done.10.theirs_ref), custom_call_target="tpu_custom_call" | custom-call | tf_op jit(solution)/shard_map/join_cores/pallas_call | solution.py:164
  (2 shorter events, 0.0 us)
Async XLA Ops:
  0.7 1.5 %copy-start = (bf16[1,1,1,2,128,3584]{5,4,3,2,1,0:T(8,128)(2,1)S(1)}, bf16[1,1,1,2,128,3584]{5,4,3,2,1,0:T(8,128)(2,1)}, u32[]{:S(2)}) copy-start(bf16[1,1,1,2,128,3584]{5,4,3,2,1,0:T(8,128)(2,1)} %param.9) | copy-start | bytes 5505028
  3.6 10.9 %collective-permute-start.3 = (bf16[4,32,3584]{2,1,0:T(8,128)(2,1)S(1)}, bf16[4,32,3584]{2,1,0:T(8,128)(2,1)S(1)}, u32[]{:S(2)}, u32[]{:S(2)}) collective-permute-start(bf16[4,32,3584]{2,1,0:T(8,128)(2,1)S(1)} %get-tuple-element.25), channel_id=1, source_target_pairs={{0,1},{1,0},{2,3},{3,2},{4,5},{5,4},{6,7},{7,6},{8,9},{9,8},{10,11... | collective-permute-start | bytes 2752520 | tf_op jit(solution)/shard_map/ppermute | solution.py:20
  14.5 49.7 %copy-start.1 = (f32[1,2,4,3584]{3,2,1,0:T(4,128)S(1)}, f32[1,2,4,3584]{3,2,1,0:T(4,128)}, u32[]{:S(2)}) copy-start(f32[1,2,4,3584]{3,2,1,0:T(4,128)} %param.10) | copy-start | bytes 344068
  14.5 49.7 %copy-start.2 = (f32[1,2,4,3584]{3,2,1,0:T(4,128)S(1)}, f32[1,2,4,3584]{3,2,1,0:T(4,128)}, u32[]{:S(2)}) copy-start(f32[1,2,4,3584]{3,2,1,0:T(4,128)} %param.11) | copy-start | bytes 344068
  14.5 49.7 %copy-start.3 = (f32[1,2,4,3584]{3,2,1,0:T(4,128)S(1)}, f32[1,2,4,3584]{3,2,1,0:T(4,128)}, u32[]{:S(2)}) copy-start(f32[1,2,4,3584]{3,2,1,0:T(4,128)} %param.12) | copy-start | bytes 344068
  14.7 24.7 %collective-permute-start.4 = (f32[32,3584]{1,0:T(8,128)S(1)}, f32[32,3584]{1,0:T(8,128)S(1)}, u32[]{:S(2)}, u32[]{:S(2)}) collective-permute-start(f32[32,3584]{1,0:T(8,128)S(1)} %get-tuple-element.26), channel_id=1, source_target_pairs={{0,8},{8,16},{16,24},{24,0},{1,9},{9,17},{17,25},{25,1},{2,10},{10... | collective-permute-start | bytes 1376264 | tf_op jit(solution)/shard_map/ppermute | solution.py:20
  16.6 22.7 %collective-permute-start.5 = (f32[32,3584]{1,0:T(8,128)S(1)}, f32[32,3584]{1,0:T(8,128)S(1)}, u32[]{:S(2)}, u32[]{:S(2)}) collective-permute-start(f32[32,3584]{1,0:T(8,128)S(1)} %get-tuple-element.27), channel_id=1, source_target_pairs={{0,24},{8,0},{16,8},{24,16},{1,25},{9,1},{17,9},{25,17},{2,26},{10... | collective-permute-start | bytes 1376264 | tf_op jit(solution)/shard_map/ppermute | solution.py:20
  21.2 18.2 %collective-permute-start.6 = (f32[32,3584]{1,0:T(8,128)S(1)}, f32[32,3584]{1,0:T(8,128)S(1)}, u32[]{:S(2)}, u32[]{:S(2)}) collective-permute-start(f32[32,3584]{1,0:T(8,128)S(1)} %get-tuple-element.28), channel_id=1, source_target_pairs={{0,16},{8,24},{16,0},{24,8},{1,17},{9,25},{17,1},{25,9},{2,18},{10... | collective-permute-start | bytes 1376264 | tf_op jit(solution)/shard_map/ppermute | solution.py:20
  40.0 12.2 %collective-permute-start.8 = (f32[8,3584]{1,0:T(8,128)S(1)}, f32[8,3584]{1,0:T(8,128)S(1)}, u32[]{:S(2)}, u32[]{:S(2)}) collective-permute-start(f32[8,3584]{1,0:T(8,128)S(1)} %get-tuple-element.33), channel_id=1, source_target_pairs={{0,2},{1,7},{2,4},{3,1},{4,6},{5,3},{6,0},{7,5},{8,10},{9,15},{10,... | collective-permute-start | bytes 344072 | tf_op jit(solution)/shard_map/ppermute | solution.py:29
  48.3 13.6 %collective-permute-start.7 = (f32[8,3584]{1,0:T(8,128)S(1)}, f32[8,3584]{1,0:T(8,128)S(1)}, u32[]{:S(2)}, u32[]{:S(2)}) collective-permute-start(f32[8,3584]{1,0:T(8,128)S(1)} %get-tuple-element.31), channel_id=1, source_target_pairs={{0,6},{1,3},{2,0},{3,5},{4,2},{5,7},{6,4},{7,1},{8,14},{9,11},{10,... | collective-permute-start | bytes 344072 | tf_op jit(solution)/shard_map/ppermute | solution.py:29
  52.2 11.9 %collective-permute-start.9 = (f32[8,3584]{1,0:T(8,128)S(1)}, f32[8,3584]{1,0:T(8,128)S(1)}, u32[]{:S(2)}, u32[]{:S(2)}) collective-permute-start(f32[8,3584]{1,0:T(8,128)S(1)} %add.15), channel_id=1, source_target_pairs={{0,2},{1,7},{2,4},{3,1},{4,6},{5,3},{6,0},{7,5},{8,10},{9,15},{10,... | collective-permute-start | bytes 344072 | tf_op jit(solution)/shard_map/ppermute | solution.py:29
  65.4 7.8 %collective-permute-start.2 = (f32[2,4,3584]{2,1,0:T(4,128)S(1)}, f32[2,4,3584]{2,1,0:T(4,128)}, u32[]{:S(2)}, u32[]{:S(2)}) collective-permute-start(f32[2,4,3584]{2,1,0:T(4,128)S(1)} %param.2), channel_id=1, source_target_pairs={{0,128},{32,160},{64,192},{96,224},{128,256},{160,288},{192,320},{... | collective-permute-start | bytes 344072 | tf_op jit(solution)/shard_map/cond/branch_2_fun/ppermute | solution.py:20
  104.0 19.5 %collective-permute-start.10 = (bf16[128,3584]{1,0:T(8,128)(2,1)S(1)}, bf16[128,3584]{1,0:T(8,128)(2,1)S(1)}, u32[]{:S(2)}, u32[]{:S(2)}) collective-permute-start(bf16[128,3584]{1,0:T(8,128)(2,1)S(1)} %all_gather.7.mine_ref), channel_id=1, source_target_pairs={{0,1},{1,0},{2,3},{3,2},{4,5},{5,4},{6,7},{7,6},{8,9},{9,8},{10,11... | collective-permute-start | bytes 2752520 | tf_op jit(solution)/shard_map/ppermute | solution.py:20

commit v3 on v1

--- a/solution.py
+++ b/solution.py
@@ -27,8 +27,8 @@
     return low, high
 
 
-def split_kernel(where_ref, grads_ref, mine_ref, theirs_ref):
-    first = where_ref[1] == 0
+def split_kernel(core_ref, grads_ref, mine_ref, theirs_ref):
+    first = core_ref[0] == 0
     depth = grads_ref.shape[-1]
     for at in range(0, depth, LANES):
         cols = slice(at, at + LANES)
@@ -43,7 +43,7 @@
         theirs_ref[0, :, cols] = jnp.concatenate(theirs, 0).astype(BF16)
 
 
-def split_cores(grads, y, core):
+def split_cores(grads, core):
     layers, rows, depth = grads.shape
     ny = lax.axis_size("y")
     per = rows // ny
@@ -54,56 +54,104 @@
         grid_spec=pltpu.PrefetchScalarGridSpec(
             num_scalar_prefetch=1,
             grid=(ny,),
-            in_specs=[pl.BlockSpec((layers, per, depth), lambda k, w: (0, (w[0] + k) % ny, 0))],
+            in_specs=[pl.BlockSpec((layers, per, depth), lambda k, w: (0, k, 0))],
             out_specs=[block, block],
         ),
         out_shape=(out, out),
         compiler_params=PARAMS,
         name="split_cores",
-    )(jnp.stack([y, core]).astype(jnp.int32), grads)
-
-
-def add_pair_kernel(mine_ref, theirs_ref, *outs):
-    for k, out in enumerate(outs):
-        out[...] = mine_ref[k].astype(F32) + theirs_ref[k].astype(F32)
-
-
-def add_pair(mine, theirs):
+    )(core.astype(jnp.int32)[None], grads)
+
+
+def scale_of(largest):
+    exponent = 14.0 - jnp.floor(jnp.log2(jnp.maximum(largest, 1e-30)))
+    return jnp.exp2(exponent), -exponent
+
+
+def send_scaled(out_ref, sums):
+    n, per, _ = out_ref.shape
+    depth = sums.shape[-1]
+    largest = jnp.zeros((8, LANES), F32)
+    for at in range(0, depth, LANES):
+        for r in range(0, n * per, 8):
+            largest = jnp.maximum(largest, jnp.abs(sums[r : r + 8, at : at + LANES]))
+    scale, back = scale_of(jnp.max(largest, axis=(0, 1), keepdims=True))
+    for k in range(n):
+        for at in range(0, depth, LANES):
+            cols = slice(at, at + LANES)
+            out_ref[k, :, cols] = sums[k * per : (k + 1) * per, cols] * scale
+        out_ref[k, :, depth:] = jnp.broadcast_to(back, (per, out_ref.shape[-1] - depth))
+
+
+def add_received(total, got_ref, me, cols, depth):
+    for k in range(got_ref.shape[0]):
+        undo = jnp.exp2(got_ref[k, 0:1, depth : depth + 1])
+        total = total + jnp.where(me == k, 0.0, got_ref[k, :, cols] * undo)
+    return total
+
+
+def add_pair_kernel(y_ref, mine_ref, theirs_ref, own_ref, out_ref, sums):
+    n, per, depth = mine_ref.shape
+    for k in range(n):
+        for at in range(0, depth, LANES):
+            cols = slice(at, at + LANES)
+            sums[k * per : (k + 1) * per, cols] = mine_ref[k, :, cols].astype(F32) + theirs_ref[
+                k, :, cols
+            ].astype(F32)
+    own_ref[...] = sums[pl.ds(pl.multiple_of(y_ref[0] * per, per), per), :]
+    send_scaled(out_ref, sums)
+
+
+def add_pair(y, mine, theirs):
     n, rows, depth = mine.shape
-    out = jax.ShapeDtypeStruct((rows, depth), F32)
     return pl.pallas_call(
         add_pair_kernel,
-        in_specs=[VMEM, VMEM],
-        out_specs=[VMEM] * n,
-        out_shape=[out] * n,
+        in_specs=[SMEM, VMEM, VMEM],
+        out_specs=[VMEM] * 2,
+        out_shape=[
+            jax.ShapeDtypeStruct((rows, depth), F32),
+            jax.ShapeDtypeStruct((n, rows, depth + 128), F32),
+        ],
+        scratch_shapes=[pltpu.VMEM((n * rows, depth), F32)],
         compiler_params=PARAMS,
         name="add_pair",
-    )(mine, theirs)
-
-
-def add_four_kernel(z_ref, a_ref, b_ref, c_ref, d_ref, *outs):
-    n = len(outs)
-    for k, out in enumerate(outs):
-        at = pl.ds(pl.multiple_of(((z_ref[0] + k) % n) * 8, 8), 8)
-        out[...] = (a_ref[at, :] + b_ref[at, :]) + (c_ref[at, :] + d_ref[at, :])
-
-
-def add_four(z, parts):
-    rows, depth = parts[0].shape
-    n = rows // 8
-    out = jax.ShapeDtypeStruct((8, depth), F32)
-    return pl.pallas_call(
-        add_four_kernel,
-        in_specs=[SMEM] + [VMEM] * 4,
-        out_specs=[VMEM] * n,
-        out_shape=[out] * n,
-        compiler_params=PARAMS,
-        name="add_four",
-    )(z.astype(jnp.int32)[None], *parts)
-
-
-def adam_kernel(corr_ref, a_ref, b_ref, c_ref, d_ref, master_ref, first_ref, second_ref, nf_ref, ns_ref, up_ref):
-    mean_all = ((a_ref[...] + b_ref[...]) + (c_ref[...] + d_ref[...])) * (1.0 / 32)
+    )(y.astype(jnp.int32)[None], mine, theirs)
+
+
+def add_y_kernel(at_ref, own_ref, got_ref, keep_ref, out_ref, sums):
+    depth = own_ref.shape[-1]
+    for at in range(0, depth, LANES):
+        cols = slice(at, at + LANES)
+        sums[:, cols] = add_received(own_ref[:, cols], got_ref, at_ref[0], cols, depth)
+    keep_ref[...] = sums[pl.ds(pl.multiple_of(at_ref[1] * 8, 8), 8), :]
+    send_scaled(out_ref, sums)
+
+
+def add_y(y, z, own, got):
+    rows, depth = own.shape
+    return pl.pallas_call(
+        add_y_kernel,
+        in_specs=[SMEM, VMEM, VMEM],
+        out_specs=[VMEM] * 2,
+        out_shape=[
+            jax.ShapeDtypeStruct((8, depth), F32),
+            jax.ShapeDtypeStruct((rows // 8, 8, depth + 128), F32),
+        ],
+        scratch_shapes=[pltpu.VMEM((rows, depth), F32)],
+        compiler_params=PARAMS,
+        name="add_y",
+    )(jnp.stack([y, z]).astype(jnp.int32), own, got)
+
+
+def exchanged(blocks, axis):
+    got = lax.all_to_all(blocks.astype(jnp.float16), axis, 0, 0, tiled=True)
+    return got.astype(F32)
+
+
+def adam_kernel(z_ref, corr_ref, own_ref, got_ref, master_ref, first_ref, second_ref, nf_ref, ns_ref, up_ref):
+    depth = own_ref.shape[-1]
+    total = add_received(own_ref[...], got_ref, z_ref[0], slice(0, depth), depth)
+    mean_all = total * (1.0 / 32)
     for layer in range(2):
         mean = mean_all[4 * layer : 4 * layer + 4]
         master = master_ref[layer]
@@ -116,16 +164,16 @@
         )
 
 
-def adam(corr, parts, master, first, second):
+def adam(z, corr, own, got, master, first, second):
     out = jax.ShapeDtypeStruct(master.shape, F32)
     return pl.pallas_call(
         adam_kernel,
-        in_specs=[SMEM] + [VMEM] * 7,
+        in_specs=[SMEM] * 2 + [VMEM] * 5,
         out_specs=[VMEM] * 3,
         out_shape=[out] * 3,
         compiler_params=PARAMS,
         name="adam",
-    )(corr, *parts, master, first, second)
+    )(z.astype(jnp.int32)[None], corr, own, got, master, first, second)
 
 
 def join_kernel(core_ref, mine_ref, theirs_ref, out_ref):
@@ -172,15 +220,11 @@
     depth = master.shape[-1]
     y, z, core = (lax.axis_index(a) for a in ZERO)
 
-    mine, theirs = split_cores(grads[0, 0, 0], y, core)
-    parts = add_pair(mine, shifted(theirs, "core", 1))
-    two = shifted(parts[2], "y", 2)
-    parts = [parts[0], shifted(parts[1], "y", 1), two, shifted(parts[3], "y", 3)]
-    parts = add_four(z, parts)
-    two = shifted(parts[2], "zhi", 2)
-    parts = [parts[0], shifted(parts[1], "zhi", 1), two, shifted(parts[3], "zhi", 3)]
+    mine, theirs = split_cores(grads[0, 0, 0], core)
+    own, out = add_pair(y, mine, shifted(theirs, "core", 1))
+    own, out = add_y(y, z, own, exchanged(out, "y"))
     new_first, new_second, updated = adam(
-        corr, parts, master[0], first_moment[0], second_moment[0]
+        z, corr, own, exchanged(out, "zhi"), master[0], first_moment[0], second_moment[0]
     )
     partner = lax.switch(
         t % 3, [lambda u, d=d: shifted(u, PEER, d) for d in (1, 2, 4)], updated

time: 135 us -> 113 us (0.84)
  waiting for transfers between devices: 43.1 us -> 31.8 us
  starting transfers between devices: 50.3 us -> 41.7 us
  blocking collectives: 31.8 us -> 26 us
  other arithmetic: 1.74 us -> 3.64 us
    ppermute x9 -> x3, waiting for transfers between devices: 43.1 us -> 5.92 us  [shifted(): lax.ppermute(block, axis, [(i, (i + distance) % n) for i in range(n)])]
    all_to_all x0 -> x2, waiting for transfers between devices: none -> 25.9 us  [exchanged(): got = lax.all_to_all(blocks.astype(jnp.float16), axis, 0, 0, tiled=True)]
    ppermute x9 -> x3, starting transfers between devices: 50.3 us -> 28.4 us  [shifted(): lax.ppermute(block, axis, [(i, (i + distance) % n) for i in range(n)])]
    all_to_all x0 -> x2, starting transfers between devices: none -> 13.3 us  [exchanged(): got = lax.all_to_all(blocks.astype(jnp.float16), axis, 0, 0, tiled=True)]
    all_gather x1, blocking collectives: 18.2 us -> 15 us  [body(): whole = lax.all_gather(whole, 'zhi', axis=0, tiled=True)]
    all_gather x1, blocking collectives: 13.6 us -> 11 us  [body(): whole = lax.all_gather(whole, 'y', axis=0, tiled=True)]
    convert_element_type x0 -> x4, other arithmetic: none -> 1.9 us  [the longest x2 1.75 us: exchanged(): got = lax.all_to_all(blocks.astype(jnp.float16), axis, 0, 0, tiled=True)]
    pallas_call x3, Pallas kernels: 1.56 us -> 3 us  [the longest x1 1.43 us: adam(): pl.pallas_call(adam_kernel, in_specs=[SMEM] * 2 + [VMEM] * 5, out_specs=[...]
  transfers between devices with their start and end apart: 9 -> 5, of which waited for: 7 -> 5; matrix products, arithmetic and copies ran while one was open for 0% -> 0% of each run, Pallas kernels for 0% -> 0%
where the time goes in v3:
time: 113 us; the launch traced here: 112 us
  starting transfers between devices  41.7 us (37%)
  waiting for transfers between devices  31.8 us (28%)
  blocking collectives  26 us (23%)
  Pallas kernels  5.71 us (5%)
  other arithmetic  3.64 us (3%)
  local copies, waits for them, and re-layouts  1.53 us (1%)
  between operations  1.51 us (1%)
    ppermute x3, starting transfers between devices, shifted(): lax.ppermute(block, axis, [(i, (i + distance) % n) for i in range(n)])  28.4 us
    all_to_all x2, waiting for transfers between devices, exchanged(): got = lax.all_to_all(blocks.astype(jnp.float16), axis, 0, 0, tiled=True)  25.9 us
    all_gather x1, blocking collectives, body(): whole = lax.all_gather(whole, 'zhi', axis=0, tiled=True)  15 us
    all_to_all x2, starting transfers between devices, exchanged(): got = lax.all_to_all(blocks.astype(jnp.float16), axis, 0, 0, tiled=True)  13.3 us
    all_gather x1, blocking collectives, body(): whole = lax.all_gather(whole, 'y', axis=0, tiled=True)  11 us
    ppermute x3, waiting for transfers between devices, shifted(): lax.ppermute(block, axis, [(i, (i + distance) % n) for i in range(n)])  5.92 us
  transfers between devices with their start and end apart: 5, of which 5 were waited for; matrix products, arithmetic and copies ran while one was open for 0% of the time, Pallas kernels for 0%

profile of v3, /device:TPU:1, one launch (start us, length us, event | category | flops | bytes accessed | tf_op | source)
XLA Modules:
  0.0 111.9 jit_solution(10168198719838364792)
XLA Ops:
  0.6 0.0 copy-start
  0.6 1.5 %copy-done = bf16[1,1,1,2,128,3584]{5,4,3,2,1,0:T(8,128)(2,1)S(1)} copy-done((bf16[1,1,1,2,128,3584]{5,4,3,2,1,0:T(8,128)(2,1)S(1)}, bf16[1,1,1,2,128,3584]{5,4,3,2,1,0:T(8,128)(2,1)}, u32[]{:S(2)}) %copy-start) | copy-done | bytes 1835032
  2.1 0.7 split_cores.1
  2.9 8.8 %collective-permute-start.3 = (bf16[4,32,3584]{2,1,0:T(8,128)(2,1)S(1)}, bf16[4,32,3584]{2,1,0:T(8,128)(2,1)S(1)}, u32[]{:S(2)}, u32[]{:S(2)}) collective-permute-start(bf16[4,32,3584]{2,1,0:T(8,128)(2,1)S(1)} %get-tuple-element.21), channel_id=1, source_target_pairs={{0,1},{1,0},{2,3},{3,2},{4,5},{5,4},{6,7},{7,6},{8,9},{9,8},{10,11... | collective-permute-start | bytes 2752520 | tf_op jit(solution)/shard_map/ppermute | solution.py:20
  11.7 2.1 %collective-permute-done.3.theirs_ref = bf16[4,32,3584]{2,1,0:T(8,128)(2,1)S(1)} collective-permute-done((bf16[4,32,3584]{2,1,0:T(8,128)(2,1)S(1)}, bf16[4,32,3584]{2,1,0:T(8,128)(2,1)S(1)}, u32[]{:S(2)}, u32[]{:S(2)}) %collective-permute-start.3) | collective-permute-done | bytes 917536 | tf_op jit(solution)/shard_map/ppermute | solution.py:20
  13.8 0.6 add_pair.1
  14.3 1.0 convert_element_type.20
  15.4 3.5 %all-to-all-start = ((f16[4,32,3712]{2,1,0:T(8,128)(2,1)}), f16[4,32,3712]{2,1,0:T(8,128)(2,1)S(1)}, u32[]{:S(2)}, u32[]{:S(2)}) async-start(f16[4,32,3712]{2,1,0:T(8,128)(2,1)} %convert_element_type.20), calls=%async_computation | async-start | bytes 1900544 | tf_op jit(solution)/shard_map/all_to_all | solution.py:147
  18.9 0.1 pad_add_fusion.at_ref
  19.0 13.7 %all-to-all-done = f16[4,32,3712]{2,1,0:T(8,128)(2,1)S(1)} async-done(((f16[4,32,3712]{2,1,0:T(8,128)(2,1)}), f16[4,32,3712]{2,1,0:T(8,128)(2,1)S(1)}, u32[]{:S(2)}, u32[]{:S(2)}) %all-to-all-start) | async-done | bytes 950304 | tf_op jit(solution)/shard_map/all_to_all | solution.py:147
  32.6 0.1 convert_element_type.21.got_ref
  32.8 0.0 copy-start.1
  32.8 0.0 copy-start.2
  32.8 0.0 copy-start.3
  32.8 1.0 add_y.1
  33.8 0.7 convert_element_type.22
  34.5 9.8 %all-to-all-start.1 = ((f16[4,8,3712]{2,1,0:T(8,128)(2,1)}), f16[4,8,3712]{2,1,0:T(8,128)(2,1)S(1)}, u32[]{:S(2)}, u32[]{:S(2)}) async-start(f16[4,8,3712]{2,1,0:T(8,128)(2,1)} %convert_element_type.22), calls=%async_computation.1 | async-start | bytes 475136 | tf_op jit(solution)/shard_map/all_to_all | solution.py:147
  45.1 0.1 pad_maximum_fusion.corr_ref
  45.2 12.2 %all-to-all-done.1 = f16[4,8,3712]{2,1,0:T(8,128)(2,1)S(1)} async-done(((f16[4,8,3712]{2,1,0:T(8,128)(2,1)}), f16[4,8,3712]{2,1,0:T(8,128)(2,1)S(1)}, u32[]{:S(2)}, u32[]{:S(2)}) %all-to-all-start.1) | async-done | bytes 237600 | tf_op jit(solution)/shard_map/all_to_all | solution.py:147
  57.4 0.0 copy-done.1
  57.4 0.0 copy-done.2
  57.4 0.0 copy-done.3
  57.4 1.4 %adam.1 = (f32[2,4,3584]{2,1,0:T(4,128)}, f32[2,4,3584]{2,1,0:T(4,128)}, f32[2,4,3584]{2,1,0:T(4,128)S(1)}) custom-call(s32[1]{0:T(128)} %bitcast.z_ref, f32[2]{0:T(128)S(1)} %pad_maximum_fusion.corr_ref, f32[8,3584]{1,0:T(8,128)S(1)} %get-tuple-element.24.own_ref, f32[4,8,3712]{2,1,0:T(8,128)S(1)} %convert_element_type.23.got_ref, ...), custom_call_target="tpu_custom_call" | custom-call | tf_op jit(solution)/shard_map/adam/pallas_call | solution.py:169
  58.9 9.6 %conditional.1 = (f32[2,4,3584]{2,1,0:T(4,128)}) conditional(s32[]{:T(128)} %clamp.3, f32[2,4,3584]{2,1,0:T(4,128)S(1)} %get-tuple-element.26, f32[2,4,3584]{2,1,0:T(4,128)S(1)} %get-tuple-element.26, f32[2,4,3584]{2,1,0:T(4,128)S(1)} %get-tuple-element.26), branch_computations={%region_0.1_spmd, %region_1.2_spmd, %region_2.3_spmd} | conditional | bytes 458800 | solution.py:229
  58.9 7.8 %collective-permute-start.2 = (f32[2,4,3584]{2,1,0:T(4,128)S(1)}, f32[2,4,3584]{2,1,0:T(4,128)}, u32[]{:S(2)}, u32[]{:S(2)}) collective-permute-start(f32[2,4,3584]{2,1,0:T(4,128)S(1)} %param.2), channel_id=1, source_target_pairs={{0,128},{32,160},{64,192},{96,224},{128,256},{160,288},{192,320},{... | collective-permute-start | bytes 344072 | tf_op jit(solution)/shard_map/cond/branch_2_fun/ppermute | solution.py:20
  66.7 1.8 %collective-permute-done.2 = f32[2,4,3584]{2,1,0:T(4,128)} collective-permute-done((f32[2,4,3584]{2,1,0:T(4,128)S(1)}, f32[2,4,3584]{2,1,0:T(4,128)}, u32[]{:S(2)}, u32[]{:S(2)}) %collective-permute-start.2) | collective-permute-done | bytes 114720 | tf_op jit(solution)/shard_map/cond/branch_2_fun/ppermute | solution.py:20
  68.4 1.6 %fusion = (bf16[2,4,3584]{2,1,0:T(4,128)(2,1)S(1)}, f32[1,2,4,3584]{3,2,1,0:T(4,128)}) fusion(f32[2,4,3584]{2,1,0:T(4,128)S(1)} %get-tuple-element.26, f32[2,4,3584]{2,1,0:T(4,128)} %get-tuple-element.31), kind=kLoop, calls=%fused_computation.1 | loop fusion | flops 86016 | bytes 401408 | tf_op jit(solution)/shard_map/convert_element_type | solution.py:234
  70.1 15.0 %all_gather.6 = bf16[32,3584]{1,0:T(8,128)(2,1)S(1)} all-gather(bf16[8,3584]{1,0:T(8,128)(2,1)S(1)} %reshape.26), channel_id=1, replica_groups=mesh['zlo'=4,'x'=4,'y'=4,'zhi'=4,'core'=2] {'zhi'}, dimensions={0}, use_global_device_ids=true | all-gather | bytes 286720 | tf_op jit(solution)/shard_map/all_gather | solution.py:235
  85.1 11.0 %all_gather.7.mine_ref = bf16[128,3584]{1,0:T(8,128)(2,1)S(1)} all-gather(bf16[32,3584]{1,0:T(8,128)(2,1)S(1)} %all_gather.6), channel_id=1, replica_groups=mesh['zlo'=4,'x'=4,'y'=4,'zhi'=4,'core'=2] {'y'}, dimensions={0}, use_global_device_ids=true | all-gather | bytes 1146880 | tf_op jit(solution)/shard_map/all_gather | solution.py:236
  96.1 11.8 %collective-permute-start.4 = (bf16[128,3584]{1,0:T(8,128)(2,1)S(1)}, bf16[128,3584]{1,0:T(8,128)(2,1)S(1)}, u32[]{:S(2)}, u32[]{:S(2)}) collective-permute-start(bf16[128,3584]{1,0:T(8,128)(2,1)S(1)} %all_gather.7.mine_ref), channel_id=1, source_target_pairs={{0,1},{1,0},{2,3},{3,2},{4,5},{5,4},{6,7},{7,6},{8,9},{9,8},{10,11... | collective-permute-start | bytes 2752520 | tf_op jit(solution)/shard_map/ppermute | solution.py:20
  107.9 2.1 %collective-permute-done.4.theirs_ref = bf16[128,3584]{1,0:T(8,128)(2,1)S(1)} collective-permute-done((bf16[128,3584]{1,0:T(8,128)(2,1)S(1)}, bf16[128,3584]{1,0:T(8,128)(2,1)S(1)}, u32[]{:S(2)}, u32[]{:S(2)}) %collective-permute-start.4) | collective-permute-done | bytes 917536 | tf_op jit(solution)/shard_map/ppermute | solution.py:20
  110.0 2.0 %join_cores.1 = bf16[2,128,3584]{2,1,0:T(8,128)(2,1)} custom-call(s32[1]{0:T(128)} %bitcast.2.core_ref, bf16[128,3584]{1,0:T(8,128)(2,1)S(1)} %all_gather.7.mine_ref, bf16[128,3584]{1,0:T(8,128)(2,1)S(1)} %collective-permute-done.4.theirs_ref), custom_call_target="tpu_custom_call" | custom-call | tf_op jit(solution)/shard_map/join_cores/pallas_call | solution.py:202
  (2 shorter events, 0.1 us)
Async XLA Ops:
  0.6 1.5 %copy-start = (bf16[1,1,1,2,128,3584]{5,4,3,2,1,0:T(8,128)(2,1)S(1)}, bf16[1,1,1,2,128,3584]{5,4,3,2,1,0:T(8,128)(2,1)}, u32[]{:S(2)}) copy-start(bf16[1,1,1,2,128,3584]{5,4,3,2,1,0:T(8,128)(2,1)} %param.9) | copy-start | bytes 5505028
  2.9 10.9 %collective-permute-start.3 = (bf16[4,32,3584]{2,1,0:T(8,128)(2,1)S(1)}, bf16[4,32,3584]{2,1,0:T(8,128)(2,1)S(1)}, u32[]{:S(2)}, u32[]{:S(2)}) collective-permute-start(bf16[4,32,3584]{2,1,0:T(8,128)(2,1)S(1)} %get-tuple-element.21), channel_id=1, source_target_pairs={{0,1},{1,0},{2,3},{3,2},{4,5},{5,4},{6,7},{7,6},{8,9},{9,8},{10,11... | collective-permute-start | bytes 2752520 | tf_op jit(solution)/shard_map/ppermute | solution.py:20
  15.4 17.3 %all-to-all-start = ((f16[4,32,3712]{2,1,0:T(8,128)(2,1)}), f16[4,32,3712]{2,1,0:T(8,128)(2,1)S(1)}, u32[]{:S(2)}, u32[]{:S(2)}) async-start(f16[4,32,3712]{2,1,0:T(8,128)(2,1)} %convert_element_type.20), calls=%async_computation | async-start | bytes 1900544 | tf_op jit(solution)/shard_map/all_to_all | solution.py:147
  32.8 24.6 %copy-start.1 = (f32[1,2,4,3584]{3,2,1,0:T(4,128)S(1)}, f32[1,2,4,3584]{3,2,1,0:T(4,128)}, u32[]{:S(2)}) copy-start(f32[1,2,4,3584]{3,2,1,0:T(4,128)} %param.10) | copy-start | bytes 344068
  32.8 24.6 %copy-start.2 = (f32[1,2,4,3584]{3,2,1,0:T(4,128)S(1)}, f32[1,2,4,3584]{3,2,1,0:T(4,128)}, u32[]{:S(2)}) copy-start(f32[1,2,4,3584]{3,2,1,0:T(4,128)} %param.11) | copy-start | bytes 344068
  32.8 24.6 %copy-start.3 = (f32[1,2,4,3584]{3,2,1,0:T(4,128)S(1)}, f32[1,2,4,3584]{3,2,1,0:T(4,128)}, u32[]{:S(2)}) copy-start(f32[1,2,4,3584]{3,2,1,0:T(4,128)} %param.12) | copy-start | bytes 344068
  34.5 22.8 %all-to-all-start.1 = ((f16[4,8,3712]{2,1,0:T(8,128)(2,1)}), f16[4,8,3712]{2,1,0:T(8,128)(2,1)S(1)}, u32[]{:S(2)}, u32[]{:S(2)}) async-start(f16[4,8,3712]{2,1,0:T(8,128)(2,1)} %convert_element_type.22), calls=%async_computation.1 | async-start | bytes 475136 | tf_op jit(solution)/shard_map/all_to_all | solution.py:147
  58.9 9.6 %collective-permute-start.2 = (f32[2,4,3584]{2,1,0:T(4,128)S(1)}, f32[2,4,3584]{2,1,0:T(4,128)}, u32[]{:S(2)}, u32[]{:S(2)}) collective-permute-start(f32[2,4,3584]{2,1,0:T(4,128)S(1)} %param.2), channel_id=1, source_target_pairs={{0,128},{32,160},{64,192},{96,224},{128,256},{160,288},{192,320},{... | collective-permute-start | bytes 344072 | tf_op jit(solution)/shard_map/cond/branch_2_fun/ppermute | solution.py:20
  96.1 13.9 %collective-permute-start.4 = (bf16[128,3584]{1,0:T(8,128)(2,1)S(1)}, bf16[128,3584]{1,0:T(8,128)(2,1)S(1)}, u32[]{:S(2)}, u32[]{:S(2)}) collective-permute-start(bf16[128,3584]{1,0:T(8,128)(2,1)S(1)} %all_gather.7.mine_ref), channel_id=1, source_target_pairs={{0,1},{1,0},{2,3},{3,2},{4,5},{5,4},{6,7},{7,6},{8,9},{9,8},{10,11... | collective-permute-start | bytes 2752520 | tf_op jit(solution)/shard_map/ppermute | solution.py:20

commit v4 on v3

--- a/solution.py
+++ b/solution.py
@@ -60,7 +60,7 @@
         out_shape=(out, out),
         compiler_params=PARAMS,
         name="split_cores",
-    )(core.astype(jnp.int32)[None], grads)
+    )(core, grads)
 
 
 def scale_of(largest):
@@ -115,7 +115,7 @@
         scratch_shapes=[pltpu.VMEM((n * rows, depth), F32)],
         compiler_params=PARAMS,
         name="add_pair",
-    )(y.astype(jnp.int32)[None], mine, theirs)
+    )(y, mine, theirs)
 
 
 def add_y_kernel(at_ref, own_ref, got_ref, keep_ref, out_ref, sums):
@@ -127,7 +127,7 @@
     send_scaled(out_ref, sums)
 
 
-def add_y(y, z, own, got):
+def add_y(at, own, got):
     rows, depth = own.shape
     return pl.pallas_call(
         add_y_kernel,
@@ -140,7 +140,7 @@
         scratch_shapes=[pltpu.VMEM((rows, depth), F32)],
         compiler_params=PARAMS,
         name="add_y",
-    )(jnp.stack([y, z]).astype(jnp.int32), own, got)
+    )(at, own, got)
 
 
 def exchanged(blocks, axis):
@@ -173,7 +173,7 @@
         out_shape=[out] * 3,
         compiler_params=PARAMS,
         name="adam",
-    )(z.astype(jnp.int32)[None], corr, own, got, master, first, second)
+    )(z, corr, own, got, master, first, second)
 
 
 def join_kernel(core_ref, mine_ref, theirs_ref, out_ref):
@@ -210,7 +210,7 @@
         out_shape=jax.ShapeDtypeStruct((2, rows, depth), BF16),
         compiler_params=PARAMS,
         name="join_cores",
-    )(core.astype(jnp.int32)[None], mine, theirs)
+    )(core, mine, theirs)
 
 
 def body(step, grads, master, first_moment, second_moment):
@@ -218,16 +218,19 @@
     power = (t + 1).astype(F32)
     corr = jnp.stack([1.0 - jnp.power(F32(0.9), power), 1.0 - jnp.power(F32(0.95), power)])
     depth = master.shape[-1]
-    y, z, core = (lax.axis_index(a) for a in ZERO)
+    y, z, core = (lax.axis_index(a).astype(jnp.int32)[None] for a in ZERO)
+    at = jnp.concatenate([y, z])
+    which = t % 3
 
     mine, theirs = split_cores(grads[0, 0, 0], core)
+    theirs, y, z, at, corr, which = lax.optimization_barrier((theirs, y, z, at, corr, which))
     own, out = add_pair(y, mine, shifted(theirs, "core", 1))
-    own, out = add_y(y, z, own, exchanged(out, "y"))
+    own, out = add_y(at, own, exchanged(out, "y"))
     new_first, new_second, updated = adam(
         z, corr, own, exchanged(out, "zhi"), master[0], first_moment[0], second_moment[0]
     )
     partner = lax.switch(
-        t % 3, [lambda u, d=d: shifted(u, PEER, d) for d in (1, 2, 4)], updated
+        which, [lambda u, d=d: shifted(u, PEER, d) for d in (1, 2, 4)], updated
     )
     averaged = (updated + partner) * 0.5
 

time: 113 us -> 113 us (level)
  blocking collectives: 26 us -> 42 us
  waiting for transfers between devices: 31.8 us -> 19 us
  starting transfers between devices: 41.7 us -> 39.2 us
    all_to_all x0 -> x1, blocking collectives: none -> 16 us  [exchanged(): got = lax.all_to_all(blocks.astype(jnp.float16), axis, 0, 0, tiled=True)]
    all_to_all x2 -> x1, waiting for transfers between devices: 25.9 us -> 13 us  [exchanged(): got = lax.all_to_all(blocks.astype(jnp.float16), axis, 0, 0, tiled=True)]
    all_to_all x2 -> x1, starting transfers between devices: 13.3 us -> 10.8 us  [exchanged(): got = lax.all_to_all(blocks.astype(jnp.float16), axis, 0, 0, tiled=True)]
  transfers between devices with their start and end apart: 5 -> 4, of which waited for: 5 -> 4; matrix products, arithmetic and copies ran while one was open for 0% -> 0% of each run, Pallas kernels for 0% -> 0%
where the time goes in v4:
time: 113 us; the launch traced here: 112 us
  blocking collectives  42 us (37%)
  starting transfers between devices  39.2 us (35%)
  waiting for transfers between devices  19 us (17%)
  Pallas kernels  5.71 us (5%)
  other arithmetic  2.71 us (2%)
  local copies, waits for them, and re-layouts  1.54 us (1%)
  between operations  1.49 us (1%)
    ppermute x3, starting transfers between devices, shifted(): lax.ppermute(block, axis, [(i, (i + distance) % n) for i in range(n)])  28.4 us
    all_to_all x1, blocking collectives, exchanged(): got = lax.all_to_all(blocks.astype(jnp.float16), axis, 0, 0, tiled=True)  16 us
    all_gather x1, blocking collectives, body(): whole = lax.all_gather(whole, 'zhi', axis=0, tiled=True)  15 us
    all_to_all x1, waiting for transfers between devices, exchanged(): got = lax.all_to_all(blocks.astype(jnp.float16), axis, 0, 0, tiled=True)  13 us
    all_gather x1, blocking collectives, body(): whole = lax.all_gather(whole, 'y', axis=0, tiled=True)  11 us
    all_to_all x1, starting transfers between devices, exchanged(): got = lax.all_to_all(blocks.astype(jnp.float16), axis, 0, 0, tiled=True)  10.8 us
    ppermute x3, waiting for transfers between devices, shifted(): lax.ppermute(block, axis, [(i, (i + distance) % n) for i in range(n)])  5.93 us
  transfers between devices with their start and end apart: 4, of which 4 were waited for; matrix products, arithmetic and copies ran while one was open for 0% of the time, Pallas kernels for 0%

profile of v4, /device:TPU:1, one launch (start us, length us, event | category | flops | bytes accessed | tf_op | source)
XLA Modules:
  0.0 111.7 jit_solution(2409530709678388898)
XLA Ops:
  1.4 0.1 pad_maximum_fusion.corr_ref
  1.5 0.1 pad_add_fusion.at_ref
  1.5 0.0 copy-start
  1.5 1.5 %copy-done = bf16[1,1,1,2,128,3584]{5,4,3,2,1,0:T(8,128)(2,1)S(1)} copy-done((bf16[1,1,1,2,128,3584]{5,4,3,2,1,0:T(8,128)(2,1)S(1)}, bf16[1,1,1,2,128,3584]{5,4,3,2,1,0:T(8,128)(2,1)}, u32[]{:S(2)}) %copy-start) | copy-done | bytes 1835032
  3.0 0.7 split_cores.1
  3.8 8.8 %collective-permute-start.3 = (bf16[4,32,3584]{2,1,0:T(8,128)(2,1)S(1)}, bf16[4,32,3584]{2,1,0:T(8,128)(2,1)S(1)}, u32[]{:S(2)}, u32[]{:S(2)}) collective-permute-start(bf16[4,32,3584]{2,1,0:T(8,128)(2,1)S(1)} %get-tuple-element.32), channel_id=1, source_target_pairs={{0,1},{1,0},{2,3},{3,2},{4,5},{5,4},{6,7},{7,6},{8,9},{9,8},{10,11... | collective-permute-start | bytes 2752520 | tf_op jit(solution)/shard_map/ppermute | solution.py:20
  12.6 2.1 %collective-permute-done.3.theirs_ref = bf16[4,32,3584]{2,1,0:T(8,128)(2,1)S(1)} collective-permute-done((bf16[4,32,3584]{2,1,0:T(8,128)(2,1)S(1)}, bf16[4,32,3584]{2,1,0:T(8,128)(2,1)S(1)}, u32[]{:S(2)}, u32[]{:S(2)}) %collective-permute-start.3) | collective-permute-done | bytes 917536 | tf_op jit(solution)/shard_map/ppermute | solution.py:20
  14.7 0.6 add_pair.1
  15.2 0.1 convert_element_type.20
  15.3 16.0 %all_to_all.10 = f16[4,32,3712]{2,1,0:T(8,128)(2,1)S(1)} all-to-all(f16[4,32,3712]{2,1,0:T(8,128)(2,1)S(1)} %convert_element_type.20), channel_id=1, replica_groups=mesh['zlo'=4,'x'=4,'y'=4,'zhi'=4,'core'=2] {'y'}, dimensions={0} | all-to-all | bytes 1900544 | tf_op jit(solution)/shard_map/all_to_all | solution.py:147
  31.4 0.1 convert_element_type.21.got_ref
  31.5 0.0 copy-start.1
  31.5 0.0 copy-start.2
  31.5 0.0 copy-start.3
  31.5 1.0 add_y.1
  32.6 0.7 convert_element_type.22
  33.3 10.8 %all-to-all-start.1 = ((f16[4,8,3712]{2,1,0:T(8,128)(2,1)}), f16[4,8,3712]{2,1,0:T(8,128)(2,1)S(1)}, u32[]{:S(2)}, u32[]{:S(2)}) async-start(f16[4,8,3712]{2,1,0:T(8,128)(2,1)} %convert_element_type.22), calls=%async_computation.1 | async-start | bytes 475136 | tf_op jit(solution)/shard_map/all_to_all | solution.py:147
  44.1 13.0 %all-to-all-done.1 = f16[4,8,3712]{2,1,0:T(8,128)(2,1)S(1)} async-done(((f16[4,8,3712]{2,1,0:T(8,128)(2,1)}), f16[4,8,3712]{2,1,0:T(8,128)(2,1)S(1)}, u32[]{:S(2)}, u32[]{:S(2)}) %all-to-all-start.1) | async-done | bytes 237600 | tf_op jit(solution)/shard_map/all_to_all | solution.py:147
  57.2 0.0 copy-done.1
  57.2 0.0 copy-done.2
  57.2 0.0 copy-done.3
  57.2 1.4 %adam.1 = (f32[2,4,3584]{2,1,0:T(4,128)}, f32[2,4,3584]{2,1,0:T(4,128)}, f32[2,4,3584]{2,1,0:T(4,128)S(1)}) custom-call(s32[1]{0:T(128)} %bitcast.3.z_ref, f32[2]{0:T(128)S(1)} %pad_maximum_fusion.corr_ref, f32[8,3584]{1,0:T(8,128)S(1)} %get-tuple-element.35.own_ref, f32[4,8,3712]{2,1,0:T(8,128)S(1)} %convert_element_type.23.got_ref, ...), custom_call_target="tpu_custom_call" | custom-call | tf_op jit(solution)/shard_map/adam/pallas_call | solution.py:169
  58.7 9.6 %conditional.1 = (f32[2,4,3584]{2,1,0:T(4,128)}) conditional(s32[]{:T(128)} %clamp.3, f32[2,4,3584]{2,1,0:T(4,128)S(1)} %get-tuple-element.37, f32[2,4,3584]{2,1,0:T(4,128)S(1)} %get-tuple-element.37, f32[2,4,3584]{2,1,0:T(4,128)S(1)} %get-tuple-element.37), branch_computations={%region_0.1_spmd, %region_1.2_spmd, %region_2.3_spmd} | conditional | bytes 458800 | solution.py:232
  58.7 7.8 %collective-permute-start.2 = (f32[2,4,3584]{2,1,0:T(4,128)S(1)}, f32[2,4,3584]{2,1,0:T(4,128)}, u32[]{:S(2)}, u32[]{:S(2)}) collective-permute-start(f32[2,4,3584]{2,1,0:T(4,128)S(1)} %param.2), channel_id=1, source_target_pairs={{0,128},{32,160},{64,192},{96,224},{128,256},{160,288},{192,320},{... | collective-permute-start | bytes 344072 | tf_op jit(solution)/shard_map/cond/branch_2_fun/ppermute | solution.py:20
  66.5 1.8 %collective-permute-done.2 = f32[2,4,3584]{2,1,0:T(4,128)} collective-permute-done((f32[2,4,3584]{2,1,0:T(4,128)S(1)}, f32[2,4,3584]{2,1,0:T(4,128)}, u32[]{:S(2)}, u32[]{:S(2)}) %collective-permute-start.2) | collective-permute-done | bytes 114720 | tf_op jit(solution)/shard_map/cond/branch_2_fun/ppermute | solution.py:20
  68.2 1.6 %fusion = (bf16[2,4,3584]{2,1,0:T(4,128)(2,1)S(1)}, f32[1,2,4,3584]{3,2,1,0:T(4,128)}) fusion(f32[2,4,3584]{2,1,0:T(4,128)S(1)} %get-tuple-element.37, f32[2,4,3584]{2,1,0:T(4,128)} %get-tuple-element.43), kind=kLoop, calls=%fused_computation.1 | loop fusion | flops 86016 | bytes 401408 | tf_op jit(solution)/shard_map/convert_element_type | solution.py:237
  69.8 15.0 %all_gather.6 = bf16[32,3584]{1,0:T(8,128)(2,1)S(1)} all-gather(bf16[8,3584]{1,0:T(8,128)(2,1)S(1)} %reshape.26), channel_id=1, replica_groups=mesh['zlo'=4,'x'=4,'y'=4,'zhi'=4,'core'=2] {'zhi'}, dimensions={0}, use_global_device_ids=true | all-gather | bytes 286720 | tf_op jit(solution)/shard_map/all_gather | solution.py:238
  84.9 11.0 %all_gather.7.mine_ref = bf16[128,3584]{1,0:T(8,128)(2,1)S(1)} all-gather(bf16[32,3584]{1,0:T(8,128)(2,1)S(1)} %all_gather.6), channel_id=1, replica_groups=mesh['zlo'=4,'x'=4,'y'=4,'zhi'=4,'core'=2] {'y'}, dimensions={0}, use_global_device_ids=true | all-gather | bytes 1146880 | tf_op jit(solution)/shard_map/all_gather | solution.py:239
  95.8 11.8 %collective-permute-start.4 = (bf16[128,3584]{1,0:T(8,128)(2,1)S(1)}, bf16[128,3584]{1,0:T(8,128)(2,1)S(1)}, u32[]{:S(2)}, u32[]{:S(2)}) collective-permute-start(bf16[128,3584]{1,0:T(8,128)(2,1)S(1)} %all_gather.7.mine_ref), channel_id=1, source_target_pairs={{0,1},{1,0},{2,3},{3,2},{4,5},{5,4},{6,7},{7,6},{8,9},{9,8},{10,11... | collective-permute-start | bytes 2752520 | tf_op jit(solution)/shard_map/ppermute | solution.py:20
  107.7 2.1 %collective-permute-done.4.theirs_ref = bf16[128,3584]{1,0:T(8,128)(2,1)S(1)} collective-permute-done((bf16[128,3584]{1,0:T(8,128)(2,1)S(1)}, bf16[128,3584]{1,0:T(8,128)(2,1)S(1)}, u32[]{:S(2)}, u32[]{:S(2)}) %collective-permute-start.4) | collective-permute-done | bytes 917536 | tf_op jit(solution)/shard_map/ppermute | solution.py:20
  109.7 2.0 %join_cores.1 = bf16[2,128,3584]{2,1,0:T(8,128)(2,1)} custom-call(s32[1]{0:T(128)} %bitcast.core_ref, bf16[128,3584]{1,0:T(8,128)(2,1)S(1)} %all_gather.7.mine_ref, bf16[128,3584]{1,0:T(8,128)(2,1)S(1)} %collective-permute-done.4.theirs_ref), custom_call_target="tpu_custom_call" | custom-call | tf_op jit(solution)/shard_map/join_cores/pallas_call | solution.py:202
  (2 shorter events, 0.1 us)
Async XLA Ops:
  1.5 1.5 %copy-start = (bf16[1,1,1,2,128,3584]{5,4,3,2,1,0:T(8,128)(2,1)S(1)}, bf16[1,1,1,2,128,3584]{5,4,3,2,1,0:T(8,128)(2,1)}, u32[]{:S(2)}) copy-start(bf16[1,1,1,2,128,3584]{5,4,3,2,1,0:T(8,128)(2,1)} %param.9) | copy-start | bytes 5505028
  3.8 10.9 %collective-permute-start.3 = (bf16[4,32,3584]{2,1,0:T(8,128)(2,1)S(1)}, bf16[4,32,3584]{2,1,0:T(8,128)(2,1)S(1)}, u32[]{:S(2)}, u32[]{:S(2)}) collective-permute-start(bf16[4,32,3584]{2,1,0:T(8,128)(2,1)S(1)} %get-tuple-element.32), channel_id=1, source_target_pairs={{0,1},{1,0},{2,3},{3,2},{4,5},{5,4},{6,7},{7,6},{8,9},{9,8},{10,11... | collective-permute-start | bytes 2752520 | tf_op jit(solution)/shard_map/ppermute | solution.py:20
  31.5 25.7 %copy-start.1 = (f32[1,2,4,3584]{3,2,1,0:T(4,128)S(1)}, f32[1,2,4,3584]{3,2,1,0:T(4,128)}, u32[]{:S(2)}) copy-start(f32[1,2,4,3584]{3,2,1,0:T(4,128)} %param.10) | copy-start | bytes 344068
  31.5 25.7 %copy-start.2 = (f32[1,2,4,3584]{3,2,1,0:T(4,128)S(1)}, f32[1,2,4,3584]{3,2,1,0:T(4,128)}, u32[]{:S(2)}) copy-start(f32[1,2,4,3584]{3,2,1,0:T(4,128)} %param.11) | copy-start | bytes 344068
  31.5 25.7 %copy-start.3 = (f32[1,2,4,3584]{3,2,1,0:T(4,128)S(1)}, f32[1,2,4,3584]{3,2,1,0:T(4,128)}, u32[]{:S(2)}) copy-start(f32[1,2,4,3584]{3,2,1,0:T(4,128)} %param.12) | copy-start | bytes 344068
  33.3 23.9 %all-to-all-start.1 = ((f16[4,8,3712]{2,1,0:T(8,128)(2,1)}), f16[4,8,3712]{2,1,0:T(8,128)(2,1)S(1)}, u32[]{:S(2)}, u32[]{:S(2)}) async-start(f16[4,8,3712]{2,1,0:T(8,128)(2,1)} %convert_element_type.22), calls=%async_computation.1 | async-start | bytes 475136 | tf_op jit(solution)/shard_map/all_to_all | solution.py:147
  58.7 9.6 %collective-permute-start.2 = (f32[2,4,3584]{2,1,0:T(4,128)S(1)}, f32[2,4,3584]{2,1,0:T(4,128)}, u32[]{:S(2)}, u32[]{:S(2)}) collective-permute-start(f32[2,4,3584]{2,1,0:T(4,128)S(1)} %param.2), channel_id=1, source_target_pairs={{0,128},{32,160},{64,192},{96,224},{128,256},{160,288},{192,320},{... | collective-permute-start | bytes 344072 | tf_op jit(solution)/shard_map/cond/branch_2_fun/ppermute | solution.py:20
  95.8 13.9 %collective-permute-start.4 = (bf16[128,3584]{1,0:T(8,128)(2,1)S(1)}, bf16[128,3584]{1,0:T(8,128)(2,1)S(1)}, u32[]{:S(2)}, u32[]{:S(2)}) collective-permute-start(bf16[128,3584]{1,0:T(8,128)(2,1)S(1)} %all_gather.7.mine_ref), channel_id=1, source_target_pairs={{0,1},{1,0},{2,3},{3,2},{4,5},{5,4},{6,7},{7,6},{8,9},{9,8},{10,11... | collective-permute-start | bytes 2752520 | tf_op jit(solution)/shard_map/ppermute | solution.py:20

commit v5 on v4

--- a/solution.py
+++ b/solution.py
@@ -118,29 +118,76 @@
     )(y, mine, theirs)
 
 
-def add_y_kernel(at_ref, own_ref, got_ref, keep_ref, out_ref, sums):
+def scaled(block_ref, out_ref):
+    depth = block_ref.shape[-1]
+    largest = jnp.zeros((8, LANES), F32)
+    for at in range(0, depth, LANES):
+        largest = jnp.maximum(largest, jnp.abs(block_ref[:, at : at + LANES]))
+    scale, back = scale_of(jnp.max(largest, axis=(0, 1), keepdims=True))
+    out_ref[:, :depth] = block_ref[...] * scale
+    out_ref[:, depth:] = jnp.broadcast_to(back, (8, out_ref.shape[-1] - depth))
+
+
+def restored(got_ref, depth):
+    return got_ref[:, :depth] * jnp.exp2(got_ref[0:1, depth : depth + 1])
+
+
+def add_y_kernel(at_ref, own_ref, got_ref, keep_ref, near_ref, far_ref, back_ref, sums):
     depth = own_ref.shape[-1]
+    n = sums.shape[0] // 8
     for at in range(0, depth, LANES):
         cols = slice(at, at + LANES)
         sums[:, cols] = add_received(own_ref[:, cols], got_ref, at_ref[0], cols, depth)
-    keep_ref[...] = sums[pl.ds(pl.multiple_of(at_ref[1] * 8, 8), 8), :]
-    send_scaled(out_ref, sums)
+
+    def piece(k):
+        step = jnp.where(at_ref[2] == 0, k, n - k)
+        return pl.ds(pl.multiple_of(((at_ref[1] + step) % n) * 8, 8), 8)
+
+    keep_ref[...] = sums[piece(0), :]
+    near_ref[...] = sums[piece(1), :]
+    scaled(sums.at[piece(2)], far_ref)
+    scaled(sums.at[piece(3)], back_ref)
 
 
 def add_y(at, own, got):
     rows, depth = own.shape
+    kept = jax.ShapeDtypeStruct((8, depth), F32)
+    sent = jax.ShapeDtypeStruct((8, depth + 128), F32)
     return pl.pallas_call(
         add_y_kernel,
         in_specs=[SMEM, VMEM, VMEM],
-        out_specs=[VMEM] * 2,
-        out_shape=[
-            jax.ShapeDtypeStruct((8, depth), F32),
-            jax.ShapeDtypeStruct((rows // 8, 8, depth + 128), F32),
-        ],
+        out_specs=[VMEM] * 4,
+        out_shape=[kept, kept, sent, sent],
         scratch_shapes=[pltpu.VMEM((rows, depth), F32)],
         compiler_params=PARAMS,
         name="add_y",
     )(at, own, got)
+
+
+def add_through_kernel(near_ref, got_ref, out_ref, total):
+    total[...] = near_ref[...] + restored(got_ref, near_ref.shape[-1])
+    scaled(total, out_ref)
+
+
+def add_through(near, got):
+    return pl.pallas_call(
+        add_through_kernel,
+        in_specs=[VMEM] * 2,
+        out_specs=VMEM,
+        out_shape=jax.ShapeDtypeStruct(got.shape, F32),
+        scratch_shapes=[pltpu.VMEM(near.shape, F32)],
+        compiler_params=PARAMS,
+        name="add_through",
+    )(near, got)
+
+
+def turned(block, distance):
+    n = lax.axis_size("zhi")
+    pairs = []
+    for z in range(n):
+        pairs.append((2 * z, 2 * ((z + distance) % n)))
+        pairs.append((2 * z + 1, 2 * ((z - distance) % n) + 1))
+    return lax.ppermute(block.astype(jnp.float16), ("zhi", "core"), pairs).astype(F32)
 
 
 def exchanged(blocks, axis):
@@ -148,9 +195,9 @@
     return got.astype(F32)
 
 
-def adam_kernel(z_ref, corr_ref, own_ref, got_ref, master_ref, first_ref, second_ref, nf_ref, ns_ref, up_ref):
+def adam_kernel(corr_ref, own_ref, far_ref, back_ref, master_ref, first_ref, second_ref, nf_ref, ns_ref, up_ref):
     depth = own_ref.shape[-1]
-    total = add_received(own_ref[...], got_ref, z_ref[0], slice(0, depth), depth)
+    total = own_ref[...] + (restored(far_ref, depth) + restored(back_ref, depth))
     mean_all = total * (1.0 / 32)
     for layer in range(2):
         mean = mean_all[4 * layer : 4 * layer + 4]
@@ -164,16 +211,38 @@
         )
 
 
-def adam(z, corr, own, got, master, first, second):
+def adam(corr, own, far, back, master, first, second):
     out = jax.ShapeDtypeStruct(master.shape, F32)
     return pl.pallas_call(
         adam_kernel,
-        in_specs=[SMEM] * 2 + [VMEM] * 5,
+        in_specs=[SMEM] + [VMEM] * 6,
         out_specs=[VMEM] * 3,
         out_shape=[out] * 3,
         compiler_params=PARAMS,
         name="adam",
-    )(z, corr, own, got, master, first, second)
+    )(corr, own, far, back, master, first, second)
+
+
+def average_kernel(up_ref, partner_ref, out_ref, rounded_ref):
+    mean = [(up_ref[i] + partner_ref[i]) * 0.5 for i in range(2)]
+    for i in range(2):
+        out_ref[i] = mean[i]
+    rounded_ref[...] = jnp.concatenate(mean, 0).astype(BF16)
+
+
+def average(updated, partner):
+    layers, rows, depth = updated.shape
+    return pl.pallas_call(
+        average_kernel,
+        in_specs=[VMEM] * 2,
+        out_specs=[VMEM] * 2,
+        out_shape=[
+            jax.ShapeDtypeStruct(updated.shape, F32),
+            jax.ShapeDtypeStruct((layers * rows, depth), BF16),
+        ],
+        compiler_params=PARAMS,
+        name="average",
+    )(updated, partner)
 
 
 def join_kernel(core_ref, mine_ref, theirs_ref, out_ref):
@@ -217,24 +286,24 @@
     t = step[0]
     power = (t + 1).astype(F32)
     corr = jnp.stack([1.0 - jnp.power(F32(0.9), power), 1.0 - jnp.power(F32(0.95), power)])
-    depth = master.shape[-1]
     y, z, core = (lax.axis_index(a).astype(jnp.int32)[None] for a in ZERO)
-    at = jnp.concatenate([y, z])
-    which = t % 3
+    at = jnp.concatenate([y, z, core])
 
     mine, theirs = split_cores(grads[0, 0, 0], core)
-    theirs, y, z, at, corr, which = lax.optimization_barrier((theirs, y, z, at, corr, which))
-    own, out = add_pair(y, mine, shifted(theirs, "core", 1))
-    own, out = add_y(at, own, exchanged(out, "y"))
+    theirs = shifted(theirs, "core", 1)
+    theirs, y, at, corr = lax.optimization_barrier((theirs, y, at, corr))
+    own, out = add_pair(y, mine, theirs)
+    own, near, far, back = add_y(at, own, exchanged(out, "y"))
+    far = turned(far, 1)
+    back = turned(back, -1)
+    far = turned(add_through(near, far), 1)
     new_first, new_second, updated = adam(
-        z, corr, own, exchanged(out, "zhi"), master[0], first_moment[0], second_moment[0]
+        corr, own, back, far, master[0], first_moment[0], second_moment[0]
     )
     partner = lax.switch(
-        which, [lambda u, d=d: shifted(u, PEER, d) for d in (1, 2, 4)], updated
+        t % 3, [lambda u, d=d: shifted(u, PEER, d) for d in (1, 2, 4)], updated
     )
-    averaged = (updated + partner) * 0.5
-
-    whole = averaged.astype(BF16).reshape(8, depth)
+    averaged, whole = average(updated, partner)
     whole = lax.all_gather(whole, "zhi", axis=0, tiled=True)
     whole = lax.all_gather(whole, "y", axis=0, tiled=True)
     whole = join_cores(whole, shifted(whole, "core", 1), core)

time: 113 us -> 114 us (level)
  waiting for transfers between devices: 19 us -> 11 us
  blocking collectives: 42 us -> 48 us
  starting transfers between devices: 39.2 us -> 43.2 us
  other arithmetic: 2.71 us -> 0.44 us
  Pallas kernels: 5.71 us -> 7.43 us
    ppermute x0 -> x3, starting transfers between devices: none -> 19.5 us  [turned(): lax.ppermute(block.astype(jnp.float16), ('zhi', 'core'), pairs).astype(F32)]
    all_to_all x1 -> x0, waiting for transfers between devices: 13 us -> none  [exchanged(): got = lax.all_to_all(blocks.astype(jnp.float16), axis, 0, 0, tiled=True)]
    all_to_all x1 -> x0, starting transfers between devices: 10.8 us -> none  [exchanged(): got = lax.all_to_all(blocks.astype(jnp.float16), axis, 0, 0, tiled=True)]
    all_gather x1, blocking collectives: 15 us -> 20.5 us  [body(): whole = lax.all_gather(whole, 'zhi', axis=0, tiled=True)]
    ppermute x3, starting transfers between devices: 28.4 us -> 23.7 us  [shifted(): lax.ppermute(block, axis, [(i, (i + distance) % n) for i in range(n)])]
    ppermute x0 -> x3, waiting for transfers between devices: none -> 2.55 us  [turned(): lax.ppermute(block.astype(jnp.float16), ('zhi', 'core'), pairs).astype(F32)]
    ppermute x3, waiting for transfers between devices: 5.93 us -> 8.45 us  [shifted(): lax.ppermute(block, axis, [(i, (i + distance) % n) for i in range(n)])]
    pallas_call x1 -> x3, Pallas kernels: 1.43 us -> 3.18 us  [the longest x1 1.56 us: average(): pl.pallas_call(average_kernel, in_specs=[VMEM] * 2, out_specs=[VMEM] * 2,...]
  transfers between devices with their start and end apart: 4 -> 6, of which waited for: 4 -> 4; matrix products, arithmetic and copies ran while one was open for 0% -> 0% of each run, Pallas kernels for 0% -> 0%
where the time goes in v5:
time: 114 us; the launch traced here: 113 us
  blocking collectives  48 us (42%)
  starting transfers between devices  43.2 us (38%)
  waiting for transfers between devices  11 us (10%)
  Pallas kernels  7.43 us (7%)
  between operations  1.6 us (1%)
  local copies, waits for them, and re-layouts  1.51 us (1%)
    ppermute x3, starting transfers between devices, shifted(): lax.ppermute(block, axis, [(i, (i + distance) % n) for i in range(n)])  23.7 us
    all_gather x1, blocking collectives, body(): whole = lax.all_gather(whole, 'zhi', axis=0, tiled=True)  20.5 us
    ppermute x3, starting transfers between devices, turned(): lax.ppermute(block.astype(jnp.float16), ('zhi', 'core'), pairs).astype(F32)  19.5 us
    all_to_all x1, blocking collectives, exchanged(): got = lax.all_to_all(blocks.astype(jnp.float16), axis, 0, 0, tiled=True)  16 us
    all_gather x1, blocking collectives, body(): whole = lax.all_gather(whole, 'y', axis=0, tiled=True)  11.4 us
    ppermute x3, waiting for transfers between devices, shifted(): lax.ppermute(block, axis, [(i, (i + distance) % n) for i in range(n)])  8.45 us
    ppermute x3, waiting for transfers between devices, turned(): lax.ppermute(block.astype(jnp.float16), ('zhi', 'core'), pairs).astype(F32)  2.55 us
  transfers between devices with their start and end apart: 6, of which 4 were waited for; matrix products, arithmetic and copies ran while one was open for 0% of the time, Pallas kernels for 0%

profile of v5, /device:TPU:1, one launch (start us, length us, event | category | flops | bytes accessed | tf_op | source)
XLA Modules:
  0.0 113.2 jit_solution(8657895197762720344)
XLA Ops:
  0.6 0.0 copy-start
  0.6 1.5 %copy-done = bf16[1,1,1,2,128,3584]{5,4,3,2,1,0:T(8,128)(2,1)S(1)} copy-done((bf16[1,1,1,2,128,3584]{5,4,3,2,1,0:T(8,128)(2,1)S(1)}, bf16[1,1,1,2,128,3584]{5,4,3,2,1,0:T(8,128)(2,1)}, u32[]{:S(2)}) %copy-start) | copy-done | bytes 1835032
  2.1 0.7 split_cores.1
  2.9 8.8 %collective-permute-start.3 = (bf16[4,32,3584]{2,1,0:T(8,128)(2,1)S(1)}, bf16[4,32,3584]{2,1,0:T(8,128)(2,1)S(1)}, u32[]{:S(2)}, u32[]{:S(2)}) collective-permute-start(bf16[4,32,3584]{2,1,0:T(8,128)(2,1)S(1)} %get-tuple-element.28), channel_id=1, source_target_pairs={{0,1},{1,0},{2,3},{3,2},{4,5},{5,4},{6,7},{7,6},{8,9},{9,8},{10,11... | collective-permute-start | bytes 2752520 | tf_op jit(solution)/shard_map/ppermute | solution.py:20
  12.4 0.1 pad_maximum_fusion.corr_ref
  12.5 0.1 pad_add_fusion.at_ref
  12.6 1.2 %collective-permute-done.3.theirs_ref = bf16[4,32,3584]{2,1,0:T(8,128)(2,1)S(1)} collective-permute-done((bf16[4,32,3584]{2,1,0:T(8,128)(2,1)S(1)}, bf16[4,32,3584]{2,1,0:T(8,128)(2,1)S(1)}, u32[]{:S(2)}, u32[]{:S(2)}) %collective-permute-start.3) | collective-permute-done | bytes 917536 | tf_op jit(solution)/shard_map/ppermute | solution.py:20
  13.8 0.6 add_pair.1
  14.3 0.1 convert_element_type.29
  14.4 16.0 %all_to_all.5 = f16[4,32,3712]{2,1,0:T(8,128)(2,1)S(1)} all-to-all(f16[4,32,3712]{2,1,0:T(8,128)(2,1)S(1)} %convert_element_type.29), channel_id=1, replica_groups=mesh['zlo'=4,'x'=4,'y'=4,'zhi'=4,'core'=2] {'y'}, dimensions={0} | all-to-all | bytes 1900544 | tf_op jit(solution)/shard_map/all_to_all | solution.py:194
  30.5 0.1 convert_element_type.30.got_ref
  30.6 0.0 copy-start.1
  30.6 0.0 copy-start.2
  30.6 0.0 copy-start.3
  30.6 1.0 add_y.1
  31.6 8.5 %collective-permute-start.5 = (f16[8,3712]{1,0:T(8,128)(2,1)S(1)}, f16[8,3712]{1,0:T(8,128)(2,1)S(1)}, u32[]{:S(2)}, u32[]{:S(2)}) collective-permute-start(f16[8,3712]{1,0:T(8,128)(2,1)S(1)} %convert_element_type.33), channel_id=1, source_target_pairs={{0,2},{1,7},{2,4},{3,1},{4,6},{5,3},{6,0},{7,5},{8,10},{9,15},{10,... | collective-permute-start | bytes 178184 | tf_op jit(solution)/shard_map/ppermute | solution.py:190
  40.2 1.9 %collective-permute-start.4 = (f16[8,3712]{1,0:T(8,128)(2,1)S(1)}, f16[8,3712]{1,0:T(8,128)(2,1)S(1)}, u32[]{:S(2)}, u32[]{:S(2)}) collective-permute-start(f16[8,3712]{1,0:T(8,128)(2,1)S(1)} %convert_element_type.31), channel_id=1, source_target_pairs={{0,6},{1,3},{2,0},{3,5},{4,2},{5,7},{6,4},{7,1},{8,14},{9,11},{10,... | collective-permute-start | bytes 178184 | tf_op jit(solution)/shard_map/ppermute | solution.py:190
  42.1 0.0 collective-permute-done.5
  42.1 0.2 add_through.1
  42.4 9.1 %collective-permute-start.6 = (f16[8,3712]{1,0:T(8,128)(2,1)S(1)}, f16[8,3712]{1,0:T(8,128)(2,1)S(1)}, u32[]{:S(2)}, u32[]{:S(2)}) collective-permute-start(f16[8,3712]{1,0:T(8,128)(2,1)S(1)} %convert_element_type.35), channel_id=1, source_target_pairs={{0,2},{1,7},{2,4},{3,1},{4,6},{5,3},{6,0},{7,5},{8,10},{9,15},{10,... | collective-permute-start | bytes 178184 | tf_op jit(solution)/shard_map/ppermute | solution.py:190
  51.5 0.0 collective-permute-done.4
  51.5 2.5 %collective-permute-done.6 = f16[8,3712]{1,0:T(8,128)(2,1)S(1)} collective-permute-done((f16[8,3712]{1,0:T(8,128)(2,1)S(1)}, f16[8,3712]{1,0:T(8,128)(2,1)S(1)}, u32[]{:S(2)}, u32[]{:S(2)}) %collective-permute-start.6) | collective-permute-done | bytes 59424 | tf_op jit(solution)/shard_map/ppermute | solution.py:190
  54.1 0.0 copy-done.1
  54.1 0.0 copy-done.2
  54.1 0.0 copy-done.3
  54.1 1.4 %adam.1 = (f32[2,4,3584]{2,1,0:T(4,128)}, f32[2,4,3584]{2,1,0:T(4,128)}, f32[2,4,3584]{2,1,0:T(4,128)S(1)}) custom-call(f32[2]{0:T(128)S(1)} %pad_maximum_fusion.corr_ref, f32[8,3584]{1,0:T(8,128)S(1)} %get-tuple-element.36.own_ref, f32[8,3712]{1,0:T(8,128)S(1)} %convert_element_type.32.far_ref, f32[8,3712]{1,0:T(8,128)S(1)} %convert_element_type.36.back_ref, ...), custom_call_target="tpu_custom_call" | custom-call | tf_op jit(solution)/shard_map/adam/pallas_call | solution.py:216
  55.5 9.8 %conditional.1 = (f32[2,4,3584]{2,1,0:T(4,128)}) conditional(s32[]{:T(128)} %clamp.3, f32[2,4,3584]{2,1,0:T(4,128)S(1)} %get-tuple-element.40.up_ref, f32[2,4,3584]{2,1,0:T(4,128)S(1)} %get-tuple-element.40.up_ref, f32[2,4,3584]{2,1,0:T(4,128)S(1)} %get-tuple-element.40.up_ref), branch_computations={%region_0.1_spmd, %region_1.2_spmd, %region_2.3_spmd} | conditional | bytes 458800 | solution.py:303
  55.5 4.6 %collective-permute-start.1 = (f32[2,4,3584]{2,1,0:T(4,128)S(1)}, f32[2,4,3584]{2,1,0:T(4,128)}, u32[]{:S(2)}, u32[]{:S(2)}) collective-permute-start(f32[2,4,3584]{2,1,0:T(4,128)S(1)} %param.1), channel_id=1, source_target_pairs={{0,64},{32,96},{64,128},{96,160},{128,192},{160,224},{192,256},{22... | collective-permute-start | bytes 344072 | tf_op jit(solution)/shard_map/cond/branch_1_fun/ppermute | solution.py:20
  60.2 5.2 %collective-permute-done.1 = f32[2,4,3584]{2,1,0:T(4,128)} collective-permute-done((f32[2,4,3584]{2,1,0:T(4,128)S(1)}, f32[2,4,3584]{2,1,0:T(4,128)}, u32[]{:S(2)}, u32[]{:S(2)}) %collective-permute-start.1) | collective-permute-done | bytes 114720 | tf_op jit(solution)/shard_map/cond/branch_1_fun/ppermute | solution.py:20
  65.3 1.6 %average.1 = (f32[2,4,3584]{2,1,0:T(4,128)}, bf16[8,3584]{1,0:T(8,128)(2,1)S(1)}) custom-call(f32[2,4,3584]{2,1,0:T(4,128)S(1)} %get-tuple-element.40.up_ref, f32[2,4,3584]{2,1,0:T(4,128)} %get-tuple-element.45.partner_ref), custom_call_target="tpu_custom_call" | custom-call | tf_op jit(solution)/shard_map/average/pallas_call | solution.py:235
  66.9 20.5 %all_gather.6 = bf16[32,3584]{1,0:T(8,128)(2,1)S(1)} all-gather(bf16[8,3584]{1,0:T(8,128)(2,1)S(1)} %get-tuple-element.44), channel_id=1, replica_groups=mesh['zlo'=4,'x'=4,'y'=4,'zhi'=4,'core'=2] {'zhi'}, dimensions={0}, use_global_device_ids=true | all-gather | bytes 286720 | tf_op jit(solution)/shard_map/all_gather | solution.py:307
  87.4 11.4 %all_gather.7.mine_ref = bf16[128,3584]{1,0:T(8,128)(2,1)S(1)} all-gather(bf16[32,3584]{1,0:T(8,128)(2,1)S(1)} %all_gather.6), channel_id=1, replica_groups=mesh['zlo'=4,'x'=4,'y'=4,'zhi'=4,'core'=2] {'y'}, dimensions={0}, use_global_device_ids=true | all-gather | bytes 1146880 | tf_op jit(solution)/shard_map/all_gather | solution.py:308
  98.8 10.3 %collective-permute-start.7 = (bf16[128,3584]{1,0:T(8,128)(2,1)S(1)}, bf16[128,3584]{1,0:T(8,128)(2,1)S(1)}, u32[]{:S(2)}, u32[]{:S(2)}) collective-permute-start(bf16[128,3584]{1,0:T(8,128)(2,1)S(1)} %all_gather.7.mine_ref), channel_id=1, source_target_pairs={{0,1},{1,0},{2,3},{3,2},{4,5},{5,4},{6,7},{7,6},{8,9},{9,8},{10,11... | collective-permute-start | bytes 2752520 | tf_op jit(solution)/shard_map/ppermute | solution.py:20
  109.1 2.1 %collective-permute-done.7.theirs_ref = bf16[128,3584]{1,0:T(8,128)(2,1)S(1)} collective-permute-done((bf16[128,3584]{1,0:T(8,128)(2,1)S(1)}, bf16[128,3584]{1,0:T(8,128)(2,1)S(1)}, u32[]{:S(2)}, u32[]{:S(2)}) %collective-permute-start.7) | collective-permute-done | bytes 917536 | tf_op jit(solution)/shard_map/ppermute | solution.py:20
  111.2 2.0 %join_cores.1 = bf16[2,128,3584]{2,1,0:T(8,128)(2,1)} custom-call(s32[1]{0:T(128)} %bitcast.core_ref, bf16[128,3584]{1,0:T(8,128)(2,1)S(1)} %all_gather.7.mine_ref, bf16[128,3584]{1,0:T(8,128)(2,1)S(1)} %collective-permute-done.7.theirs_ref), custom_call_target="tpu_custom_call" | custom-call | tf_op jit(solution)/shard_map/join_cores/pallas_call | solution.py:271
  (6 shorter events, 0.1 us)
Async XLA Ops:
  0.6 1.5 %copy-start = (bf16[1,1,1,2,128,3584]{5,4,3,2,1,0:T(8,128)(2,1)S(1)}, bf16[1,1,1,2,128,3584]{5,4,3,2,1,0:T(8,128)(2,1)}, u32[]{:S(2)}) copy-start(bf16[1,1,1,2,128,3584]{5,4,3,2,1,0:T(8,128)(2,1)} %param.9) | copy-start | bytes 5505028
  2.9 10.9 %collective-permute-start.3 = (bf16[4,32,3584]{2,1,0:T(8,128)(2,1)S(1)}, bf16[4,32,3584]{2,1,0:T(8,128)(2,1)S(1)}, u32[]{:S(2)}, u32[]{:S(2)}) collective-permute-start(bf16[4,32,3584]{2,1,0:T(8,128)(2,1)S(1)} %get-tuple-element.28), channel_id=1, source_target_pairs={{0,1},{1,0},{2,3},{3,2},{4,5},{5,4},{6,7},{7,6},{8,9},{9,8},{10,11... | collective-permute-start | bytes 2752520 | tf_op jit(solution)/shard_map/ppermute | solution.py:20
  30.6 23.5 %copy-start.1 = (f32[1,2,4,3584]{3,2,1,0:T(4,128)S(1)}, f32[1,2,4,3584]{3,2,1,0:T(4,128)}, u32[]{:S(2)}) copy-start(f32[1,2,4,3584]{3,2,1,0:T(4,128)} %param.10) | copy-start | bytes 344068
  30.6 23.5 %copy-start.2 = (f32[1,2,4,3584]{3,2,1,0:T(4,128)S(1)}, f32[1,2,4,3584]{3,2,1,0:T(4,128)}, u32[]{:S(2)}) copy-start(f32[1,2,4,3584]{3,2,1,0:T(4,128)} %param.11) | copy-start | bytes 344068
  30.6 23.5 %copy-start.3 = (f32[1,2,4,3584]{3,2,1,0:T(4,128)S(1)}, f32[1,2,4,3584]{3,2,1,0:T(4,128)}, u32[]{:S(2)}) copy-start(f32[1,2,4,3584]{3,2,1,0:T(4,128)} %param.12) | copy-start | bytes 344068
  31.6 10.5 %collective-permute-start.5 = (f16[8,3712]{1,0:T(8,128)(2,1)S(1)}, f16[8,3712]{1,0:T(8,128)(2,1)S(1)}, u32[]{:S(2)}, u32[]{:S(2)}) collective-permute-start(f16[8,3712]{1,0:T(8,128)(2,1)S(1)} %convert_element_type.33), channel_id=1, source_target_pairs={{0,2},{1,7},{2,4},{3,1},{4,6},{5,3},{6,0},{7,5},{8,10},{9,15},{10,... | collective-permute-start | bytes 178184 | tf_op jit(solution)/shard_map/ppermute | solution.py:190
  40.2 11.3 %collective-permute-start.4 = (f16[8,3712]{1,0:T(8,128)(2,1)S(1)}, f16[8,3712]{1,0:T(8,128)(2,1)S(1)}, u32[]{:S(2)}, u32[]{:S(2)}) collective-permute-start(f16[8,3712]{1,0:T(8,128)(2,1)S(1)} %convert_element_type.31), channel_id=1, source_target_pairs={{0,6},{1,3},{2,0},{3,5},{4,2},{5,7},{6,4},{7,1},{8,14},{9,11},{10,... | collective-permute-start | bytes 178184 | tf_op jit(solution)/shard_map/ppermute | solution.py:190
  42.4 11.7 %collective-permute-start.6 = (f16[8,3712]{1,0:T(8,128)(2,1)S(1)}, f16[8,3712]{1,0:T(8,128)(2,1)S(1)}, u32[]{:S(2)}, u32[]{:S(2)}) collective-permute-start(f16[8,3712]{1,0:T(8,128)(2,1)S(1)} %convert_element_type.35), channel_id=1, source_target_pairs={{0,2},{1,7},{2,4},{3,1},{4,6},{5,3},{6,0},{7,5},{8,10},{9,15},{10,... | collective-permute-start | bytes 178184 | tf_op jit(solution)/shard_map/ppermute | solution.py:190
  55.5 9.8 %collective-permute-start.1 = (f32[2,4,3584]{2,1,0:T(4,128)S(1)}, f32[2,4,3584]{2,1,0:T(4,128)}, u32[]{:S(2)}, u32[]{:S(2)}) collective-permute-start(f32[2,4,3584]{2,1,0:T(4,128)S(1)} %param.1), channel_id=1, source_target_pairs={{0,64},{32,96},{64,128},{96,160},{128,192},{160,224},{192,256},{22... | collective-permute-start | bytes 344072 | tf_op jit(solution)/shard_map/cond/branch_1_fun/ppermute | solution.py:20
  98.8 12.4 %collective-permute-start.7 = (bf16[128,3584]{1,0:T(8,128)(2,1)S(1)}, bf16[128,3584]{1,0:T(8,128)(2,1)S(1)}, u32[]{:S(2)}, u32[]{:S(2)}) collective-permute-start(bf16[128,3584]{1,0:T(8,128)(2,1)S(1)} %all_gather.7.mine_ref), channel_id=1, source_target_pairs={{0,1},{1,0},{2,3},{3,2},{4,5},{5,4},{6,7},{7,6},{8,9},{9,8},{10,11... | collective-permute-start | bytes 2752520 | tf_op jit(solution)/shard_map/ppermute | solution.py:20

commit v6 on v5

--- a/solution.py
+++ b/solution.py
@@ -27,20 +27,30 @@
     return low, high
 
 
-def split_kernel(core_ref, grads_ref, mine_ref, theirs_ref):
+def split_kernel(core_ref, grads_ref, mine_ref, theirs_ref, held, sems):
     first = core_ref[0] == 0
-    depth = grads_ref.shape[-1]
-    for at in range(0, depth, LANES):
-        cols = slice(at, at + LANES)
-        a = grads_ref[0, :, cols].astype(F32)
-        b = grads_ref[1, :, cols].astype(F32)
-        mine, theirs = [], []
-        for r in range(0, a.shape[0], 8):
-            low, high = low_high(a[r : r + 8], b[r : r + 8])
-            mine.append(jnp.where(first, low, high))
-            theirs.append(jnp.where(first, high, low))
-        mine_ref[0, :, cols] = jnp.concatenate(mine, 0).astype(BF16)
-        theirs_ref[0, :, cols] = jnp.concatenate(theirs, 0).astype(BF16)
+    n, _, per, depth = held.shape
+    copies = [
+        pltpu.make_async_copy(
+            grads_ref.at[:, k * per : (k + 1) * per, :], held.at[k], sems.at[k]
+        )
+        for k in range(n)
+    ]
+    for copy in copies:
+        copy.start()
+    for k, copy in enumerate(copies):
+        copy.wait()
+        for at in range(0, depth, LANES):
+            cols = slice(at, at + LANES)
+            a = held[k, 0, :, cols].astype(F32)
+            b = held[k, 1, :, cols].astype(F32)
+            mine, theirs = [], []
+            for r in range(0, per, 8):
+                low, high = low_high(a[r : r + 8], b[r : r + 8])
+                mine.append(jnp.where(first, low, high))
+                theirs.append(jnp.where(first, high, low))
+            mine_ref[k, :, cols] = jnp.concatenate(mine, 0).astype(BF16)
+            theirs_ref[k, :, cols] = jnp.concatenate(theirs, 0).astype(BF16)
 
 
 def split_cores(grads, core):
@@ -48,17 +58,16 @@
     ny = lax.axis_size("y")
     per = rows // ny
     out = jax.ShapeDtypeStruct((ny, per, depth), BF16)
-    block = pl.BlockSpec((1, per, depth), lambda k, w: (k, 0, 0))
     return pl.pallas_call(
         split_kernel,
-        grid_spec=pltpu.PrefetchScalarGridSpec(
-            num_scalar_prefetch=1,
-            grid=(ny,),
-            in_specs=[pl.BlockSpec((layers, per, depth), lambda k, w: (0, k, 0))],
-            out_specs=[block, block],
-        ),
+        in_specs=[SMEM, pl.BlockSpec(memory_space=pltpu.HBM)],
+        out_specs=[VMEM] * 2,
         out_shape=(out, out),
-        compiler_params=PARAMS,
+        scratch_shapes=[
+            pltpu.VMEM((ny, layers, per, depth), BF16),
+            pltpu.SemaphoreType.DMA((ny,)),
+        ],
+        compiler_params=pltpu.CompilerParams(vmem_limit_bytes=52 * 2**20),
         name="split_cores",
     )(core, grads)
 
@@ -195,38 +204,40 @@
     return got.astype(F32)
 
 
-def adam_kernel(corr_ref, own_ref, far_ref, back_ref, master_ref, first_ref, second_ref, nf_ref, ns_ref, up_ref):
+def moments(mean, first, second):
+    return 0.9 * first + 0.1 * mean, 0.95 * second + 0.05 * mean * mean
+
+
+def adam_kernel(corr_ref, own_ref, far_ref, back_ref, master_ref, first_ref, second_ref, mean_ref, up_ref):
     depth = own_ref.shape[-1]
     total = own_ref[...] + (restored(far_ref, depth) + restored(back_ref, depth))
     mean_all = total * (1.0 / 32)
+    mean_ref[...] = mean_all
     for layer in range(2):
         mean = mean_all[4 * layer : 4 * layer + 4]
         master = master_ref[layer]
-        nf = 0.9 * first_ref[layer] + 0.1 * mean
-        ns = 0.95 * second_ref[layer] + 0.05 * mean * mean
-        nf_ref[layer] = nf
-        ns_ref[layer] = ns
+        nf, ns = moments(mean, first_ref[layer], second_ref[layer])
         up_ref[layer] = master - 0.05 * (
             nf / corr_ref[0] / (jnp.sqrt(ns / corr_ref[1]) + 1e-08) + 0.1 * master
         )
 
 
 def adam(corr, own, far, back, master, first, second):
-    out = jax.ShapeDtypeStruct(master.shape, F32)
     return pl.pallas_call(
         adam_kernel,
         in_specs=[SMEM] + [VMEM] * 6,
-        out_specs=[VMEM] * 3,
-        out_shape=[out] * 3,
+        out_specs=[VMEM] * 2,
+        out_shape=[
+            jax.ShapeDtypeStruct(own.shape, F32),
+            jax.ShapeDtypeStruct(master.shape, F32),
+        ],
         compiler_params=PARAMS,
         name="adam",
     )(corr, own, far, back, master, first, second)
 
 
-def average_kernel(up_ref, partner_ref, out_ref, rounded_ref):
+def average_kernel(up_ref, partner_ref, rounded_ref):
     mean = [(up_ref[i] + partner_ref[i]) * 0.5 for i in range(2)]
-    for i in range(2):
-        out_ref[i] = mean[i]
     rounded_ref[...] = jnp.concatenate(mean, 0).astype(BF16)
 
 
@@ -235,48 +246,70 @@
     return pl.pallas_call(
         average_kernel,
         in_specs=[VMEM] * 2,
-        out_specs=[VMEM] * 2,
-        out_shape=[
-            jax.ShapeDtypeStruct(updated.shape, F32),
-            jax.ShapeDtypeStruct((layers * rows, depth), BF16),
-        ],
+        out_specs=VMEM,
+        out_shape=jax.ShapeDtypeStruct((layers * rows, depth), BF16),
         compiler_params=PARAMS,
         name="average",
     )(updated, partner)
 
 
-def join_kernel(core_ref, mine_ref, theirs_ref, out_ref):
+def finish_kernel(mean_ref, first_ref, second_ref, up_ref, partner_ref, out_ref, nf_ref, ns_ref):
+    for layer in range(2):
+        mean = mean_ref[4 * layer : 4 * layer + 4, :]
+        nf, ns = moments(mean, first_ref[layer], second_ref[layer])
+        nf_ref[layer] = nf
+        ns_ref[layer] = ns
+        out_ref[layer] = (up_ref[layer] + partner_ref[layer]) * 0.5
+
+
+def finish(mean, first, second, updated, partner):
+    return pl.pallas_call(
+        finish_kernel,
+        in_specs=[VMEM] * 5,
+        out_specs=[VMEM] * 3,
+        out_shape=[jax.ShapeDtypeStruct(first.shape, F32)] * 3,
+        compiler_params=PARAMS,
+        name="finish",
+    )(mean, first, second, updated, partner)
+
+
+def join_kernel(core_ref, mine_ref, theirs_ref, out_ref, held, sems):
     first = core_ref[0] == 0
-    depth = mine_ref.shape[-1]
-    for at in range(0, depth, LANES):
-        cols = slice(at, at + LANES)
-        mine = mine_ref[:, cols].astype(F32)
-        theirs = theirs_ref[:, cols].astype(F32)
-        a = jnp.where(first, mine, theirs)
-        b = jnp.where(first, theirs, mine)
-        lows, highs = [], []
-        for r in range(0, a.shape[0], 8):
-            low, high = low_high(a[r : r + 8], b[r : r + 8])
-            lows.append(low)
-            highs.append(high)
-        out_ref[0, :, cols] = jnp.concatenate(lows, 0).astype(BF16)
-        out_ref[1, :, cols] = jnp.concatenate(highs, 0).astype(BF16)
+    n, _, per, depth = held.shape
+    copies = []
+    for k in range(n):
+        rows = slice(k * per, (k + 1) * per)
+        for at in range(0, depth, LANES):
+            cols = slice(at, at + LANES)
+            mine = mine_ref[rows, cols].astype(F32)
+            theirs = theirs_ref[rows, cols].astype(F32)
+            a = jnp.where(first, mine, theirs)
+            b = jnp.where(first, theirs, mine)
+            lows, highs = [], []
+            for r in range(0, per, 8):
+                low, high = low_high(a[r : r + 8], b[r : r + 8])
+                lows.append(low)
+                highs.append(high)
+            held[k, 0, :, cols] = jnp.concatenate(lows, 0).astype(BF16)
+            held[k, 1, :, cols] = jnp.concatenate(highs, 0).astype(BF16)
+        copies.append(pltpu.make_async_copy(held.at[k], out_ref.at[:, rows, :], sems.at[k]))
+        copies[k].start()
+    for copy in copies:
+        copy.wait()
 
 
 def join_cores(mine, theirs, core):
     rows, depth = mine.shape
     steps = 4
-    per = rows // steps
-    block = pl.BlockSpec((per, depth), lambda k, w: (k, 0))
     return pl.pallas_call(
         join_kernel,
-        grid_spec=pltpu.PrefetchScalarGridSpec(
-            num_scalar_prefetch=1,
-            grid=(steps,),
-            in_specs=[block, block],
-            out_specs=pl.BlockSpec((2, per, depth), lambda k, w: (0, k, 0)),
-        ),
+        in_specs=[SMEM, VMEM, VMEM],
+        out_specs=pl.BlockSpec(memory_space=pltpu.HBM),
         out_shape=jax.ShapeDtypeStruct((2, rows, depth), BF16),
+        scratch_shapes=[
+            pltpu.VMEM((steps, 2, rows // steps, depth), BF16),
+            pltpu.SemaphoreType.DMA((steps,)),
+        ],
         compiler_params=PARAMS,
         name="join_cores",
     )(core, mine, theirs)
@@ -297,16 +330,21 @@
     far = turned(far, 1)
     back = turned(back, -1)
     far = turned(add_through(near, far), 1)
-    new_first, new_second, updated = adam(
+    mean, updated = adam(
         corr, own, back, far, master[0], first_moment[0], second_moment[0]
     )
     partner = lax.switch(
         t % 3, [lambda u, d=d: shifted(u, PEER, d) for d in (1, 2, 4)], updated
     )
-    averaged, whole = average(updated, partner)
+    whole = average(updated, partner)
     whole = lax.all_gather(whole, "zhi", axis=0, tiled=True)
     whole = lax.all_gather(whole, "y", axis=0, tiled=True)
-    whole = join_cores(whole, shifted(whole, "core", 1), core)
+    whole, mean, updated, partner = lax.optimization_barrier((whole, mean, updated, partner))
+    other = shifted(whole, "core", 1)
+    averaged, new_first, new_second = finish(
+        mean, first_moment[0], second_moment[0], updated, partner
+    )
+    whole = join_cores(whole, other, core)
     return (averaged[None], new_first[None], new_second[None], whole[None])
 
 

time: 114 us -> 111 us (0.974)
  waiting for transfers between devices: 11 us -> 9.34 us
  local copies, waits for them, and re-layouts: 1.51 us -> 0.02 us
  blocking collectives: 48 us -> 46.8 us
    ppermute x3, waiting for transfers between devices: 8.45 us -> 6.79 us  [shifted(): lax.ppermute(block, axis, [(i, (i + distance) % n) for i in range(n)])]
    unnamed x8 -> x6, local copies, waits for them, and re-layouts: 1.51 us -> 0.02 us
    pallas_call x3 -> x4, Pallas kernels: 4.27 us -> 5.57 us  [the longest x1 1.66 us: finish(): pl.pallas_call(finish_kernel, in_specs=[VMEM] * 5, out_specs=[VMEM] * 3,...]
  transfers between devices with their start and end apart: 6 -> 6, of which waited for: 4 -> 4; matrix products, arithmetic and copies ran while one was open for 0% -> 0% of each run, Pallas kernels for 0% -> 2%
where the time goes in v6:
time: 111 us; the launch traced here: 110 us
  blocking collectives  46.8 us (42%)
  starting transfers between devices  44.1 us (40%)
  waiting for transfers between devices  9.34 us (8%)
  Pallas kernels  8.09 us (7%)
  between operations  1.6 us (1%)
    ppermute x3, starting transfers between devices, shifted(): lax.ppermute(block, axis, [(i, (i + distance) % n) for i in range(n)])  24.6 us
    all_gather x1, blocking collectives, body(): whole = lax.all_gather(whole, 'zhi', axis=0, tiled=True)  19.8 us
    ppermute x3, starting transfers between devices, turned(): lax.ppermute(block.astype(jnp.float16), ('zhi', 'core'), pairs).astype(F32)  19.5 us
    all_to_all x1, blocking collectives, exchanged(): got = lax.all_to_all(blocks.astype(jnp.float16), axis, 0, 0, tiled=True)  16 us
    all_gather x1, blocking collectives, body(): whole = lax.all_gather(whole, 'y', axis=0, tiled=True)  11 us
    ppermute x3, waiting for transfers between devices, shifted(): lax.ppermute(block, axis, [(i, (i + distance) % n) for i in range(n)])  6.79 us
    ppermute x3, waiting for transfers between devices, turned(): lax.ppermute(block.astype(jnp.float16), ('zhi', 'core'), pairs).astype(F32)  2.55 us
  transfers between devices with their start and end apart: 6, of which 4 were waited for; matrix products, arithmetic and copies ran while one was open for 0% of the time, Pallas kernels for 2%

profile of v6, /device:TPU:1, one launch (start us, length us, event | category | flops | bytes accessed | tf_op | source)
XLA Modules:
  0.0 110.4 jit_solution(14297174008183548100)
XLA Ops:
  0.6 1.6 %split_cores.1 = (bf16[4,32,3584]{2,1,0:T(8,128)(2,1)S(1)}, bf16[4,32,3584]{2,1,0:T(8,128)(2,1)S(1)}) custom-call(s32[1]{0:T(128)} %bitcast.core_ref, bf16[2,128,3584]{2,1,0:T(8,128)(2,1)} %bitcast.17), custom_call_target="tpu_custom_call" | custom-call | tf_op jit(solution)/shard_map/split_cores/pallas_call | solution.py:61
  2.2 8.8 %collective-permute-start.3 = (bf16[4,32,3584]{2,1,0:T(8,128)(2,1)S(1)}, bf16[4,32,3584]{2,1,0:T(8,128)(2,1)S(1)}, u32[]{:S(2)}, u32[]{:S(2)}) collective-permute-start(bf16[4,32,3584]{2,1,0:T(8,128)(2,1)S(1)} %get-tuple-element.32), channel_id=1, source_target_pairs={{0,1},{1,0},{2,3},{3,2},{4,5},{5,4},{6,7},{7,6},{8,9},{9,8},{10,11... | collective-permute-start | bytes 2752520 | tf_op jit(solution)/shard_map/ppermute | solution.py:20
  11.8 0.1 pad_maximum_fusion.corr_ref
  11.9 0.1 pad_add_fusion.at_ref
  11.9 1.2 %collective-permute-done.3.theirs_ref = bf16[4,32,3584]{2,1,0:T(8,128)(2,1)S(1)} collective-permute-done((bf16[4,32,3584]{2,1,0:T(8,128)(2,1)S(1)}, bf16[4,32,3584]{2,1,0:T(8,128)(2,1)S(1)}, u32[]{:S(2)}, u32[]{:S(2)}) %collective-permute-start.3) | collective-permute-done | bytes 917536 | tf_op jit(solution)/shard_map/ppermute | solution.py:20
  13.1 0.6 add_pair.1
  13.7 0.1 convert_element_type.29
  13.8 16.0 %all_to_all.5 = f16[4,32,3712]{2,1,0:T(8,128)(2,1)S(1)} all-to-all(f16[4,32,3712]{2,1,0:T(8,128)(2,1)S(1)} %convert_element_type.29), channel_id=1, replica_groups=mesh['zlo'=4,'x'=4,'y'=4,'zhi'=4,'core'=2] {'y'}, dimensions={0} | all-to-all | bytes 1900544 | tf_op jit(solution)/shard_map/all_to_all | solution.py:203
  29.8 0.1 convert_element_type.30.got_ref
  30.0 0.0 copy-start
  30.0 0.0 copy-start.1
  30.0 0.0 copy-start.2
  30.0 1.0 add_y.1
  31.0 8.5 %collective-permute-start.5 = (f16[8,3712]{1,0:T(8,128)(2,1)S(1)}, f16[8,3712]{1,0:T(8,128)(2,1)S(1)}, u32[]{:S(2)}, u32[]{:S(2)}) collective-permute-start(f16[8,3712]{1,0:T(8,128)(2,1)S(1)} %convert_element_type.33), channel_id=1, source_target_pairs={{0,2},{1,7},{2,4},{3,1},{4,6},{5,3},{6,0},{7,5},{8,10},{9,15},{10,... | collective-permute-start | bytes 178184 | tf_op jit(solution)/shard_map/ppermute | solution.py:199
  39.5 1.9 %collective-permute-start.4 = (f16[8,3712]{1,0:T(8,128)(2,1)S(1)}, f16[8,3712]{1,0:T(8,128)(2,1)S(1)}, u32[]{:S(2)}, u32[]{:S(2)}) collective-permute-start(f16[8,3712]{1,0:T(8,128)(2,1)S(1)} %convert_element_type.31), channel_id=1, source_target_pairs={{0,6},{1,3},{2,0},{3,5},{4,2},{5,7},{6,4},{7,1},{8,14},{9,11},{10,... | collective-permute-start | bytes 178184 | tf_op jit(solution)/shard_map/ppermute | solution.py:199
  41.5 0.0 collective-permute-done.5
  41.5 0.2 add_through.1
  41.7 9.1 %collective-permute-start.6 = (f16[8,3712]{1,0:T(8,128)(2,1)S(1)}, f16[8,3712]{1,0:T(8,128)(2,1)S(1)}, u32[]{:S(2)}, u32[]{:S(2)}) collective-permute-start(f16[8,3712]{1,0:T(8,128)(2,1)S(1)} %convert_element_type.35), channel_id=1, source_target_pairs={{0,2},{1,7},{2,4},{3,1},{4,6},{5,3},{6,0},{7,5},{8,10},{9,15},{10,... | collective-permute-start | bytes 178184 | tf_op jit(solution)/shard_map/ppermute | solution.py:199
  50.9 0.0 collective-permute-done.4
  50.9 2.5 %collective-permute-done.6 = f16[8,3712]{1,0:T(8,128)(2,1)S(1)} collective-permute-done((f16[8,3712]{1,0:T(8,128)(2,1)S(1)}, f16[8,3712]{1,0:T(8,128)(2,1)S(1)}, u32[]{:S(2)}, u32[]{:S(2)}) %collective-permute-start.6) | collective-permute-done | bytes 59424 | tf_op jit(solution)/shard_map/ppermute | solution.py:199
  53.4 0.0 copy-done
  53.5 0.0 copy-done.1
  53.5 0.0 copy-done.2
  53.5 0.8 adam.1
  54.2 9.9 %conditional.1 = (f32[2,4,3584]{2,1,0:T(4,128)}) conditional(s32[]{:T(128)} %clamp.3, f32[2,4,3584]{2,1,0:T(4,128)S(1)} %get-tuple-element.47.up_ref, f32[2,4,3584]{2,1,0:T(4,128)S(1)} %get-tuple-element.47.up_ref, f32[2,4,3584]{2,1,0:T(4,128)S(1)} %get-tuple-element.47.up_ref), branch_computations={%region_0.1_spmd, %region_1.2_spmd, %region_2.3_spmd} | conditional | bytes 458800 | solution.py:336
  54.3 4.7 %collective-permute-start.1 = (f32[2,4,3584]{2,1,0:T(4,128)S(1)}, f32[2,4,3584]{2,1,0:T(4,128)}, u32[]{:S(2)}, u32[]{:S(2)}) collective-permute-start(f32[2,4,3584]{2,1,0:T(4,128)S(1)} %param.1), channel_id=1, source_target_pairs={{0,64},{32,96},{64,128},{96,160},{128,192},{160,224},{192,256},{22... | collective-permute-start | bytes 344072 | tf_op jit(solution)/shard_map/cond/branch_1_fun/ppermute | solution.py:20
  58.9 5.2 %collective-permute-done.1 = f32[2,4,3584]{2,1,0:T(4,128)} collective-permute-done((f32[2,4,3584]{2,1,0:T(4,128)S(1)}, f32[2,4,3584]{2,1,0:T(4,128)}, u32[]{:S(2)}, u32[]{:S(2)}) %collective-permute-start.1) | collective-permute-done | bytes 114720 | tf_op jit(solution)/shard_map/cond/branch_1_fun/ppermute | solution.py:20
  64.1 0.9 average.1
  65.0 19.8 %all_gather.6 = bf16[32,3584]{1,0:T(8,128)(2,1)S(1)} all-gather(bf16[8,3584]{1,0:T(8,128)(2,1)S(1)} %average.1), channel_id=1, replica_groups=mesh['zlo'=4,'x'=4,'y'=4,'zhi'=4,'core'=2] {'zhi'}, dimensions={0}, use_global_device_ids=true | all-gather | bytes 286720 | tf_op jit(solution)/shard_map/all_gather | solution.py:340
  84.8 11.0 %all_gather.7.mine_ref = bf16[128,3584]{1,0:T(8,128)(2,1)S(1)} all-gather(bf16[32,3584]{1,0:T(8,128)(2,1)S(1)} %all_gather.6), channel_id=1, replica_groups=mesh['zlo'=4,'x'=4,'y'=4,'zhi'=4,'core'=2] {'y'}, dimensions={0}, use_global_device_ids=true | all-gather | bytes 1146880 | tf_op jit(solution)/shard_map/all_gather | solution.py:341
  95.8 11.1 %collective-permute-start.7 = (bf16[128,3584]{1,0:T(8,128)(2,1)S(1)}, bf16[128,3584]{1,0:T(8,128)(2,1)S(1)}, u32[]{:S(2)}, u32[]{:S(2)}) collective-permute-start(bf16[128,3584]{1,0:T(8,128)(2,1)S(1)} %all_gather.7.mine_ref), channel_id=1, source_target_pairs={{0,1},{1,0},{2,3},{3,2},{4,5},{5,4},{6,7},{7,6},{8,9},{9,8},{10,11... | collective-permute-start | bytes 2752520 | tf_op jit(solution)/shard_map/ppermute | solution.py:20
  106.9 1.7 %finish.1 = (f32[2,4,3584]{2,1,0:T(4,128)}, f32[2,4,3584]{2,1,0:T(4,128)}, f32[2,4,3584]{2,1,0:T(4,128)}) custom-call(f32[8,3584]{1,0:T(8,128)S(1)} %get-tuple-element.46.mean_ref, f32[2,4,3584]{2,1,0:T(4,128)S(1)} %bitcast.13, f32[2,4,3584]{2,1,0:T(4,128)S(1)} %bitcast.15, f32[2,4,3584]{2,1,0:T(4,128)S(1)} %get-tuple-element.47.up_ref, ...), custom_call_target="tpu_custom_call" | custom-call | tf_op jit(solution)/shard_map/finish/pallas_call | solution.py:266
  108.6 0.4 collective-permute-done.7.theirs_ref
  109.0 1.4 %join_cores.1 = bf16[2,128,3584]{2,1,0:T(8,128)(2,1)} custom-call(s32[1]{0:T(128)} %bitcast.core_ref, bf16[128,3584]{1,0:T(8,128)(2,1)S(1)} %all_gather.7.mine_ref, bf16[128,3584]{1,0:T(8,128)(2,1)S(1)} %collective-permute-done.7.theirs_ref), custom_call_target="tpu_custom_call" | custom-call | tf_op jit(solution)/shard_map/join_cores/pallas_call | solution.py:304
  (6 shorter events, 0.1 us)
Async XLA Ops:
  2.2 10.9 %collective-permute-start.3 = (bf16[4,32,3584]{2,1,0:T(8,128)(2,1)S(1)}, bf16[4,32,3584]{2,1,0:T(8,128)(2,1)S(1)}, u32[]{:S(2)}, u32[]{:S(2)}) collective-permute-start(bf16[4,32,3584]{2,1,0:T(8,128)(2,1)S(1)} %get-tuple-element.32), channel_id=1, source_target_pairs={{0,1},{1,0},{2,3},{3,2},{4,5},{5,4},{6,7},{7,6},{8,9},{9,8},{10,11... | collective-permute-start | bytes 2752520 | tf_op jit(solution)/shard_map/ppermute | solution.py:20
  30.0 23.5 %copy-start = (f32[1,2,4,3584]{3,2,1,0:T(4,128)S(1)}, f32[1,2,4,3584]{3,2,1,0:T(4,128)}, u32[]{:S(2)}) copy-start(f32[1,2,4,3584]{3,2,1,0:T(4,128)} %param.11) | copy-start | bytes 344068
  30.0 23.5 %copy-start.1 = (f32[1,2,4,3584]{3,2,1,0:T(4,128)S(1)}, f32[1,2,4,3584]{3,2,1,0:T(4,128)}, u32[]{:S(2)}) copy-start(f32[1,2,4,3584]{3,2,1,0:T(4,128)} %param.12) | copy-start | bytes 344068
  30.0 23.5 %copy-start.2 = (f32[1,2,4,3584]{3,2,1,0:T(4,128)S(1)}, f32[1,2,4,3584]{3,2,1,0:T(4,128)}, u32[]{:S(2)}) copy-start(f32[1,2,4,3584]{3,2,1,0:T(4,128)} %param.10) | copy-start | bytes 344068
  31.0 10.5 %collective-permute-start.5 = (f16[8,3712]{1,0:T(8,128)(2,1)S(1)}, f16[8,3712]{1,0:T(8,128)(2,1)S(1)}, u32[]{:S(2)}, u32[]{:S(2)}) collective-permute-start(f16[8,3712]{1,0:T(8,128)(2,1)S(1)} %convert_element_type.33), channel_id=1, source_target_pairs={{0,2},{1,7},{2,4},{3,1},{4,6},{5,3},{6,0},{7,5},{8,10},{9,15},{10,... | collective-permute-start | bytes 178184 | tf_op jit(solution)/shard_map/ppermute | solution.py:199
  39.5 11.3 %collective-permute-start.4 = (f16[8,3712]{1,0:T(8,128)(2,1)S(1)}, f16[8,3712]{1,0:T(8,128)(2,1)S(1)}, u32[]{:S(2)}, u32[]{:S(2)}) collective-permute-start(f16[8,3712]{1,0:T(8,128)(2,1)S(1)} %convert_element_type.31), channel_id=1, source_target_pairs={{0,6},{1,3},{2,0},{3,5},{4,2},{5,7},{6,4},{7,1},{8,14},{9,11},{10,... | collective-permute-start | bytes 178184 | tf_op jit(solution)/shard_map/ppermute | solution.py:199
  41.7 11.7 %collective-permute-start.6 = (f16[8,3712]{1,0:T(8,128)(2,1)S(1)}, f16[8,3712]{1,0:T(8,128)(2,1)S(1)}, u32[]{:S(2)}, u32[]{:S(2)}) collective-permute-start(f16[8,3712]{1,0:T(8,128)(2,1)S(1)} %convert_element_type.35), channel_id=1, source_target_pairs={{0,2},{1,7},{2,4},{3,1},{4,6},{5,3},{6,0},{7,5},{8,10},{9,15},{10,... | collective-permute-start | bytes 178184 | tf_op jit(solution)/shard_map/ppermute | solution.py:199
  54.3 9.8 %collective-permute-start.1 = (f32[2,4,3584]{2,1,0:T(4,128)S(1)}, f32[2,4,3584]{2,1,0:T(4,128)}, u32[]{:S(2)}, u32[]{:S(2)}) collective-permute-start(f32[2,4,3584]{2,1,0:T(4,128)S(1)} %param.1), channel_id=1, source_target_pairs={{0,64},{32,96},{64,128},{96,160},{128,192},{160,224},{192,256},{22... | collective-permute-start | bytes 344072 | tf_op jit(solution)/shard_map/cond/branch_1_fun/ppermute | solution.py:20
  95.8 13.2 %collective-permute-start.7 = (bf16[128,3584]{1,0:T(8,128)(2,1)S(1)}, bf16[128,3584]{1,0:T(8,128)(2,1)S(1)}, u32[]{:S(2)}, u32[]{:S(2)}) collective-permute-start(bf16[128,3584]{1,0:T(8,128)(2,1)S(1)} %all_gather.7.mine_ref), channel_id=1, source_target_pairs={{0,1},{1,0},{2,3},{3,2},{4,5},{5,4},{6,7},{7,6},{8,9},{9,8},{10,11... | collective-permute-start | bytes 2752520 | tf_op jit(solution)/shard_map/ppermute | solution.py:20

commit v7 on v6

--- a/solution.py
+++ b/solution.py
@@ -77,54 +77,43 @@
     return jnp.exp2(exponent), -exponent
 
 
-def send_scaled(out_ref, sums):
-    n, per, _ = out_ref.shape
-    depth = sums.shape[-1]
+def add_pair_kernel(at_ref, mine_ref, theirs_ref, own_ref, near_ref, far_ref, back_ref, sums):
+    n, per, depth = mine_ref.shape
     largest = jnp.zeros((8, LANES), F32)
-    for at in range(0, depth, LANES):
-        for r in range(0, n * per, 8):
-            largest = jnp.maximum(largest, jnp.abs(sums[r : r + 8, at : at + LANES]))
-    scale, back = scale_of(jnp.max(largest, axis=(0, 1), keepdims=True))
     for k in range(n):
         for at in range(0, depth, LANES):
             cols = slice(at, at + LANES)
-            out_ref[k, :, cols] = sums[k * per : (k + 1) * per, cols] * scale
-        out_ref[k, :, depth:] = jnp.broadcast_to(back, (per, out_ref.shape[-1] - depth))
-
-
-def add_received(total, got_ref, me, cols, depth):
-    for k in range(got_ref.shape[0]):
-        undo = jnp.exp2(got_ref[k, 0:1, depth : depth + 1])
-        total = total + jnp.where(me == k, 0.0, got_ref[k, :, cols] * undo)
-    return total
-
-
-def add_pair_kernel(y_ref, mine_ref, theirs_ref, own_ref, out_ref, sums):
-    n, per, depth = mine_ref.shape
-    for k in range(n):
+            total = mine_ref[k, :, cols].astype(F32) + theirs_ref[k, :, cols].astype(F32)
+            sums[k * per : (k + 1) * per, cols] = total
+            for r in range(0, per, 8):
+                largest = jnp.maximum(largest, jnp.abs(total[r : r + 8]))
+    scale, back = scale_of(jnp.max(largest, axis=(0, 1), keepdims=True))
+
+    def piece(k):
+        step = jnp.where(at_ref[2] == 0, k, n - k)
+        return pl.ds(pl.multiple_of(((at_ref[0] + step) % n) * per, per), per)
+
+    own_ref[...] = sums[piece(0), :]
+    for k, out_ref in ((1, near_ref), (2, far_ref), (3, back_ref)):
+        rows = piece(k)
         for at in range(0, depth, LANES):
             cols = slice(at, at + LANES)
-            sums[k * per : (k + 1) * per, cols] = mine_ref[k, :, cols].astype(F32) + theirs_ref[
-                k, :, cols
-            ].astype(F32)
-    own_ref[...] = sums[pl.ds(pl.multiple_of(y_ref[0] * per, per), per), :]
-    send_scaled(out_ref, sums)
-
-
-def add_pair(y, mine, theirs):
+            out_ref[:, cols] = sums[rows, cols] * scale
+        out_ref[:, depth:] = jnp.broadcast_to(back, (per, out_ref.shape[-1] - depth))
+
+
+def add_pair(at, mine, theirs):
     n, rows, depth = mine.shape
     return pl.pallas_call(
         add_pair_kernel,
         in_specs=[SMEM, VMEM, VMEM],
-        out_specs=[VMEM] * 2,
-        out_shape=[
-            jax.ShapeDtypeStruct((rows, depth), F32),
-            jax.ShapeDtypeStruct((n, rows, depth + 128), F32),
-        ],
+        out_specs=[VMEM] * 4,
+        out_shape=[jax.ShapeDtypeStruct((rows, depth), F32)]
+        + [jax.ShapeDtypeStruct((rows, depth + 128), F32)] * 3,
         scratch_shapes=[pltpu.VMEM((n * rows, depth), F32)],
         compiler_params=PARAMS,
         name="add_pair",
-    )(y, mine, theirs)
+    )(at, mine, theirs)
 
 
 def scaled(block_ref, out_ref):
@@ -141,12 +130,15 @@
     return got_ref[:, :depth] * jnp.exp2(got_ref[0:1, depth : depth + 1])
 
 
-def add_y_kernel(at_ref, own_ref, got_ref, keep_ref, near_ref, far_ref, back_ref, sums):
+def add_y_kernel(at_ref, own_ref, a_ref, b_ref, c_ref, keep_ref, near_ref, far_ref, back_ref, sums):
     depth = own_ref.shape[-1]
     n = sums.shape[0] // 8
     for at in range(0, depth, LANES):
         cols = slice(at, at + LANES)
-        sums[:, cols] = add_received(own_ref[:, cols], got_ref, at_ref[0], cols, depth)
+        total = own_ref[:, cols]
+        for got_ref in (a_ref, b_ref, c_ref):
+            total = total + got_ref[:, cols] * jnp.exp2(got_ref[0:1, depth : depth + 1])
+        sums[:, cols] = total
 
     def piece(k):
         step = jnp.where(at_ref[2] == 0, k, n - k)
@@ -158,19 +150,19 @@
     scaled(sums.at[piece(3)], back_ref)
 
 
-def add_y(at, own, got):
+def add_y(at, own, parts):
     rows, depth = own.shape
     kept = jax.ShapeDtypeStruct((8, depth), F32)
     sent = jax.ShapeDtypeStruct((8, depth + 128), F32)
     return pl.pallas_call(
         add_y_kernel,
-        in_specs=[SMEM, VMEM, VMEM],
+        in_specs=[SMEM] + [VMEM] * 4,
         out_specs=[VMEM] * 4,
         out_shape=[kept, kept, sent, sent],
         scratch_shapes=[pltpu.VMEM((rows, depth), F32)],
         compiler_params=PARAMS,
         name="add_y",
-    )(at, own, got)
+    )(at, own, *parts)
 
 
 def add_through_kernel(near_ref, got_ref, out_ref, total):
@@ -190,18 +182,13 @@
     )(near, got)
 
 
-def turned(block, distance):
-    n = lax.axis_size("zhi")
+def turned(block, axis, distance):
+    n = lax.axis_size(axis)
     pairs = []
-    for z in range(n):
-        pairs.append((2 * z, 2 * ((z + distance) % n)))
-        pairs.append((2 * z + 1, 2 * ((z - distance) % n) + 1))
-    return lax.ppermute(block.astype(jnp.float16), ("zhi", "core"), pairs).astype(F32)
-
-
-def exchanged(blocks, axis):
-    got = lax.all_to_all(blocks.astype(jnp.float16), axis, 0, 0, tiled=True)
-    return got.astype(F32)
+    for i in range(n):
+        pairs.append((2 * i, 2 * ((i + distance) % n)))
+        pairs.append((2 * i + 1, 2 * ((i - distance) % n) + 1))
+    return lax.ppermute(block.astype(jnp.float16), (axis, "core"), pairs).astype(F32)
 
 
 def moments(mean, first, second):
@@ -324,12 +311,13 @@
 
     mine, theirs = split_cores(grads[0, 0, 0], core)
     theirs = shifted(theirs, "core", 1)
-    theirs, y, at, corr = lax.optimization_barrier((theirs, y, at, corr))
-    own, out = add_pair(y, mine, theirs)
-    own, near, far, back = add_y(at, own, exchanged(out, "y"))
-    far = turned(far, 1)
-    back = turned(back, -1)
-    far = turned(add_through(near, far), 1)
+    theirs, at, corr = lax.optimization_barrier((theirs, at, corr))
+    own, near, far, back = add_pair(at, mine, theirs)
+    parts = [turned(near, "y", 1), turned(back, "y", -1), turned(far, "y", 2)]
+    own, near, far, back = add_y(at, own, parts)
+    far = turned(far, "zhi", 1)
+    back = turned(back, "zhi", -1)
+    far = turned(add_through(near, far), "zhi", 1)
     mean, updated = adam(
         corr, own, back, far, master[0], first_moment[0], second_moment[0]
     )

time: 111 us -> 109 us (0.982)
  blocking collectives: 46.8 us -> 30.6 us
  waiting for transfers between devices: 9.34 us -> 18.1 us
  starting transfers between devices: 44.1 us -> 50 us
    all_to_all x1 -> x0, blocking collectives: 16 us -> none  [exchanged(): got = lax.all_to_all(blocks.astype(jnp.float16), axis, 0, 0, tiled=True)]
    ppermute x3 -> x6, starting transfers between devices: 19.5 us -> 27.1 us  [turned(): lax.ppermute(block.astype(jnp.float16), (axis, 'core'), pairs).astype(F32)]
    ppermute x3 -> x6, waiting for transfers between devices: 2.55 us -> 10 us  [turned(): lax.ppermute(block.astype(jnp.float16), (axis, 'core'), pairs).astype(F32)]
    ppermute x3, starting transfers between devices: 24.6 us -> 23 us  [shifted(): lax.ppermute(block, axis, [(i, (i + distance) % n) for i in range(n)])]
    ppermute x3, waiting for transfers between devices: 6.79 us -> 8.03 us  [shifted(): lax.ppermute(block, axis, [(i, (i + distance) % n) for i in range(n)])]
  transfers between devices with their start and end apart: 6 -> 9, of which waited for: 4 -> 6; matrix products, arithmetic and copies ran while one was open for 0% -> 0% of each run, Pallas kernels for 2% -> 2%
where the time goes in v7:
time: 109 us; the launch traced here: 110 us
  starting transfers between devices  50 us (46%)
  blocking collectives  30.6 us (28%)
  waiting for transfers between devices  18.1 us (17%)
  Pallas kernels  8.67 us (8%)
  between operations  1.65 us (2%)
    ppermute x6, starting transfers between devices, turned(): lax.ppermute(block.astype(jnp.float16), (axis, 'core'), pairs).astype(F32)  27.1 us
    ppermute x3, starting transfers between devices, shifted(): lax.ppermute(block, axis, [(i, (i + distance) % n) for i in range(n)])  23 us
    all_gather x1, blocking collectives, body(): whole = lax.all_gather(whole, 'zhi', axis=0, tiled=True)  19.6 us
    all_gather x1, blocking collectives, body(): whole = lax.all_gather(whole, 'y', axis=0, tiled=True)  11 us
    ppermute x6, waiting for transfers between devices, turned(): lax.ppermute(block.astype(jnp.float16), (axis, 'core'), pairs).astype(F32)  10 us
    ppermute x3, waiting for transfers between devices, shifted(): lax.ppermute(block, axis, [(i, (i + distance) % n) for i in range(n)])  8.03 us
  transfers between devices with their start and end apart: 9, of which 6 were waited for; matrix products, arithmetic and copies ran while one was open for 0% of the time, Pallas kernels for 2%

profile of v7, /device:TPU:1, one launch (start us, length us, event | category | flops | bytes accessed | tf_op | source)
XLA Modules:
  0.0 109.5 jit_solution(17777318565018416952)
XLA Ops:
  0.6 1.6 %split_cores.1 = (bf16[4,32,3584]{2,1,0:T(8,128)(2,1)S(1)}, bf16[4,32,3584]{2,1,0:T(8,128)(2,1)S(1)}) custom-call(s32[1]{0:T(128)} %bitcast.core_ref, bf16[2,128,3584]{2,1,0:T(8,128)(2,1)} %bitcast.17), custom_call_target="tpu_custom_call" | custom-call | tf_op jit(solution)/shard_map/split_cores/pallas_call | solution.py:61
  2.2 8.8 %collective-permute-start.3 = (bf16[4,32,3584]{2,1,0:T(8,128)(2,1)S(1)}, bf16[4,32,3584]{2,1,0:T(8,128)(2,1)S(1)}, u32[]{:S(2)}, u32[]{:S(2)}) collective-permute-start(bf16[4,32,3584]{2,1,0:T(8,128)(2,1)S(1)} %get-tuple-element.33), channel_id=1, source_target_pairs={{0,1},{1,0},{2,3},{3,2},{4,5},{5,4},{6,7},{7,6},{8,9},{9,8},{10,11... | collective-permute-start | bytes 2752520 | tf_op jit(solution)/shard_map/ppermute | solution.py:20
  11.8 0.1 pad_maximum_fusion.corr_ref
  11.9 0.1 pad_add_fusion.at_ref
  11.9 1.2 %collective-permute-done.3.theirs_ref = bf16[4,32,3584]{2,1,0:T(8,128)(2,1)S(1)} collective-permute-done((bf16[4,32,3584]{2,1,0:T(8,128)(2,1)S(1)}, bf16[4,32,3584]{2,1,0:T(8,128)(2,1)S(1)}, u32[]{:S(2)}, u32[]{:S(2)}) %collective-permute-start.3) | collective-permute-done | bytes 917536 | tf_op jit(solution)/shard_map/ppermute | solution.py:20
  13.1 1.2 %add_pair.1 = (f32[32,3584]{1,0:T(8,128)S(1)}, f32[32,3712]{1,0:T(8,128)S(1)}, f32[32,3712]{1,0:T(8,128)S(1)}, f32[32,3712]{1,0:T(8,128)S(1)}) custom-call(s32[3]{0:T(128)S(1)} %pad_add_fusion.at_ref, bf16[4,32,3584]{2,1,0:T(8,128)(2,1)S(1)} %get-tuple-element.36.mine_ref, bf16[4,32,3584]{2,1,0:T(8,128)(2,1)S(1)} %collective-permute-done.3.theirs_ref), custom_call_target="tpu_custom_call" | custom-call | tf_op jit(solution)/shard_map/add_pair/pallas_call | solution.py:107
  14.4 1.9 %collective-permute-start.6 = (f16[32,3712]{1,0:T(8,128)(2,1)S(1)}, f16[32,3712]{1,0:T(8,128)(2,1)S(1)}, u32[]{:S(2)}, u32[]{:S(2)}) collective-permute-start(f16[32,3712]{1,0:T(8,128)(2,1)S(1)} %convert_element_type.45), channel_id=1, source_target_pairs={{0,16},{1,17},{8,24},{9,25},{16,0},{17,1},{24,8},{25,9},{2,18},{3,... | collective-permute-start | bytes 712712 | tf_op jit(solution)/shard_map/ppermute | solution.py:191
  16.4 1.9 %collective-permute-start.5 = (f16[32,3712]{1,0:T(8,128)(2,1)S(1)}, f16[32,3712]{1,0:T(8,128)(2,1)S(1)}, u32[]{:S(2)}, u32[]{:S(2)}) collective-permute-start(f16[32,3712]{1,0:T(8,128)(2,1)S(1)} %convert_element_type.43), channel_id=1, source_target_pairs={{0,24},{1,9},{8,0},{9,17},{16,8},{17,25},{24,16},{25,1},{2,26},{3,... | collective-permute-start | bytes 712712 | tf_op jit(solution)/shard_map/ppermute | solution.py:191
  18.3 4.6 %collective-permute-start.4 = (f16[32,3712]{1,0:T(8,128)(2,1)S(1)}, f16[32,3712]{1,0:T(8,128)(2,1)S(1)}, u32[]{:S(2)}, u32[]{:S(2)}) collective-permute-start(f16[32,3712]{1,0:T(8,128)(2,1)S(1)} %convert_element_type.41), channel_id=1, source_target_pairs={{0,8},{1,25},{8,16},{9,1},{16,24},{17,9},{24,0},{25,17},{2,10},{3,... | collective-permute-start | bytes 712712 | tf_op jit(solution)/shard_map/ppermute | solution.py:191
  22.9 2.0 %collective-permute-done.6 = f16[32,3712]{1,0:T(8,128)(2,1)S(1)} collective-permute-done((f16[32,3712]{1,0:T(8,128)(2,1)S(1)}, f16[32,3712]{1,0:T(8,128)(2,1)S(1)}, u32[]{:S(2)}, u32[]{:S(2)}) %collective-permute-start.6) | collective-permute-done | bytes 237600 | tf_op jit(solution)/shard_map/ppermute | solution.py:191
  24.9 5.2 %collective-permute-done.5 = f16[32,3712]{1,0:T(8,128)(2,1)S(1)} collective-permute-done((f16[32,3712]{1,0:T(8,128)(2,1)S(1)}, f16[32,3712]{1,0:T(8,128)(2,1)S(1)}, u32[]{:S(2)}, u32[]{:S(2)}) %collective-permute-start.5) | collective-permute-done | bytes 237600 | tf_op jit(solution)/shard_map/ppermute | solution.py:191
  30.2 0.0 collective-permute-done.4
  30.2 0.0 copy-start
  30.2 0.0 copy-start.1
  30.2 0.0 copy-start.2
  30.3 0.9 add_y.1
  31.2 8.0 %collective-permute-start.8 = (f16[8,3712]{1,0:T(8,128)(2,1)S(1)}, f16[8,3712]{1,0:T(8,128)(2,1)S(1)}, u32[]{:S(2)}, u32[]{:S(2)}) collective-permute-start(f16[8,3712]{1,0:T(8,128)(2,1)S(1)} %convert_element_type.49), channel_id=1, source_target_pairs={{0,2},{1,7},{2,4},{3,1},{4,6},{5,3},{6,0},{7,5},{8,10},{9,15},{10,... | collective-permute-start | bytes 178184 | tf_op jit(solution)/shard_map/ppermute | solution.py:191
  39.2 1.9 %collective-permute-start.7 = (f16[8,3712]{1,0:T(8,128)(2,1)S(1)}, f16[8,3712]{1,0:T(8,128)(2,1)S(1)}, u32[]{:S(2)}, u32[]{:S(2)}) collective-permute-start(f16[8,3712]{1,0:T(8,128)(2,1)S(1)} %convert_element_type.47), channel_id=1, source_target_pairs={{0,6},{1,3},{2,0},{3,5},{4,2},{5,7},{6,4},{7,1},{8,14},{9,11},{10,... | collective-permute-start | bytes 178184 | tf_op jit(solution)/shard_map/ppermute | solution.py:191
  41.1 0.0 collective-permute-done.8
  41.1 0.2 add_through.1
  41.4 8.8 %collective-permute-start.9 = (f16[8,3712]{1,0:T(8,128)(2,1)S(1)}, f16[8,3712]{1,0:T(8,128)(2,1)S(1)}, u32[]{:S(2)}, u32[]{:S(2)}) collective-permute-start(f16[8,3712]{1,0:T(8,128)(2,1)S(1)} %convert_element_type.51), channel_id=1, source_target_pairs={{0,2},{1,7},{2,4},{3,1},{4,6},{5,3},{6,0},{7,5},{8,10},{9,15},{10,... | collective-permute-start | bytes 178184 | tf_op jit(solution)/shard_map/ppermute | solution.py:191
  50.2 0.0 collective-permute-done.7
  50.2 2.8 %collective-permute-done.9 = f16[8,3712]{1,0:T(8,128)(2,1)S(1)} collective-permute-done((f16[8,3712]{1,0:T(8,128)(2,1)S(1)}, f16[8,3712]{1,0:T(8,128)(2,1)S(1)}, u32[]{:S(2)}, u32[]{:S(2)}) %collective-permute-start.9) | collective-permute-done | bytes 59424 | tf_op jit(solution)/shard_map/ppermute | solution.py:191
  53.1 0.0 copy-done
  53.1 0.0 copy-done.1
  53.1 0.0 copy-done.2
  53.1 0.8 adam.1
  53.9 9.6 %conditional.1 = (f32[2,4,3584]{2,1,0:T(4,128)}) conditional(s32[]{:T(128)} %clamp.3, f32[2,4,3584]{2,1,0:T(4,128)S(1)} %get-tuple-element.49.up_ref, f32[2,4,3584]{2,1,0:T(4,128)S(1)} %get-tuple-element.49.up_ref, f32[2,4,3584]{2,1,0:T(4,128)S(1)} %get-tuple-element.49.up_ref), branch_computations={%region_0.1_spmd, %region_1.2_spmd, %region_2.3_spmd} | conditional | bytes 458800 | solution.py:324
  53.9 3.1 %collective-permute-start = (f32[2,4,3584]{2,1,0:T(4,128)S(1)}, f32[2,4,3584]{2,1,0:T(4,128)}, u32[]{:S(2)}, u32[]{:S(2)}) collective-permute-start(f32[2,4,3584]{2,1,0:T(4,128)S(1)} %param), channel_id=1, source_target_pairs={{0,32},{32,64},{64,96},{96,128},{128,160},{160,192},{192,224},{224... | collective-permute-start | bytes 344072 | tf_op jit(solution)/shard_map/cond/branch_0_fun/ppermute | solution.py:20
  57.0 6.4 %collective-permute-done = f32[2,4,3584]{2,1,0:T(4,128)} collective-permute-done((f32[2,4,3584]{2,1,0:T(4,128)S(1)}, f32[2,4,3584]{2,1,0:T(4,128)}, u32[]{:S(2)}, u32[]{:S(2)}) %collective-permute-start) | collective-permute-done | bytes 114720 | tf_op jit(solution)/shard_map/cond/branch_0_fun/ppermute | solution.py:20
  63.4 0.9 average.1
  64.3 19.6 %all_gather.6 = bf16[32,3584]{1,0:T(8,128)(2,1)S(1)} all-gather(bf16[8,3584]{1,0:T(8,128)(2,1)S(1)} %average.1), channel_id=1, replica_groups=mesh['zlo'=4,'x'=4,'y'=4,'zhi'=4,'core'=2] {'zhi'}, dimensions={0}, use_global_device_ids=true | all-gather | bytes 286720 | tf_op jit(solution)/shard_map/all_gather | solution.py:328
  84.0 11.0 %all_gather.7.mine_ref = bf16[128,3584]{1,0:T(8,128)(2,1)S(1)} all-gather(bf16[32,3584]{1,0:T(8,128)(2,1)S(1)} %all_gather.6), channel_id=1, replica_groups=mesh['zlo'=4,'x'=4,'y'=4,'zhi'=4,'core'=2] {'y'}, dimensions={0}, use_global_device_ids=true | all-gather | bytes 1146880 | tf_op jit(solution)/shard_map/all_gather | solution.py:329
  95.0 11.0 %collective-permute-start.10 = (bf16[128,3584]{1,0:T(8,128)(2,1)S(1)}, bf16[128,3584]{1,0:T(8,128)(2,1)S(1)}, u32[]{:S(2)}, u32[]{:S(2)}) collective-permute-start(bf16[128,3584]{1,0:T(8,128)(2,1)S(1)} %all_gather.7.mine_ref), channel_id=1, source_target_pairs={{0,1},{1,0},{2,3},{3,2},{4,5},{5,4},{6,7},{7,6},{8,9},{9,8},{10,11... | collective-permute-start | bytes 2752520 | tf_op jit(solution)/shard_map/ppermute | solution.py:20
  106.0 1.7 %finish.1 = (f32[2,4,3584]{2,1,0:T(4,128)}, f32[2,4,3584]{2,1,0:T(4,128)}, f32[2,4,3584]{2,1,0:T(4,128)}) custom-call(f32[8,3584]{1,0:T(8,128)S(1)} %get-tuple-element.48.mean_ref, f32[2,4,3584]{2,1,0:T(4,128)S(1)} %bitcast.13, f32[2,4,3584]{2,1,0:T(4,128)S(1)} %bitcast.15, f32[2,4,3584]{2,1,0:T(4,128)S(1)} %get-tuple-element.49.up_ref, ...), custom_call_target="tpu_custom_call" | custom-call | tf_op jit(solution)/shard_map/finish/pallas_call | solution.py:253
  107.7 0.4 collective-permute-done.10.theirs_ref
  108.1 1.4 %join_cores.1 = bf16[2,128,3584]{2,1,0:T(8,128)(2,1)} custom-call(s32[1]{0:T(128)} %bitcast.core_ref, bf16[128,3584]{1,0:T(8,128)(2,1)S(1)} %all_gather.7.mine_ref, bf16[128,3584]{1,0:T(8,128)(2,1)S(1)} %collective-permute-done.10.theirs_ref), custom_call_target="tpu_custom_call" | custom-call | tf_op jit(solution)/shard_map/join_cores/pallas_call | solution.py:291
  (12 shorter events, 0.2 us)
Async XLA Ops:
  2.2 10.9 %collective-permute-start.3 = (bf16[4,32,3584]{2,1,0:T(8,128)(2,1)S(1)}, bf16[4,32,3584]{2,1,0:T(8,128)(2,1)S(1)}, u32[]{:S(2)}, u32[]{:S(2)}) collective-permute-start(bf16[4,32,3584]{2,1,0:T(8,128)(2,1)S(1)} %get-tuple-element.33), channel_id=1, source_target_pairs={{0,1},{1,0},{2,3},{3,2},{4,5},{5,4},{6,7},{7,6},{8,9},{9,8},{10,11... | collective-permute-start | bytes 2752520 | tf_op jit(solution)/shard_map/ppermute | solution.py:20
  14.4 10.4 %collective-permute-start.6 = (f16[32,3712]{1,0:T(8,128)(2,1)S(1)}, f16[32,3712]{1,0:T(8,128)(2,1)S(1)}, u32[]{:S(2)}, u32[]{:S(2)}) collective-permute-start(f16[32,3712]{1,0:T(8,128)(2,1)S(1)} %convert_element_type.45), channel_id=1, source_target_pairs={{0,16},{1,17},{8,24},{9,25},{16,0},{17,1},{24,8},{25,9},{2,18},{3,... | collective-permute-start | bytes 712712 | tf_op jit(solution)/shard_map/ppermute | solution.py:191
  16.4 13.8 %collective-permute-start.5 = (f16[32,3712]{1,0:T(8,128)(2,1)S(1)}, f16[32,3712]{1,0:T(8,128)(2,1)S(1)}, u32[]{:S(2)}, u32[]{:S(2)}) collective-permute-start(f16[32,3712]{1,0:T(8,128)(2,1)S(1)} %convert_element_type.43), channel_id=1, source_target_pairs={{0,24},{1,9},{8,0},{9,17},{16,8},{17,25},{24,16},{25,1},{2,26},{3,... | collective-permute-start | bytes 712712 | tf_op jit(solution)/shard_map/ppermute | solution.py:191
  18.3 11.9 %collective-permute-start.4 = (f16[32,3712]{1,0:T(8,128)(2,1)S(1)}, f16[32,3712]{1,0:T(8,128)(2,1)S(1)}, u32[]{:S(2)}, u32[]{:S(2)}) collective-permute-start(f16[32,3712]{1,0:T(8,128)(2,1)S(1)} %convert_element_type.41), channel_id=1, source_target_pairs={{0,8},{1,25},{8,16},{9,1},{16,24},{17,9},{24,0},{25,17},{2,10},{3,... | collective-permute-start | bytes 712712 | tf_op jit(solution)/shard_map/ppermute | solution.py:191
  30.2 22.8 %copy-start = (f32[1,2,4,3584]{3,2,1,0:T(4,128)S(1)}, f32[1,2,4,3584]{3,2,1,0:T(4,128)}, u32[]{:S(2)}) copy-start(f32[1,2,4,3584]{3,2,1,0:T(4,128)} %param.11) | copy-start | bytes 344068
  30.2 22.8 %copy-start.1 = (f32[1,2,4,3584]{3,2,1,0:T(4,128)S(1)}, f32[1,2,4,3584]{3,2,1,0:T(4,128)}, u32[]{:S(2)}) copy-start(f32[1,2,4,3584]{3,2,1,0:T(4,128)} %param.12) | copy-start | bytes 344068
  30.2 22.8 %copy-start.2 = (f32[1,2,4,3584]{3,2,1,0:T(4,128)S(1)}, f32[1,2,4,3584]{3,2,1,0:T(4,128)}, u32[]{:S(2)}) copy-start(f32[1,2,4,3584]{3,2,1,0:T(4,128)} %param.10) | copy-start | bytes 344068
  31.2 9.9 %collective-permute-start.8 = (f16[8,3712]{1,0:T(8,128)(2,1)S(1)}, f16[8,3712]{1,0:T(8,128)(2,1)S(1)}, u32[]{:S(2)}, u32[]{:S(2)}) collective-permute-start(f16[8,3712]{1,0:T(8,128)(2,1)S(1)} %convert_element_type.49), channel_id=1, source_target_pairs={{0,2},{1,7},{2,4},{3,1},{4,6},{5,3},{6,0},{7,5},{8,10},{9,15},{10,... | collective-permute-start | bytes 178184 | tf_op jit(solution)/shard_map/ppermute | solution.py:191
  39.2 11.0 %collective-permute-start.7 = (f16[8,3712]{1,0:T(8,128)(2,1)S(1)}, f16[8,3712]{1,0:T(8,128)(2,1)S(1)}, u32[]{:S(2)}, u32[]{:S(2)}) collective-permute-start(f16[8,3712]{1,0:T(8,128)(2,1)S(1)} %convert_element_type.47), channel_id=1, source_target_pairs={{0,6},{1,3},{2,0},{3,5},{4,2},{5,7},{6,4},{7,1},{8,14},{9,11},{10,... | collective-permute-start | bytes 178184 | tf_op jit(solution)/shard_map/ppermute | solution.py:191
  41.4 11.7 %collective-permute-start.9 = (f16[8,3712]{1,0:T(8,128)(2,1)S(1)}, f16[8,3712]{1,0:T(8,128)(2,1)S(1)}, u32[]{:S(2)}, u32[]{:S(2)}) collective-permute-start(f16[8,3712]{1,0:T(8,128)(2,1)S(1)} %convert_element_type.51), channel_id=1, source_target_pairs={{0,2},{1,7},{2,4},{3,1},{4,6},{5,3},{6,0},{7,5},{8,10},{9,15},{10,... | collective-permute-start | bytes 178184 | tf_op jit(solution)/shard_map/ppermute | solution.py:191
  53.9 9.6 %collective-permute-start = (f32[2,4,3584]{2,1,0:T(4,128)S(1)}, f32[2,4,3584]{2,1,0:T(4,128)}, u32[]{:S(2)}, u32[]{:S(2)}) collective-permute-start(f32[2,4,3584]{2,1,0:T(4,128)S(1)} %param), channel_id=1, source_target_pairs={{0,32},{32,64},{64,96},{96,128},{128,160},{160,192},{192,224},{224... | collective-permute-start | bytes 344072 | tf_op jit(solution)/shard_map/cond/branch_0_fun/ppermute | solution.py:20
  95.0 13.1 %collective-permute-start.10 = (bf16[128,3584]{1,0:T(8,128)(2,1)S(1)}, bf16[128,3584]{1,0:T(8,128)(2,1)S(1)}, u32[]{:S(2)}, u32[]{:S(2)}) collective-permute-start(bf16[128,3584]{1,0:T(8,128)(2,1)S(1)} %all_gather.7.mine_ref), channel_id=1, source_target_pairs={{0,1},{1,0},{2,3},{3,2},{4,5},{5,4},{6,7},{7,6},{8,9},{9,8},{10,11... | collective-permute-start | bytes 2752520 | tf_op jit(solution)/shard_map/ppermute | solution.py:20

commit v8 on v7

--- a/solution.py
+++ b/solution.py
@@ -1,3 +1,5 @@
+import functools
+
 import jax
 import jax.numpy as jnp
 from jax import lax
@@ -77,42 +79,34 @@
     return jnp.exp2(exponent), -exponent
 
 
-def add_pair_kernel(at_ref, mine_ref, theirs_ref, own_ref, near_ref, far_ref, back_ref, sums):
+def add_pair_kernel(step, at_ref, mine_ref, theirs_ref, out_ref, sums):
     n, per, depth = mine_ref.shape
+    ahead = step if step == 2 else jnp.where(at_ref[2] == 0, step, n - step)
+    y = (at_ref[0] + ahead) % n
     largest = jnp.zeros((8, LANES), F32)
-    for k in range(n):
-        for at in range(0, depth, LANES):
-            cols = slice(at, at + LANES)
-            total = mine_ref[k, :, cols].astype(F32) + theirs_ref[k, :, cols].astype(F32)
-            sums[k * per : (k + 1) * per, cols] = total
-            for r in range(0, per, 8):
-                largest = jnp.maximum(largest, jnp.abs(total[r : r + 8]))
+    for at in range(0, depth, LANES):
+        cols = slice(at, at + LANES)
+        total = mine_ref[y, :, cols].astype(F32) + theirs_ref[y, :, cols].astype(F32)
+        sums[:, cols] = total
+        for r in range(0, per, 8):
+            largest = jnp.maximum(largest, jnp.abs(total[r : r + 8]))
     scale, back = scale_of(jnp.max(largest, axis=(0, 1), keepdims=True))
-
-    def piece(k):
-        step = jnp.where(at_ref[2] == 0, k, n - k)
-        return pl.ds(pl.multiple_of(((at_ref[0] + step) % n) * per, per), per)
-
-    own_ref[...] = sums[piece(0), :]
-    for k, out_ref in ((1, near_ref), (2, far_ref), (3, back_ref)):
-        rows = piece(k)
-        for at in range(0, depth, LANES):
-            cols = slice(at, at + LANES)
-            out_ref[:, cols] = sums[rows, cols] * scale
-        out_ref[:, depth:] = jnp.broadcast_to(back, (per, out_ref.shape[-1] - depth))
-
-
-def add_pair(at, mine, theirs):
-    n, rows, depth = mine.shape
-    return pl.pallas_call(
-        add_pair_kernel,
+    for at in range(0, depth, LANES):
+        cols = slice(at, at + LANES)
+        out_ref[:, cols] = sums[:, cols] * scale
+    out_ref[:, depth:] = jnp.broadcast_to(back, (per, out_ref.shape[-1] - depth))
+
+
+def add_pair(step, at, mine, theirs):
+    _, rows, depth = mine.shape
+    return pl.pallas_call(
+        functools.partial(add_pair_kernel, step),
         in_specs=[SMEM, VMEM, VMEM],
-        out_specs=[VMEM] * 4,
-        out_shape=[jax.ShapeDtypeStruct((rows, depth), F32)]
-        + [jax.ShapeDtypeStruct((rows, depth + 128), F32)] * 3,
-        scratch_shapes=[pltpu.VMEM((n * rows, depth), F32)],
-        compiler_params=PARAMS,
-        name="add_pair",
+        out_specs=VMEM,
+        out_shape=jax.ShapeDtypeStruct((rows, depth + 128), F32),
+        scratch_shapes=[pltpu.VMEM((rows, depth), F32)],
+        compiler_params=PARAMS,
+        name=f"add_pair_{step}",
     )(at, mine, theirs)
 
 
@@ -130,12 +124,13 @@
     return got_ref[:, :depth] * jnp.exp2(got_ref[0:1, depth : depth + 1])
 
 
-def add_y_kernel(at_ref, own_ref, a_ref, b_ref, c_ref, keep_ref, near_ref, far_ref, back_ref, sums):
-    depth = own_ref.shape[-1]
+def add_y_kernel(at_ref, mine_ref, theirs_ref, a_ref, b_ref, c_ref, keep_ref, near_ref, far_ref, back_ref, sums):
+    depth = mine_ref.shape[-1]
     n = sums.shape[0] // 8
+    y = at_ref[0]
     for at in range(0, depth, LANES):
         cols = slice(at, at + LANES)
-        total = own_ref[:, cols]
+        total = mine_ref[y, :, cols].astype(F32) + theirs_ref[y, :, cols].astype(F32)
         for got_ref in (a_ref, b_ref, c_ref):
             total = total + got_ref[:, cols] * jnp.exp2(got_ref[0:1, depth : depth + 1])
         sums[:, cols] = total
@@ -150,19 +145,19 @@
     scaled(sums.at[piece(3)], back_ref)
 
 
-def add_y(at, own, parts):
-    rows, depth = own.shape
+def add_y(at, mine, theirs, parts):
+    _, rows, depth = mine.shape
     kept = jax.ShapeDtypeStruct((8, depth), F32)
     sent = jax.ShapeDtypeStruct((8, depth + 128), F32)
     return pl.pallas_call(
         add_y_kernel,
-        in_specs=[SMEM] + [VMEM] * 4,
+        in_specs=[SMEM] + [VMEM] * 5,
         out_specs=[VMEM] * 4,
         out_shape=[kept, kept, sent, sent],
         scratch_shapes=[pltpu.VMEM((rows, depth), F32)],
         compiler_params=PARAMS,
         name="add_y",
-    )(at, own, *parts)
+    )(at, mine, theirs, *parts)
 
 
 def add_through_kernel(near_ref, got_ref, out_ref, total):
@@ -312,9 +307,10 @@
     mine, theirs = split_cores(grads[0, 0, 0], core)
     theirs = shifted(theirs, "core", 1)
     theirs, at, corr = lax.optimization_barrier((theirs, at, corr))
-    own, near, far, back = add_pair(at, mine, theirs)
-    parts = [turned(near, "y", 1), turned(back, "y", -1), turned(far, "y", 2)]
-    own, near, far, back = add_y(at, own, parts)
+    parts = [
+        turned(add_pair(step, at, mine, theirs), "y", step) for step in (1, 3, 2)
+    ]
+    own, near, far, back = add_y(at, mine, theirs, parts)
     far = turned(far, "zhi", 1)
     back = turned(back, "zhi", -1)
     far = turned(add_through(near, far), "zhi", 1)

time: 109 us -> 112 us (1.028); the launches traced: 110 us -> 111 us
  starting transfers between devices: 50 us -> 51.8 us
  waiting for transfers between devices: 18.1 us -> 16.8 us
  Pallas kernels: 8.67 us -> 9.93 us
    ppermute x3, starting transfers between devices: 23 us -> 24.7 us  [shifted(): lax.ppermute(block, axis, [(i, (i + distance) % n) for i in range(n)])]
    pallas_call x2 -> x4, Pallas kernels: 2.12 us -> 3.38 us  [the longest x3 2.47 us: add_pair(): pl.pallas_call(functools.partial(add_pair_kernel, step), in_specs=[SMEM,...]
    ppermute x3, waiting for transfers between devices: 8.03 us -> 6.79 us  [shifted(): lax.ppermute(block, axis, [(i, (i + distance) % n) for i in range(n)])]
where the time goes in v8:
time: 112 us; the launch traced here: 111 us
  starting transfers between devices  51.8 us (46%)
  blocking collectives  30.8 us (28%)
  waiting for transfers between devices  16.8 us (15%)
  Pallas kernels  9.93 us (9%)
  between operations  1.67 us (1%)
    ppermute x6, starting transfers between devices, turned(): lax.ppermute(block.astype(jnp.float16), (axis, 'core'), pairs).astype(F32)  27.1 us
    ppermute x3, starting transfers between devices, shifted(): lax.ppermute(block, axis, [(i, (i + distance) % n) for i in range(n)])  24.7 us
    all_gather x1, blocking collectives, body(): whole = lax.all_gather(whole, 'zhi', axis=0, tiled=True)  19.8 us
    all_gather x1, blocking collectives, body(): whole = lax.all_gather(whole, 'y', axis=0, tiled=True)  11 us
    ppermute x6, waiting for transfers between devices, turned(): lax.ppermute(block.astype(jnp.float16), (axis, 'core'), pairs).astype(F32)  9.99 us
    ppermute x3, waiting for transfers between devices, shifted(): lax.ppermute(block, axis, [(i, (i + distance) % n) for i in range(n)])  6.79 us
    pallas_call x3, Pallas kernels, add_pair(): pl.pallas_call(functools.partial(add_pair_kernel, step), in_specs=[SMEM,...  2.47 us
  transfers between devices with their start and end apart: 9, of which 6 were waited for; matrix products, arithmetic and copies ran while one was open for 0% of the time, Pallas kernels for 2%

profile of v8, /device:TPU:1, one launch (start us, length us, event | category | flops | bytes accessed | tf_op | source)
XLA Modules:
  0.0 111.4 jit_solution(12299326825543585277)
XLA Ops:
  0.6 1.6 %split_cores.1 = (bf16[4,32,3584]{2,1,0:T(8,128)(2,1)S(1)}, bf16[4,32,3584]{2,1,0:T(8,128)(2,1)S(1)}) custom-call(s32[1]{0:T(128)} %bitcast.core_ref, bf16[2,128,3584]{2,1,0:T(8,128)(2,1)} %bitcast.17), custom_call_target="tpu_custom_call" | custom-call | tf_op jit(solution)/shard_map/split_cores/pallas_call | solution.py:63
  2.2 8.8 %collective-permute-start.3 = (bf16[4,32,3584]{2,1,0:T(8,128)(2,1)S(1)}, bf16[4,32,3584]{2,1,0:T(8,128)(2,1)S(1)}, u32[]{:S(2)}, u32[]{:S(2)}) collective-permute-start(bf16[4,32,3584]{2,1,0:T(8,128)(2,1)S(1)} %get-tuple-element.29), channel_id=1, source_target_pairs={{0,1},{1,0},{2,3},{3,2},{4,5},{5,4},{6,7},{7,6},{8,9},{9,8},{10,11... | collective-permute-start | bytes 2752520 | tf_op jit(solution)/shard_map/ppermute | solution.py:22
  11.8 0.1 pad_maximum_fusion.corr_ref
  11.9 0.1 pad_add_fusion.at_ref
  11.9 1.2 %collective-permute-done.3.theirs_ref = bf16[4,32,3584]{2,1,0:T(8,128)(2,1)S(1)} collective-permute-done((bf16[4,32,3584]{2,1,0:T(8,128)(2,1)S(1)}, bf16[4,32,3584]{2,1,0:T(8,128)(2,1)S(1)}, u32[]{:S(2)}, u32[]{:S(2)}) %collective-permute-start.3) | collective-permute-done | bytes 917536 | tf_op jit(solution)/shard_map/ppermute | solution.py:22
  13.1 0.8 add_pair_2.1
  13.9 0.8 add_pair_3.1
  14.8 0.8 add_pair_1.1
  15.6 1.9 %collective-permute-start.6 = (f16[32,3712]{1,0:T(8,128)(2,1)S(1)}, f16[32,3712]{1,0:T(8,128)(2,1)S(1)}, u32[]{:S(2)}, u32[]{:S(2)}) collective-permute-start(f16[32,3712]{1,0:T(8,128)(2,1)S(1)} %convert_element_type.45), channel_id=1, source_target_pairs={{0,16},{1,17},{8,24},{9,25},{16,0},{17,1},{24,8},{25,9},{2,18},{3,... | collective-permute-start | bytes 712712 | tf_op jit(solution)/shard_map/ppermute | solution.py:186
  17.6 1.9 %collective-permute-start.5 = (f16[32,3712]{1,0:T(8,128)(2,1)S(1)}, f16[32,3712]{1,0:T(8,128)(2,1)S(1)}, u32[]{:S(2)}, u32[]{:S(2)}) collective-permute-start(f16[32,3712]{1,0:T(8,128)(2,1)S(1)} %convert_element_type.43), channel_id=1, source_target_pairs={{0,24},{1,9},{8,0},{9,17},{16,8},{17,25},{24,16},{25,1},{2,26},{3,... | collective-permute-start | bytes 712712 | tf_op jit(solution)/shard_map/ppermute | solution.py:186
  19.6 4.6 %collective-permute-start.4 = (f16[32,3712]{1,0:T(8,128)(2,1)S(1)}, f16[32,3712]{1,0:T(8,128)(2,1)S(1)}, u32[]{:S(2)}, u32[]{:S(2)}) collective-permute-start(f16[32,3712]{1,0:T(8,128)(2,1)S(1)} %convert_element_type.41), channel_id=1, source_target_pairs={{0,8},{1,25},{8,16},{9,1},{16,24},{17,9},{24,0},{25,17},{2,10},{3,... | collective-permute-start | bytes 712712 | tf_op jit(solution)/shard_map/ppermute | solution.py:186
  24.2 1.9 %collective-permute-done.6 = f16[32,3712]{1,0:T(8,128)(2,1)S(1)} collective-permute-done((f16[32,3712]{1,0:T(8,128)(2,1)S(1)}, f16[32,3712]{1,0:T(8,128)(2,1)S(1)}, u32[]{:S(2)}, u32[]{:S(2)}) %collective-permute-start.6) | collective-permute-done | bytes 237600 | tf_op jit(solution)/shard_map/ppermute | solution.py:186
  26.1 5.2 %collective-permute-done.5 = f16[32,3712]{1,0:T(8,128)(2,1)S(1)} collective-permute-done((f16[32,3712]{1,0:T(8,128)(2,1)S(1)}, f16[32,3712]{1,0:T(8,128)(2,1)S(1)}, u32[]{:S(2)}, u32[]{:S(2)}) %collective-permute-start.5) | collective-permute-done | bytes 237600 | tf_op jit(solution)/shard_map/ppermute | solution.py:186
  31.4 0.0 collective-permute-done.4
  31.4 0.0 copy-start
  31.4 0.0 copy-start.1
  31.4 0.0 copy-start.2
  31.5 0.9 add_y.1
  32.4 8.0 %collective-permute-start.8 = (f16[8,3712]{1,0:T(8,128)(2,1)S(1)}, f16[8,3712]{1,0:T(8,128)(2,1)S(1)}, u32[]{:S(2)}, u32[]{:S(2)}) collective-permute-start(f16[8,3712]{1,0:T(8,128)(2,1)S(1)} %convert_element_type.49), channel_id=1, source_target_pairs={{0,2},{1,7},{2,4},{3,1},{4,6},{5,3},{6,0},{7,5},{8,10},{9,15},{10,... | collective-permute-start | bytes 178184 | tf_op jit(solution)/shard_map/ppermute | solution.py:186
  40.4 1.9 %collective-permute-start.7 = (f16[8,3712]{1,0:T(8,128)(2,1)S(1)}, f16[8,3712]{1,0:T(8,128)(2,1)S(1)}, u32[]{:S(2)}, u32[]{:S(2)}) collective-permute-start(f16[8,3712]{1,0:T(8,128)(2,1)S(1)} %convert_element_type.47), channel_id=1, source_target_pairs={{0,6},{1,3},{2,0},{3,5},{4,2},{5,7},{6,4},{7,1},{8,14},{9,11},{10,... | collective-permute-start | bytes 178184 | tf_op jit(solution)/shard_map/ppermute | solution.py:186
  42.3 0.0 collective-permute-done.8
  42.4 0.2 add_through.1
  42.6 8.8 %collective-permute-start.9 = (f16[8,3712]{1,0:T(8,128)(2,1)S(1)}, f16[8,3712]{1,0:T(8,128)(2,1)S(1)}, u32[]{:S(2)}, u32[]{:S(2)}) collective-permute-start(f16[8,3712]{1,0:T(8,128)(2,1)S(1)} %convert_element_type.51), channel_id=1, source_target_pairs={{0,2},{1,7},{2,4},{3,1},{4,6},{5,3},{6,0},{7,5},{8,10},{9,15},{10,... | collective-permute-start | bytes 178184 | tf_op jit(solution)/shard_map/ppermute | solution.py:186
  51.4 0.0 collective-permute-done.7
  51.5 2.8 %collective-permute-done.9 = f16[8,3712]{1,0:T(8,128)(2,1)S(1)} collective-permute-done((f16[8,3712]{1,0:T(8,128)(2,1)S(1)}, f16[8,3712]{1,0:T(8,128)(2,1)S(1)}, u32[]{:S(2)}, u32[]{:S(2)}) %collective-permute-start.9) | collective-permute-done | bytes 59424 | tf_op jit(solution)/shard_map/ppermute | solution.py:186
  54.3 0.0 copy-done
  54.3 0.0 copy-done.1
  54.3 0.0 copy-done.2
  54.3 0.8 adam.1
  55.1 9.9 %conditional.1 = (f32[2,4,3584]{2,1,0:T(4,128)}) conditional(s32[]{:T(128)} %clamp.3, f32[2,4,3584]{2,1,0:T(4,128)S(1)} %get-tuple-element.41.up_ref, f32[2,4,3584]{2,1,0:T(4,128)S(1)} %get-tuple-element.41.up_ref, f32[2,4,3584]{2,1,0:T(4,128)S(1)} %get-tuple-element.41.up_ref), branch_computations={%region_0.1_spmd, %region_1.2_spmd, %region_2.3_spmd} | conditional | bytes 458800 | solution.py:320
  55.1 4.7 %collective-permute-start.1 = (f32[2,4,3584]{2,1,0:T(4,128)S(1)}, f32[2,4,3584]{2,1,0:T(4,128)}, u32[]{:S(2)}, u32[]{:S(2)}) collective-permute-start(f32[2,4,3584]{2,1,0:T(4,128)S(1)} %param.1), channel_id=1, source_target_pairs={{0,64},{32,96},{64,128},{96,160},{128,192},{160,224},{192,256},{22... | collective-permute-start | bytes 344072 | tf_op jit(solution)/shard_map/cond/branch_1_fun/ppermute | solution.py:22
  59.8 5.2 %collective-permute-done.1 = f32[2,4,3584]{2,1,0:T(4,128)} collective-permute-done((f32[2,4,3584]{2,1,0:T(4,128)S(1)}, f32[2,4,3584]{2,1,0:T(4,128)}, u32[]{:S(2)}, u32[]{:S(2)}) %collective-permute-start.1) | collective-permute-done | bytes 114720 | tf_op jit(solution)/shard_map/cond/branch_1_fun/ppermute | solution.py:22
  65.0 0.9 average.1
  65.9 19.8 %all_gather.6 = bf16[32,3584]{1,0:T(8,128)(2,1)S(1)} all-gather(bf16[8,3584]{1,0:T(8,128)(2,1)S(1)} %average.1), channel_id=1, replica_groups=mesh['zlo'=4,'x'=4,'y'=4,'zhi'=4,'core'=2] {'zhi'}, dimensions={0}, use_global_device_ids=true | all-gather | bytes 286720 | tf_op jit(solution)/shard_map/all_gather | solution.py:324
  85.7 11.0 %all_gather.7.mine_ref = bf16[128,3584]{1,0:T(8,128)(2,1)S(1)} all-gather(bf16[32,3584]{1,0:T(8,128)(2,1)S(1)} %all_gather.6), channel_id=1, replica_groups=mesh['zlo'=4,'x'=4,'y'=4,'zhi'=4,'core'=2] {'y'}, dimensions={0}, use_global_device_ids=true | all-gather | bytes 1146880 | tf_op jit(solution)/shard_map/all_gather | solution.py:325
  96.7 11.2 %collective-permute-start.10 = (bf16[128,3584]{1,0:T(8,128)(2,1)S(1)}, bf16[128,3584]{1,0:T(8,128)(2,1)S(1)}, u32[]{:S(2)}, u32[]{:S(2)}) collective-permute-start(bf16[128,3584]{1,0:T(8,128)(2,1)S(1)} %all_gather.7.mine_ref), channel_id=1, source_target_pairs={{0,1},{1,0},{2,3},{3,2},{4,5},{5,4},{6,7},{7,6},{8,9},{9,8},{10,11... | collective-permute-start | bytes 2752520 | tf_op jit(solution)/shard_map/ppermute | solution.py:22
  107.9 1.7 %finish.1 = (f32[2,4,3584]{2,1,0:T(4,128)}, f32[2,4,3584]{2,1,0:T(4,128)}, f32[2,4,3584]{2,1,0:T(4,128)}) custom-call(f32[8,3584]{1,0:T(8,128)S(1)} %get-tuple-element.40.mean_ref, f32[2,4,3584]{2,1,0:T(4,128)S(1)} %bitcast.13, f32[2,4,3584]{2,1,0:T(4,128)S(1)} %bitcast.15, f32[2,4,3584]{2,1,0:T(4,128)S(1)} %get-tuple-element.41.up_ref, ...), custom_call_target="tpu_custom_call" | custom-call | tf_op jit(solution)/shard_map/finish/pallas_call | solution.py:248
  109.6 0.4 collective-permute-done.10.theirs_ref
  110.0 1.4 %join_cores.1 = bf16[2,128,3584]{2,1,0:T(8,128)(2,1)} custom-call(s32[1]{0:T(128)} %bitcast.core_ref, bf16[128,3584]{1,0:T(8,128)(2,1)S(1)} %all_gather.7.mine_ref, bf16[128,3584]{1,0:T(8,128)(2,1)S(1)} %collective-permute-done.10.theirs_ref), custom_call_target="tpu_custom_call" | custom-call | tf_op jit(solution)/shard_map/join_cores/pallas_call | solution.py:286
  (12 shorter events, 0.2 us)
Async XLA Ops:
  2.2 10.9 %collective-permute-start.3 = (bf16[4,32,3584]{2,1,0:T(8,128)(2,1)S(1)}, bf16[4,32,3584]{2,1,0:T(8,128)(2,1)S(1)}, u32[]{:S(2)}, u32[]{:S(2)}) collective-permute-start(bf16[4,32,3584]{2,1,0:T(8,128)(2,1)S(1)} %get-tuple-element.29), channel_id=1, source_target_pairs={{0,1},{1,0},{2,3},{3,2},{4,5},{5,4},{6,7},{7,6},{8,9},{9,8},{10,11... | collective-permute-start | bytes 2752520 | tf_op jit(solution)/shard_map/ppermute | solution.py:22
  15.6 10.4 %collective-permute-start.6 = (f16[32,3712]{1,0:T(8,128)(2,1)S(1)}, f16[32,3712]{1,0:T(8,128)(2,1)S(1)}, u32[]{:S(2)}, u32[]{:S(2)}) collective-permute-start(f16[32,3712]{1,0:T(8,128)(2,1)S(1)} %convert_element_type.45), channel_id=1, source_target_pairs={{0,16},{1,17},{8,24},{9,25},{16,0},{17,1},{24,8},{25,9},{2,18},{3,... | collective-permute-start | bytes 712712 | tf_op jit(solution)/shard_map/ppermute | solution.py:186
  17.6 13.7 %collective-permute-start.5 = (f16[32,3712]{1,0:T(8,128)(2,1)S(1)}, f16[32,3712]{1,0:T(8,128)(2,1)S(1)}, u32[]{:S(2)}, u32[]{:S(2)}) collective-permute-start(f16[32,3712]{1,0:T(8,128)(2,1)S(1)} %convert_element_type.43), channel_id=1, source_target_pairs={{0,24},{1,9},{8,0},{9,17},{16,8},{17,25},{24,16},{25,1},{2,26},{3,... | collective-permute-start | bytes 712712 | tf_op jit(solution)/shard_map/ppermute | solution.py:186
  19.6 11.8 %collective-permute-start.4 = (f16[32,3712]{1,0:T(8,128)(2,1)S(1)}, f16[32,3712]{1,0:T(8,128)(2,1)S(1)}, u32[]{:S(2)}, u32[]{:S(2)}) collective-permute-start(f16[32,3712]{1,0:T(8,128)(2,1)S(1)} %convert_element_type.41), channel_id=1, source_target_pairs={{0,8},{1,25},{8,16},{9,1},{16,24},{17,9},{24,0},{25,17},{2,10},{3,... | collective-permute-start | bytes 712712 | tf_op jit(solution)/shard_map/ppermute | solution.py:186
  31.4 22.9 %copy-start = (f32[1,2,4,3584]{3,2,1,0:T(4,128)S(1)}, f32[1,2,4,3584]{3,2,1,0:T(4,128)}, u32[]{:S(2)}) copy-start(f32[1,2,4,3584]{3,2,1,0:T(4,128)} %param.11) | copy-start | bytes 344068
  31.4 22.9 %copy-start.1 = (f32[1,2,4,3584]{3,2,1,0:T(4,128)S(1)}, f32[1,2,4,3584]{3,2,1,0:T(4,128)}, u32[]{:S(2)}) copy-start(f32[1,2,4,3584]{3,2,1,0:T(4,128)} %param.12) | copy-start | bytes 344068
  31.4 22.9 %copy-start.2 = (f32[1,2,4,3584]{3,2,1,0:T(4,128)S(1)}, f32[1,2,4,3584]{3,2,1,0:T(4,128)}, u32[]{:S(2)}) copy-start(f32[1,2,4,3584]{3,2,1,0:T(4,128)} %param.10) | copy-start | bytes 344068
  32.4 9.9 %collective-permute-start.8 = (f16[8,3712]{1,0:T(8,128)(2,1)S(1)}, f16[8,3712]{1,0:T(8,128)(2,1)S(1)}, u32[]{:S(2)}, u32[]{:S(2)}) collective-permute-start(f16[8,3712]{1,0:T(8,128)(2,1)S(1)} %convert_element_type.49), channel_id=1, source_target_pairs={{0,2},{1,7},{2,4},{3,1},{4,6},{5,3},{6,0},{7,5},{8,10},{9,15},{10,... | collective-permute-start | bytes 178184 | tf_op jit(solution)/shard_map/ppermute | solution.py:186
  40.4 11.0 %collective-permute-start.7 = (f16[8,3712]{1,0:T(8,128)(2,1)S(1)}, f16[8,3712]{1,0:T(8,128)(2,1)S(1)}, u32[]{:S(2)}, u32[]{:S(2)}) collective-permute-start(f16[8,3712]{1,0:T(8,128)(2,1)S(1)} %convert_element_type.47), channel_id=1, source_target_pairs={{0,6},{1,3},{2,0},{3,5},{4,2},{5,7},{6,4},{7,1},{8,14},{9,11},{10,... | collective-permute-start | bytes 178184 | tf_op jit(solution)/shard_map/ppermute | solution.py:186
  42.6 11.7 %collective-permute-start.9 = (f16[8,3712]{1,0:T(8,128)(2,1)S(1)}, f16[8,3712]{1,0:T(8,128)(2,1)S(1)}, u32[]{:S(2)}, u32[]{:S(2)}) collective-permute-start(f16[8,3712]{1,0:T(8,128)(2,1)S(1)} %convert_element_type.51), channel_id=1, source_target_pairs={{0,2},{1,7},{2,4},{3,1},{4,6},{5,3},{6,0},{7,5},{8,10},{9,15},{10,... | collective-permute-start | bytes 178184 | tf_op jit(solution)/shard_map/ppermute | solution.py:186
  55.1 9.8 %collective-permute-start.1 = (f32[2,4,3584]{2,1,0:T(4,128)S(1)}, f32[2,4,3584]{2,1,0:T(4,128)}, u32[]{:S(2)}, u32[]{:S(2)}) collective-permute-start(f32[2,4,3584]{2,1,0:T(4,128)S(1)} %param.1), channel_id=1, source_target_pairs={{0,64},{32,96},{64,128},{96,160},{128,192},{160,224},{192,256},{22... | collective-permute-start | bytes 344072 | tf_op jit(solution)/shard_map/cond/branch_1_fun/ppermute | solution.py:22
  96.7 13.3 %collective-permute-start.10 = (bf16[128,3584]{1,0:T(8,128)(2,1)S(1)}, bf16[128,3584]{1,0:T(8,128)(2,1)S(1)}, u32[]{:S(2)}, u32[]{:S(2)}) collective-permute-start(bf16[128,3584]{1,0:T(8,128)(2,1)S(1)} %all_gather.7.mine_ref), channel_id=1, source_target_pairs={{0,1},{1,0},{2,3},{3,2},{4,5},{5,4},{6,7},{7,6},{8,9},{9,8},{10,11... | collective-permute-start | bytes 2752520 | tf_op jit(solution)/shard_map/ppermute | solution.py:22

commit v9 on v7

--- a/solution.py
+++ b/solution.py
@@ -77,7 +77,7 @@
     return jnp.exp2(exponent), -exponent
 
 
-def add_pair_kernel(at_ref, mine_ref, theirs_ref, own_ref, near_ref, far_ref, back_ref, sums):
+def add_pair_kernel(at_ref, mine_ref, theirs_ref, near_ref, far_ref, back_ref, sums):
     n, per, depth = mine_ref.shape
     largest = jnp.zeros((8, LANES), F32)
     for k in range(n):
@@ -93,7 +93,6 @@
         step = jnp.where(at_ref[2] == 0, k, n - k)
         return pl.ds(pl.multiple_of(((at_ref[0] + step) % n) * per, per), per)
 
-    own_ref[...] = sums[piece(0), :]
     for k, out_ref in ((1, near_ref), (2, far_ref), (3, back_ref)):
         rows = piece(k)
         for at in range(0, depth, LANES):
@@ -107,9 +106,8 @@
     return pl.pallas_call(
         add_pair_kernel,
         in_specs=[SMEM, VMEM, VMEM],
-        out_specs=[VMEM] * 4,
-        out_shape=[jax.ShapeDtypeStruct((rows, depth), F32)]
-        + [jax.ShapeDtypeStruct((rows, depth + 128), F32)] * 3,
+        out_specs=[VMEM] * 3,
+        out_shape=[jax.ShapeDtypeStruct((rows, depth + 128), F32)] * 3,
         scratch_shapes=[pltpu.VMEM((n * rows, depth), F32)],
         compiler_params=PARAMS,
         name="add_pair",
@@ -130,12 +128,13 @@
     return got_ref[:, :depth] * jnp.exp2(got_ref[0:1, depth : depth + 1])
 
 
-def add_y_kernel(at_ref, own_ref, a_ref, b_ref, c_ref, keep_ref, near_ref, far_ref, back_ref, sums):
-    depth = own_ref.shape[-1]
+def add_y_kernel(at_ref, mine_ref, theirs_ref, a_ref, b_ref, c_ref, keep_ref, near_ref, far_ref, back_ref, sums):
+    depth = mine_ref.shape[-1]
     n = sums.shape[0] // 8
+    y = at_ref[0]
     for at in range(0, depth, LANES):
         cols = slice(at, at + LANES)
-        total = own_ref[:, cols]
+        total = mine_ref[y, :, cols].astype(F32) + theirs_ref[y, :, cols].astype(F32)
         for got_ref in (a_ref, b_ref, c_ref):
             total = total + got_ref[:, cols] * jnp.exp2(got_ref[0:1, depth : depth + 1])
         sums[:, cols] = total
@@ -150,19 +149,19 @@
     scaled(sums.at[piece(3)], back_ref)
 
 
-def add_y(at, own, parts):
-    rows, depth = own.shape
+def add_y(at, mine, theirs, parts):
+    _, rows, depth = mine.shape
     kept = jax.ShapeDtypeStruct((8, depth), F32)
     sent = jax.ShapeDtypeStruct((8, depth + 128), F32)
     return pl.pallas_call(
         add_y_kernel,
-        in_specs=[SMEM] + [VMEM] * 4,
+        in_specs=[SMEM] + [VMEM] * 5,
         out_specs=[VMEM] * 4,
         out_shape=[kept, kept, sent, sent],
         scratch_shapes=[pltpu.VMEM((rows, depth), F32)],
         compiler_params=PARAMS,
         name="add_y",
-    )(at, own, *parts)
+    )(at, mine, theirs, *parts)
 
 
 def add_through_kernel(near_ref, got_ref, out_ref, total):
@@ -312,9 +311,9 @@
     mine, theirs = split_cores(grads[0, 0, 0], core)
     theirs = shifted(theirs, "core", 1)
     theirs, at, corr = lax.optimization_barrier((theirs, at, corr))
-    own, near, far, back = add_pair(at, mine, theirs)
+    near, far, back = add_pair(at, mine, theirs)
     parts = [turned(near, "y", 1), turned(back, "y", -1), turned(far, "y", 2)]
-    own, near, far, back = add_y(at, own, parts)
+    own, near, far, back = add_y(at, mine, theirs, parts)
     far = turned(far, "zhi", 1)
     back = turned(back, "zhi", -1)
     far = turned(add_through(near, far), "zhi", 1)

time: 109 us -> 110 us (level)
  no operation moved by 1% of the time
where the time goes in v9:
time: 110 us
  starting transfers between devices  50 us (45%)
  blocking collectives  30.6 us (28%)
  waiting for transfers between devices  18.1 us (16%)
  Pallas kernels  8.69 us (8%)
  between operations  1.65 us (2%)
    ppermute x6, starting transfers between devices, turned(): lax.ppermute(block.astype(jnp.float16), (axis, 'core'), pairs).astype(F32)  27.1 us
    ppermute x3, starting transfers between devices, shifted(): lax.ppermute(block, axis, [(i, (i + distance) % n) for i in range(n)])  23 us
    all_gather x1, blocking collectives, body(): whole = lax.all_gather(whole, 'zhi', axis=0, tiled=True)  19.6 us
    all_gather x1, blocking collectives, body(): whole = lax.all_gather(whole, 'y', axis=0, tiled=True)  11 us
    ppermute x6, waiting for transfers between devices, turned(): lax.ppermute(block.astype(jnp.float16), (axis, 'core'), pairs).astype(F32)  10 us
    ppermute x3, waiting for transfers between devices, shifted(): lax.ppermute(block, axis, [(i, (i + distance) % n) for i in range(n)])  8.03 us
  transfers between devices with their start and end apart: 9, of which 6 were waited for; matrix products, arithmetic and copies ran while one was open for 0% of the time, Pallas kernels for 2%

profile of v9, /device:TPU:1, one launch (start us, length us, event | category | flops | bytes accessed | tf_op | source)
XLA Modules:
  0.0 109.5 jit_solution(144601175912351960)
XLA Ops:
  0.6 1.6 %split_cores.1 = (bf16[4,32,3584]{2,1,0:T(8,128)(2,1)S(1)}, bf16[4,32,3584]{2,1,0:T(8,128)(2,1)S(1)}) custom-call(s32[1]{0:T(128)} %bitcast.core_ref, bf16[2,128,3584]{2,1,0:T(8,128)(2,1)} %bitcast.17), custom_call_target="tpu_custom_call" | custom-call | tf_op jit(solution)/shard_map/split_cores/pallas_call | solution.py:61
  2.2 8.8 %collective-permute-start.3 = (bf16[4,32,3584]{2,1,0:T(8,128)(2,1)S(1)}, bf16[4,32,3584]{2,1,0:T(8,128)(2,1)S(1)}, u32[]{:S(2)}, u32[]{:S(2)}) collective-permute-start(bf16[4,32,3584]{2,1,0:T(8,128)(2,1)S(1)} %get-tuple-element.32), channel_id=1, source_target_pairs={{0,1},{1,0},{2,3},{3,2},{4,5},{5,4},{6,7},{7,6},{8,9},{9,8},{10,11... | collective-permute-start | bytes 2752520 | tf_op jit(solution)/shard_map/ppermute | solution.py:20
  11.8 0.1 pad_maximum_fusion.corr_ref
  11.9 0.1 pad_add_fusion.at_ref
  11.9 1.2 %collective-permute-done.3.theirs_ref = bf16[4,32,3584]{2,1,0:T(8,128)(2,1)S(1)} collective-permute-done((bf16[4,32,3584]{2,1,0:T(8,128)(2,1)S(1)}, bf16[4,32,3584]{2,1,0:T(8,128)(2,1)S(1)}, u32[]{:S(2)}, u32[]{:S(2)}) %collective-permute-start.3) | collective-permute-done | bytes 917536 | tf_op jit(solution)/shard_map/ppermute | solution.py:20
  13.1 1.2 %add_pair.1 = (f32[32,3712]{1,0:T(8,128)S(1)}, f32[32,3712]{1,0:T(8,128)S(1)}, f32[32,3712]{1,0:T(8,128)S(1)}) custom-call(s32[3]{0:T(128)S(1)} %pad_add_fusion.at_ref, bf16[4,32,3584]{2,1,0:T(8,128)(2,1)S(1)} %get-tuple-element.35.mine_ref, bf16[4,32,3584]{2,1,0:T(8,128)(2,1)S(1)} %collective-permute-done.3.theirs_ref), custom_call_target="tpu_custom_call" | custom-call | tf_op jit(solution)/shard_map/add_pair/pallas_call | solution.py:106
  14.4 1.9 %collective-permute-start.6 = (f16[32,3712]{1,0:T(8,128)(2,1)S(1)}, f16[32,3712]{1,0:T(8,128)(2,1)S(1)}, u32[]{:S(2)}, u32[]{:S(2)}) collective-permute-start(f16[32,3712]{1,0:T(8,128)(2,1)S(1)} %convert_element_type.45), channel_id=1, source_target_pairs={{0,16},{1,17},{8,24},{9,25},{16,0},{17,1},{24,8},{25,9},{2,18},{3,... | collective-permute-start | bytes 712712 | tf_op jit(solution)/shard_map/ppermute | solution.py:190
  16.4 1.9 %collective-permute-start.5 = (f16[32,3712]{1,0:T(8,128)(2,1)S(1)}, f16[32,3712]{1,0:T(8,128)(2,1)S(1)}, u32[]{:S(2)}, u32[]{:S(2)}) collective-permute-start(f16[32,3712]{1,0:T(8,128)(2,1)S(1)} %convert_element_type.43), channel_id=1, source_target_pairs={{0,24},{1,9},{8,0},{9,17},{16,8},{17,25},{24,16},{25,1},{2,26},{3,... | collective-permute-start | bytes 712712 | tf_op jit(solution)/shard_map/ppermute | solution.py:190
  18.3 4.6 %collective-permute-start.4 = (f16[32,3712]{1,0:T(8,128)(2,1)S(1)}, f16[32,3712]{1,0:T(8,128)(2,1)S(1)}, u32[]{:S(2)}, u32[]{:S(2)}) collective-permute-start(f16[32,3712]{1,0:T(8,128)(2,1)S(1)} %convert_element_type.41), channel_id=1, source_target_pairs={{0,8},{1,25},{8,16},{9,1},{16,24},{17,9},{24,0},{25,17},{2,10},{3,... | collective-permute-start | bytes 712712 | tf_op jit(solution)/shard_map/ppermute | solution.py:190
  22.9 2.0 %collective-permute-done.6 = f16[32,3712]{1,0:T(8,128)(2,1)S(1)} collective-permute-done((f16[32,3712]{1,0:T(8,128)(2,1)S(1)}, f16[32,3712]{1,0:T(8,128)(2,1)S(1)}, u32[]{:S(2)}, u32[]{:S(2)}) %collective-permute-start.6) | collective-permute-done | bytes 237600 | tf_op jit(solution)/shard_map/ppermute | solution.py:190
  24.9 5.2 %collective-permute-done.5 = f16[32,3712]{1,0:T(8,128)(2,1)S(1)} collective-permute-done((f16[32,3712]{1,0:T(8,128)(2,1)S(1)}, f16[32,3712]{1,0:T(8,128)(2,1)S(1)}, u32[]{:S(2)}, u32[]{:S(2)}) %collective-permute-start.5) | collective-permute-done | bytes 237600 | tf_op jit(solution)/shard_map/ppermute | solution.py:190
  30.2 0.0 collective-permute-done.4
  30.2 0.0 copy-start
  30.2 0.0 copy-start.1
  30.2 0.0 copy-start.2
  30.3 0.9 add_y.1
  31.2 8.0 %collective-permute-start.8 = (f16[8,3712]{1,0:T(8,128)(2,1)S(1)}, f16[8,3712]{1,0:T(8,128)(2,1)S(1)}, u32[]{:S(2)}, u32[]{:S(2)}) collective-permute-start(f16[8,3712]{1,0:T(8,128)(2,1)S(1)} %convert_element_type.49), channel_id=1, source_target_pairs={{0,2},{1,7},{2,4},{3,1},{4,6},{5,3},{6,0},{7,5},{8,10},{9,15},{10,... | collective-permute-start | bytes 178184 | tf_op jit(solution)/shard_map/ppermute | solution.py:190
  39.2 1.9 %collective-permute-start.7 = (f16[8,3712]{1,0:T(8,128)(2,1)S(1)}, f16[8,3712]{1,0:T(8,128)(2,1)S(1)}, u32[]{:S(2)}, u32[]{:S(2)}) collective-permute-start(f16[8,3712]{1,0:T(8,128)(2,1)S(1)} %convert_element_type.47), channel_id=1, source_target_pairs={{0,6},{1,3},{2,0},{3,5},{4,2},{5,7},{6,4},{7,1},{8,14},{9,11},{10,... | collective-permute-start | bytes 178184 | tf_op jit(solution)/shard_map/ppermute | solution.py:190
  41.1 0.0 collective-permute-done.8
  41.1 0.2 add_through.1
  41.4 8.8 %collective-permute-start.9 = (f16[8,3712]{1,0:T(8,128)(2,1)S(1)}, f16[8,3712]{1,0:T(8,128)(2,1)S(1)}, u32[]{:S(2)}, u32[]{:S(2)}) collective-permute-start(f16[8,3712]{1,0:T(8,128)(2,1)S(1)} %convert_element_type.51), channel_id=1, source_target_pairs={{0,2},{1,7},{2,4},{3,1},{4,6},{5,3},{6,0},{7,5},{8,10},{9,15},{10,... | collective-permute-start | bytes 178184 | tf_op jit(solution)/shard_map/ppermute | solution.py:190
  50.2 0.0 collective-permute-done.7
  50.2 2.8 %collective-permute-done.9 = f16[8,3712]{1,0:T(8,128)(2,1)S(1)} collective-permute-done((f16[8,3712]{1,0:T(8,128)(2,1)S(1)}, f16[8,3712]{1,0:T(8,128)(2,1)S(1)}, u32[]{:S(2)}, u32[]{:S(2)}) %collective-permute-start.9) | collective-permute-done | bytes 59424 | tf_op jit(solution)/shard_map/ppermute | solution.py:190
  53.1 0.0 copy-done
  53.1 0.0 copy-done.1
  53.1 0.0 copy-done.2
  53.1 0.8 adam.1
  53.9 9.6 %conditional.1 = (f32[2,4,3584]{2,1,0:T(4,128)}) conditional(s32[]{:T(128)} %clamp.3, f32[2,4,3584]{2,1,0:T(4,128)S(1)} %get-tuple-element.47.up_ref, f32[2,4,3584]{2,1,0:T(4,128)S(1)} %get-tuple-element.47.up_ref, f32[2,4,3584]{2,1,0:T(4,128)S(1)} %get-tuple-element.47.up_ref), branch_computations={%region_0.1_spmd, %region_1.2_spmd, %region_2.3_spmd} | conditional | bytes 458800 | solution.py:323
  53.9 3.1 %collective-permute-start = (f32[2,4,3584]{2,1,0:T(4,128)S(1)}, f32[2,4,3584]{2,1,0:T(4,128)}, u32[]{:S(2)}, u32[]{:S(2)}) collective-permute-start(f32[2,4,3584]{2,1,0:T(4,128)S(1)} %param), channel_id=1, source_target_pairs={{0,32},{32,64},{64,96},{96,128},{128,160},{160,192},{192,224},{224... | collective-permute-start | bytes 344072 | tf_op jit(solution)/shard_map/cond/branch_0_fun/ppermute | solution.py:20
  57.0 6.4 %collective-permute-done = f32[2,4,3584]{2,1,0:T(4,128)} collective-permute-done((f32[2,4,3584]{2,1,0:T(4,128)S(1)}, f32[2,4,3584]{2,1,0:T(4,128)}, u32[]{:S(2)}, u32[]{:S(2)}) %collective-permute-start) | collective-permute-done | bytes 114720 | tf_op jit(solution)/shard_map/cond/branch_0_fun/ppermute | solution.py:20
  63.4 0.9 average.1
  64.4 19.6 %all_gather.6 = bf16[32,3584]{1,0:T(8,128)(2,1)S(1)} all-gather(bf16[8,3584]{1,0:T(8,128)(2,1)S(1)} %average.1), channel_id=1, replica_groups=mesh['zlo'=4,'x'=4,'y'=4,'zhi'=4,'core'=2] {'zhi'}, dimensions={0}, use_global_device_ids=true | all-gather | bytes 286720 | tf_op jit(solution)/shard_map/all_gather | solution.py:327
  84.0 11.0 %all_gather.7.mine_ref = bf16[128,3584]{1,0:T(8,128)(2,1)S(1)} all-gather(bf16[32,3584]{1,0:T(8,128)(2,1)S(1)} %all_gather.6), channel_id=1, replica_groups=mesh['zlo'=4,'x'=4,'y'=4,'zhi'=4,'core'=2] {'y'}, dimensions={0}, use_global_device_ids=true | all-gather | bytes 1146880 | tf_op jit(solution)/shard_map/all_gather | solution.py:328
  95.0 11.0 %collective-permute-start.10 = (bf16[128,3584]{1,0:T(8,128)(2,1)S(1)}, bf16[128,3584]{1,0:T(8,128)(2,1)S(1)}, u32[]{:S(2)}, u32[]{:S(2)}) collective-permute-start(bf16[128,3584]{1,0:T(8,128)(2,1)S(1)} %all_gather.7.mine_ref), channel_id=1, source_target_pairs={{0,1},{1,0},{2,3},{3,2},{4,5},{5,4},{6,7},{7,6},{8,9},{9,8},{10,11... | collective-permute-start | bytes 2752520 | tf_op jit(solution)/shard_map/ppermute | solution.py:20
  106.1 1.7 %finish.1 = (f32[2,4,3584]{2,1,0:T(4,128)}, f32[2,4,3584]{2,1,0:T(4,128)}, f32[2,4,3584]{2,1,0:T(4,128)}) custom-call(f32[8,3584]{1,0:T(8,128)S(1)} %get-tuple-element.46.mean_ref, f32[2,4,3584]{2,1,0:T(4,128)S(1)} %bitcast.13, f32[2,4,3584]{2,1,0:T(4,128)S(1)} %bitcast.15, f32[2,4,3584]{2,1,0:T(4,128)S(1)} %get-tuple-element.47.up_ref, ...), custom_call_target="tpu_custom_call" | custom-call | tf_op jit(solution)/shard_map/finish/pallas_call | solution.py:252
  107.7 0.4 collective-permute-done.10.theirs_ref
  108.1 1.4 %join_cores.1 = bf16[2,128,3584]{2,1,0:T(8,128)(2,1)} custom-call(s32[1]{0:T(128)} %bitcast.core_ref, bf16[128,3584]{1,0:T(8,128)(2,1)S(1)} %all_gather.7.mine_ref, bf16[128,3584]{1,0:T(8,128)(2,1)S(1)} %collective-permute-done.10.theirs_ref), custom_call_target="tpu_custom_call" | custom-call | tf_op jit(solution)/shard_map/join_cores/pallas_call | solution.py:290
  (12 shorter events, 0.2 us)
Async XLA Ops:
  2.2 10.9 %collective-permute-start.3 = (bf16[4,32,3584]{2,1,0:T(8,128)(2,1)S(1)}, bf16[4,32,3584]{2,1,0:T(8,128)(2,1)S(1)}, u32[]{:S(2)}, u32[]{:S(2)}) collective-permute-start(bf16[4,32,3584]{2,1,0:T(8,128)(2,1)S(1)} %get-tuple-element.32), channel_id=1, source_target_pairs={{0,1},{1,0},{2,3},{3,2},{4,5},{5,4},{6,7},{7,6},{8,9},{9,8},{10,11... | collective-permute-start | bytes 2752520 | tf_op jit(solution)/shard_map/ppermute | solution.py:20
  14.4 10.4 %collective-permute-start.6 = (f16[32,3712]{1,0:T(8,128)(2,1)S(1)}, f16[32,3712]{1,0:T(8,128)(2,1)S(1)}, u32[]{:S(2)}, u32[]{:S(2)}) collective-permute-start(f16[32,3712]{1,0:T(8,128)(2,1)S(1)} %convert_element_type.45), channel_id=1, source_target_pairs={{0,16},{1,17},{8,24},{9,25},{16,0},{17,1},{24,8},{25,9},{2,18},{3,... | collective-permute-start | bytes 712712 | tf_op jit(solution)/shard_map/ppermute | solution.py:190
  16.4 13.8 %collective-permute-start.5 = (f16[32,3712]{1,0:T(8,128)(2,1)S(1)}, f16[32,3712]{1,0:T(8,128)(2,1)S(1)}, u32[]{:S(2)}, u32[]{:S(2)}) collective-permute-start(f16[32,3712]{1,0:T(8,128)(2,1)S(1)} %convert_element_type.43), channel_id=1, source_target_pairs={{0,24},{1,9},{8,0},{9,17},{16,8},{17,25},{24,16},{25,1},{2,26},{3,... | collective-permute-start | bytes 712712 | tf_op jit(solution)/shard_map/ppermute | solution.py:190
  18.3 11.9 %collective-permute-start.4 = (f16[32,3712]{1,0:T(8,128)(2,1)S(1)}, f16[32,3712]{1,0:T(8,128)(2,1)S(1)}, u32[]{:S(2)}, u32[]{:S(2)}) collective-permute-start(f16[32,3712]{1,0:T(8,128)(2,1)S(1)} %convert_element_type.41), channel_id=1, source_target_pairs={{0,8},{1,25},{8,16},{9,1},{16,24},{17,9},{24,0},{25,17},{2,10},{3,... | collective-permute-start | bytes 712712 | tf_op jit(solution)/shard_map/ppermute | solution.py:190
  30.2 22.9 %copy-start = (f32[1,2,4,3584]{3,2,1,0:T(4,128)S(1)}, f32[1,2,4,3584]{3,2,1,0:T(4,128)}, u32[]{:S(2)}) copy-start(f32[1,2,4,3584]{3,2,1,0:T(4,128)} %param.11) | copy-start | bytes 344068
  30.2 22.9 %copy-start.1 = (f32[1,2,4,3584]{3,2,1,0:T(4,128)S(1)}, f32[1,2,4,3584]{3,2,1,0:T(4,128)}, u32[]{:S(2)}) copy-start(f32[1,2,4,3584]{3,2,1,0:T(4,128)} %param.12) | copy-start | bytes 344068
  30.2 22.9 %copy-start.2 = (f32[1,2,4,3584]{3,2,1,0:T(4,128)S(1)}, f32[1,2,4,3584]{3,2,1,0:T(4,128)}, u32[]{:S(2)}) copy-start(f32[1,2,4,3584]{3,2,1,0:T(4,128)} %param.10) | copy-start | bytes 344068
  31.2 9.9 %collective-permute-start.8 = (f16[8,3712]{1,0:T(8,128)(2,1)S(1)}, f16[8,3712]{1,0:T(8,128)(2,1)S(1)}, u32[]{:S(2)}, u32[]{:S(2)}) collective-permute-start(f16[8,3712]{1,0:T(8,128)(2,1)S(1)} %convert_element_type.49), channel_id=1, source_target_pairs={{0,2},{1,7},{2,4},{3,1},{4,6},{5,3},{6,0},{7,5},{8,10},{9,15},{10,... | collective-permute-start | bytes 178184 | tf_op jit(solution)/shard_map/ppermute | solution.py:190
  39.2 11.0 %collective-permute-start.7 = (f16[8,3712]{1,0:T(8,128)(2,1)S(1)}, f16[8,3712]{1,0:T(8,128)(2,1)S(1)}, u32[]{:S(2)}, u32[]{:S(2)}) collective-permute-start(f16[8,3712]{1,0:T(8,128)(2,1)S(1)} %convert_element_type.47), channel_id=1, source_target_pairs={{0,6},{1,3},{2,0},{3,5},{4,2},{5,7},{6,4},{7,1},{8,14},{9,11},{10,... | collective-permute-start | bytes 178184 | tf_op jit(solution)/shard_map/ppermute | solution.py:190
  41.4 11.7 %collective-permute-start.9 = (f16[8,3712]{1,0:T(8,128)(2,1)S(1)}, f16[8,3712]{1,0:T(8,128)(2,1)S(1)}, u32[]{:S(2)}, u32[]{:S(2)}) collective-permute-start(f16[8,3712]{1,0:T(8,128)(2,1)S(1)} %convert_element_type.51), channel_id=1, source_target_pairs={{0,2},{1,7},{2,4},{3,1},{4,6},{5,3},{6,0},{7,5},{8,10},{9,15},{10,... | collective-permute-start | bytes 178184 | tf_op jit(solution)/shard_map/ppermute | solution.py:190
  53.9 9.6 %collective-permute-start = (f32[2,4,3584]{2,1,0:T(4,128)S(1)}, f32[2,4,3584]{2,1,0:T(4,128)}, u32[]{:S(2)}, u32[]{:S(2)}) collective-permute-start(f32[2,4,3584]{2,1,0:T(4,128)S(1)} %param), channel_id=1, source_target_pairs={{0,32},{32,64},{64,96},{96,128},{128,160},{160,192},{192,224},{224... | collective-permute-start | bytes 344072 | tf_op jit(solution)/shard_map/cond/branch_0_fun/ppermute | solution.py:20
  95.0 13.1 %collective-permute-start.10 = (bf16[128,3584]{1,0:T(8,128)(2,1)S(1)}, bf16[128,3584]{1,0:T(8,128)(2,1)S(1)}, u32[]{:S(2)}, u32[]{:S(2)}) collective-permute-start(bf16[128,3584]{1,0:T(8,128)(2,1)S(1)} %all_gather.7.mine_ref), channel_id=1, source_target_pairs={{0,1},{1,0},{2,3},{3,2},{4,5},{5,4},{6,7},{7,6},{8,9},{9,8},{10,11... | collective-permute-start | bytes 2752520 | tf_op jit(solution)/shard_map/ppermute | solution.py:20
